TPU v7x, 256 devices: a whole 4x4x8 slice. The times are simulated.
256 devices in a mesh: rep: 32 (over z, y), fsdp: 8 (over x, core).
Axes of the slice: x: 4, y: 4, z: 8, core: 2. Of those that a mesh axis runs over, the one named last changes fastest.
Arguments:
- gradient: bfloat16 [32, 2, 4096, 1024], P('rep', None, 'fsdp'), may hold values from -30 to 30
- feedback: float32 [32, 2, 4096, 1024], P('rep', None, 'fsdp'), may hold values from -3 to 3
- right_prior: float32 [2, 1024, 128], replicated, may hold values from -0.1875 to 0.1875
Outputs:
- new_feedback: float32 [32, 2, 4096, 1024], P('rep', None, 'fsdp')
- left_basis: float32 [2, 4096, 128], P(None, 'fsdp')
- right_factor: float32 [2, 1024, 128], replicated
All inputs are finite; a program needn't handle non-finite values.
Results may differ from a plain program's by a relative error of at most 0.0003.
Values sent between devices are 32-bit elements; how exact they have to be, the bound alone decides.
No kernel may reach another device: no remote copies, remote signals or barrier semaphores. Data moves between devices by JAX's collectives and lax.ppermute only.
A program may use at most 64 MiB of HBM per device.

v0:
```python
import math

import jax
import jax.numpy as jnp
from jax import lax
from jax.sharding import PartitionSpec as P

FEATURES = 4096


highest = lax.Precision.HIGHEST
ridge_relative = 0.001
ridge_absolute = 1e-06


def factorize(gram_mean):
    order = gram_mean.shape[1]
    trace_mean = jnp.trace(gram_mean, axis1=1, axis2=2) / order
    identity = jnp.eye(order, dtype=gram_mean.dtype)
    shifted = gram_mean + (ridge_relative * trace_mean + ridge_absolute)[:, None, None] * identity
    return jnp.linalg.cholesky(shifted)


def solve_rows(triangle, values):

    def single(factor, block):
        return jax.scipy.linalg.solve_triangular(factor, block.T, lower=True).T

    return jax.vmap(single)(triangle, values)


def wide_sum(pieces):
    return lax.psum((pieces[0],), ("rep", "fsdp"))


def shards(gradient, feedback, right_prior):
    replicas = lax.axis_size("rep")
    merged = gradient[0].astype(jnp.float32) + feedback[0]
    left_part = jnp.einsum("mdk,mkr->mdr", merged, right_prior, precision=highest)
    left_mean = lax.psum(left_part, "rep") / replicas
    gram_part = jnp.einsum("mdr,mds->mrs", left_mean, left_mean, precision=highest)
    norm_scale = 1.0 / math.sqrt(FEATURES)
    gram_mean = lax.psum(gram_part, "fsdp") / FEATURES
    triangle = factorize(gram_mean)
    left_basis = solve_rows(triangle, left_mean)
    right_part = jnp.einsum("mdk,mdr->mkr", merged, left_basis, precision=highest)
    right_total = wide_sum((right_part,))[0]
    right_factor = right_total / replicas * norm_scale
    approx = jnp.einsum("mdr,mkr->mdk", left_basis, right_factor, precision=highest) * norm_scale
    new_feedback = merged - approx
    return (new_feedback[None], left_basis, right_factor)


def solution(mesh):
    in_specs = (P("rep", None, "fsdp", None), P("rep", None, "fsdp", None), P())
    out_specs = (P("rep", None, "fsdp", None), P(None, "fsdp", None), P())
    return jax.shard_map(shards, mesh=mesh, in_specs=in_specs, out_specs=out_specs, check_vma=False)
```

profile of v0, /device:TPU:1, one launch (start us, length us, event | category | flops | bytes accessed | tf_op | source)
XLA Modules:
  0.0 560.5 jit_solution(437025863932637151)
XLA Ops:
  7.2 0.0 copy-start
  7.2 0.0 copy-start.1
  7.2 0.0 all-reduce.4.cloned.1.call-start
  7.2 1.2 copy-done
  8.4 6.7 %fusion.2 = f32[2,512,128]{2,1,0:T(8,128)} fusion(f32[2,1024,128]{2,1,0:T(8,128)S(1)} %copy-done, f32[1,2,512,1024]{3,2,1,0:T(8,128)} %param.4, bf16[1,2,512,1024]{3,2,1,0:T(8,128)(2,1)} %param.3), kind=kOutput, calls=%fused_computation.3 | convolution fusion | flops 1612709888 | bytes 7864320 | tf_op jit(solution)/shard_map/mdk,mkr->mdr/dot_general | solution.py:39
  15.1 0.0 all-reduce.4.cloned.1.call-update
  15.2 0.0 all-reduce.6.cloned.1.call-start
  15.2 146.8 %all-reduce.4.cloned.1.call-done = f32[2,512,128]{2,1,0:T(8,128)} async-done(((f32[2,512,128]{2,1,0:T(8,128)}), f32[2,512,128]{2,1,0:T(8,128)}) %all-reduce.4.cloned.1.call-update) | async-done | bytes 524304 | tf_op jit(solution)/shard_map/psum | solution.py:40
  162.1 2.9 fusion.7
  164.9 0.0 all-reduce.6.cloned.1.call-update
  165.0 0.0 all-reduce.8.cloned.1.call-start
  165.0 63.8 %all-reduce.6.cloned.1.call-done = f32[2,128,128]{2,1,0:T(8,128)} async-done(((f32[2,128,128]{2,1,0:T(8,128)}), f32[2,128,128]{2,1,0:T(8,128)}) %all-reduce.6.cloned.1.call-update) | async-done | bytes 131088 | tf_op jit(solution)/shard_map/psum | solution.py:43
  228.8 1.0 select_reduce_fusion.1
  229.8 1.0 multiply_add_fusion
  230.8 0.1 copy.13
  230.9 1.6 fusion.12
  232.6 24.3 %custom-call.8 = f32[2,128,128]{2,1,0:T(8,128)S(1)} custom-call(f32[2,128,128]{2,1,0:T(8,128)} %fusion.12), custom_call_target="Cholesky" | custom-call | tf_op jit(solution)/shard_map/jit(cholesky)/cholesky | solution.py:21
  256.9 0.1 compare_reduce_fusion
  257.0 0.1 select_bitcast_fusion
  257.1 19.9 %custom-call.9 = f32[2,1,128,128]{2,3,1,0:T(8,128)S(1)} custom-call(f32[2,1,128,128]{3,2,1,0:T(8,128)S(1)} %select_bitcast_fusion), custom_call_target="InvertDiagBlocksLowerTriangular" | custom-call | tf_op jit(solution)/shard_map/vmap(jit(_solve_triangular))/triangular_solve | solution.py:27
  277.0 1.7 fusion.5
  278.6 0.0 copy-start.2
  278.6 0.8 copy-done.2
  279.5 0.0 copy-done.1
  279.5 9.8 %fusion = f32[2,1024,128]{2,1,0:T(8,128)} fusion(f32[2,128,512]{2,1,0:T(8,128)S(1)} %fusion.5, f32[1,2,512,1024]{3,2,1,0:T(8,128)} %param.4, bf16[1,2,512,1024]{3,2,1,0:T(8,128)(2,1)S(1)} %copy-done.1), kind=kOutput, calls=%fused_computation.1 | convolution fusion | flops 1612709888 | bytes 7864320 | tf_op jit(solution)/shard_map/mdk,mdr->mkr/dot_general | solution.py:46
  289.3 0.0 all-reduce.8.cloned.1.call-update
  289.3 2.0 copy.17
  291.3 253.8 %all-reduce.8.cloned.1.call-done = f32[2,1024,128]{2,1,0:T(8,128)} async-done(((f32[2,1024,128]{2,1,0:T(8,128)}), f32[2,1024,128]{2,1,0:T(8,128)}) %all-reduce.8.cloned.1.call-update) | async-done | bytes 1048592 | tf_op jit(solution)/shard_map/psum | solution.py:33
  545.1 1.3 broadcast_multiply_fusion
  546.4 0.0 copy-start.3
  546.4 7.5 %fusion.4 = f32[1,2,512,1024]{3,2,1,0:T(8,128)} fusion(f32[2,128,512]{2,1,0:T(8,128)} %copy-done.2, f32[2,1024,128]{2,1,0:T(8,128)S(1)} %broadcast_multiply_fusion, f32[1,2,512,1024]{3,2,1,0:T(8,128)} %param.4, bf16[1,2,512,1024]{3,2,1,0:T(8,128)(2,1)S(1)} %copy-done.1), kind=kOutput, calls=%fused_computation.5 | convolution fusion | flops 1614807040 | bytes 12058624 | tf_op jit(solution)/shard_map/mdr,mkr->mdk/dot_general | solution.py:49
  553.9 0.0 copy-done.3
  (5 shorter events, 0.1 us)
Async XLA Ops:
  7.2 1.2 copy-start
  7.2 272.3 %copy-start.1 = (bf16[1,2,512,1024]{3,2,1,0:T(8,128)(2,1)S(1)}, bf16[1,2,512,1024]{3,2,1,0:T(8,128)(2,1)}, u32[]{:S(2)}) copy-start(bf16[1,2,512,1024]{3,2,1,0:T(8,128)(2,1)} %param.3) | copy-start | bytes 6291460
  7.2 154.9 %all-reduce.4.cloned.1.call-start = ((), (), s32[]{:S(2)}) async-start(), calls=%async_computation | async-start | bytes 1048576 | tf_op jit(solution)/shard_map/psum | solution.py:40
  15.2 213.7 %all-reduce.6.cloned.1.call-start = ((), (), s32[]{:S(2)}) async-start(), calls=%async_computation.1 | async-start | bytes 262144 | tf_op jit(solution)/shard_map/psum | solution.py:43
  165.0 380.2 %all-reduce.8.cloned.1.call-start = ((), (), s32[]{:S(2)}) async-start(), calls=%async_computation.2 | async-start | bytes 2097152 | tf_op jit(solution)/shard_map/psum | solution.py:33
  278.6 0.8 copy-start.2
  546.4 7.5 %copy-start.3 = (f32[2,1024,128]{2,1,0:T(8,128)}, f32[2,1024,128]{2,1,0:T(8,128)S(1)}, u32[]{:S(2)}) copy-start(f32[2,1024,128]{2,1,0:T(8,128)S(1)} %broadcast_multiply_fusion) | copy-start | bytes 3145732
Sparse Core Ops, SparseCore 0:
  15.3 146.7 all-reduce.3
  165.1 63.6 all-reduce.5
  289.4 255.6 all-reduce.7
where the time goes:
time: 561 us; the launch traced here: 560 us
  waiting for transfers between devices  464 us (83%)
  other arithmetic  49.4 us (9%)
  matrix products  28.6 us (5%)
  between operations  13.8 us (2%)
    psum x1, waiting for transfers between devices, wide_sum(): return lax.psum((pieces[0],), ('rep', 'fsdp'))  254 us
    psum x1, waiting for transfers between devices, shards(): left_mean = lax.psum(left_part, 'rep') / replicas  147 us
    psum x1, waiting for transfers between devices, shards(): gram_mean = lax.psum(gram_part, 'fsdp') / FEATURES  63.8 us
    another operation x4, other arithmetic, factorize(): return jnp.linalg.cholesky(shifted)  24.4 us
    another operation x3, other arithmetic, single(): return jax.scipy.linalg.solve_triangular(factor, block.T, lower=True).T  20 us
  transfers between devices with their start and end apart: 3, of which 3 were waited for; matrix products, arithmetic and copies ran while one was open for 0% of the time, Pallas kernels for 0%

commit v1 on v0

v1 whole, which is shorter than its diff:
```python
import math

import jax
import jax.numpy as jnp
from jax import lax
from jax.experimental import pallas as pl
from jax.experimental.pallas import tpu as pltpu
from jax.sharding import Mesh, PartitionSpec as P

FEATURES = 4096
WIDTH = 1024
RANK = 128
MATRICES = 2
ROWS = 512
ridge_relative = 0.001
ridge_absolute = 1e-06
MIB = 1 << 20
f32 = jnp.float32
bf16 = jnp.bfloat16


def halves(x):
    high = x.astype(bf16)
    return high, (x - high.astype(f32)).astype(bf16)


def dot(a, b, dims):
    return lax.dot_general(a, b, (dims, ((), ())), preferred_element_type=f32)


NN = ((1,), (0,))
NT = ((1,), (1,))
TN = ((0,), (0,))


def dot_wide(a, b):
    a_high, a_low = halves(a)
    b_high, b_low = halves(b)
    both = dot(a_high, jnp.concatenate([b_high, b_low], axis=1), NN)
    return both[:, :RANK] + (both[:, RANK:] + dot(a_low, b_high, NN))


def dot_deep(a, b):
    a_high, a_low = halves(a)
    b_high, b_low = halves(b)
    both = jnp.concatenate([a_high, a_low], axis=1)
    return dot(both, jnp.concatenate([b_high, b_high], axis=0), NN) + dot(a_high, b_low, NN)


def left_kernel(gradient, feedback, prior, left):
    merged = gradient[0].astype(f32) + feedback[0]
    left[:, 0] = dot_wide(merged, prior[0]).reshape(left.shape[0], 16, RANK)


def left_terms(gradient, feedback, right_prior):
    steps = 2
    rows = ROWS // steps
    return pl.pallas_call(
        left_kernel,
        grid=(MATRICES, steps),
        in_specs=[
            pl.BlockSpec((1, rows, WIDTH), lambda m, t: (m, t, 0)),
            pl.BlockSpec((1, rows, WIDTH), lambda m, t: (m, t, 0)),
            pl.BlockSpec((1, WIDTH, RANK), lambda m, t: (m, 0, 0)),
        ],
        out_specs=pl.BlockSpec((rows // 16, 1, 16, RANK), lambda m, t: (t, m, 0, 0)),
        out_shape=jax.ShapeDtypeStruct((ROWS // 16, MATRICES, 16, RANK), f32),
        compiler_params=pltpu.CompilerParams(vmem_limit_bytes=32 * MIB),
        name="left_terms",
    )(gradient, feedback, right_prior)


def right_kernel(gradient, feedback, left_mean, right, gram):
    left = left_mean[:, 0].reshape(ROWS, RANK)
    high, low = halves(left)
    both = jnp.concatenate([high, low], axis=1)

    @pl.when(pl.program_id(1) == 0)
    def _():
        square = dot(both, both, TN)
        gram[0] = square[:RANK, :RANK] + (square[RANK:, :RANK] + square[:RANK, RANK:] + square[RANK:, RANK:])

    merged_high, merged_low = halves(gradient[0].astype(f32) + feedback[0])
    double = dot(both, merged_high, TN)
    total = double[:RANK] + (double[RANK:] + dot(high, merged_low, TN))
    for j in range(right.shape[2]):
        right[0, :, j] = total[:, 128 * j : 128 * (j + 1)].reshape(16, 8, 128)


def right_terms(gradient, feedback, left_mean):
    steps = 2
    cols = WIDTH // steps
    return pl.pallas_call(
        right_kernel,
        grid=(MATRICES, steps),
        in_specs=[
            pl.BlockSpec((1, ROWS, cols), lambda m, t: (m, 0, t)),
            pl.BlockSpec((1, ROWS, cols), lambda m, t: (m, 0, t)),
            pl.BlockSpec((ROWS // 16, 1, 16, RANK), lambda m, t: (0, m, 0, 0)),
        ],
        out_specs=[
            pl.BlockSpec((1, 16, cols // 128, 8, 128), lambda m, t: (m, 0, t, 0, 0)),
            pl.BlockSpec((1, RANK, RANK), lambda m, t: (m, 0, 0)),
        ],
        out_shape=[
            jax.ShapeDtypeStruct((MATRICES, 16, WIDTH // 128, 8, 128), f32),
            jax.ShapeDtypeStruct((MATRICES, RANK, RANK), f32),
        ],
        compiler_params=pltpu.CompilerParams(vmem_limit_bytes=32 * MIB),
        name="right_terms",
    )(gradient, feedback, left_mean)


def inverse_kernel(parts, out):
    rows = lax.broadcasted_iota(jnp.int32, (RANK, RANK), 0)
    cols = lax.broadcasted_iota(jnp.int32, (RANK, RANK), 1)
    diagonal = rows == cols
    matrix = (parts[0] + parts[1] + (parts[2] + parts[3])) * (1.0 / FEATURES)
    trace = jnp.sum(jnp.where(diagonal, matrix, 0.0))
    ridge = ridge_relative * (trace / RANK) + ridge_absolute
    matrix = jnp.where(diagonal, matrix + ridge, matrix)
    unit = jnp.where(diagonal, 1.0, 0.0)
    for k in range(RANK - 1):
        low = k // 8 * 8
        row = matrix[k - low : k - low + 1]
        factor = matrix[:, k : k + 1] * (1.0 / row[:, k : k + 1])
        factor = jnp.where(rows[low:, :1] > k, factor, 0.0)
        unit_row = unit[k : k + 1]
        matrix = matrix - factor * row
        unit = jnp.concatenate([unit[:low], unit[low:] - factor * unit_row], axis=0) if low else unit - factor * unit_row
        if k % 8 == 7:
            out[low : low + 8] = matrix[:8]
            matrix = matrix[8:]
    out[RANK - 8 :] = matrix
    pivot = jnp.sum(jnp.where(diagonal, out[...], 0.0), axis=1, keepdims=True)
    out[...] = unit * lax.rsqrt(pivot)


def inverse_factor(parts):
    return pl.pallas_call(
        inverse_kernel,
        out_shape=jax.ShapeDtypeStruct((RANK, RANK), f32),
        compiler_params=pltpu.CompilerParams(vmem_limit_bytes=16 * MIB),
        name="inverse_factor",
    )(parts)


def finish_kernel(core, gradient, feedback, left_mean, inverse, right_total, renewed, basis, factor):
    norm_scale = 1.0 / math.sqrt(FEATURES)
    left = left_mean[:, 0].reshape(ROWS, RANK)
    left_basis = dot_wide(left, inverse[0].T)
    basis[0] = left_basis
    total = jnp.concatenate([right_total[0, :, j].reshape(RANK, 128) for j in range(WIDTH // 128)], axis=1)
    right = dot_deep(inverse[0], total) * (norm_scale / 32)
    factor[0] = right.T
    approx = dot_deep(left_basis * norm_scale, right)
    renewed[0] = gradient[0].astype(f32) + feedback[0] - approx


def finish(core, gradient, feedback, left_mean, inverse, right_total):
    mine = lambda i, core: i ^ core[0]
    return pl.pallas_call(
        finish_kernel,
        grid_spec=pltpu.PrefetchScalarGridSpec(
            num_scalar_prefetch=1,
            grid=(MATRICES,),
            in_specs=[
                pl.BlockSpec((1, ROWS, WIDTH), lambda i, core: (i ^ core[0], 0, 0)),
                pl.BlockSpec((1, ROWS, WIDTH), lambda i, core: (i ^ core[0], 0, 0)),
                pl.BlockSpec((ROWS // 16, 1, 16, RANK), lambda i, core: (0, i ^ core[0], 0, 0)),
                pl.BlockSpec((1, RANK, RANK), lambda i, core: (i, 0, 0)),
                pl.BlockSpec((1, 16, WIDTH // 128, 8, 128), lambda i, core: (i, 0, 0, 0, 0)),
            ],
            out_specs=[
                pl.BlockSpec((1, ROWS, WIDTH), lambda i, core: (i ^ core[0], 0, 0)),
                pl.BlockSpec((1, ROWS, RANK), lambda i, core: (i ^ core[0], 0, 0)),
                pl.BlockSpec((1, WIDTH, RANK), lambda i, core: (i ^ core[0], 0, 0)),
            ],
        ),
        out_shape=[
            jax.ShapeDtypeStruct((MATRICES, ROWS, WIDTH), f32),
            jax.ShapeDtypeStruct((MATRICES, ROWS, RANK), f32),
            jax.ShapeDtypeStruct((MATRICES, WIDTH, RANK), f32),
        ],
        compiler_params=pltpu.CompilerParams(vmem_limit_bytes=40 * MIB),
        name="finish",
    )(core, gradient, feedback, left_mean, inverse, right_total)


def spread(x, axes, size):
    return lax.all_to_all(jnp.broadcast_to(x[None], (size,) + x.shape), axes, 0, 0, tiled=True)


def swap(x):
    return lax.ppermute(x, "core", [(0, 1), (1, 0)])


def shards(gradient, feedback, right_prior):
    gradient, feedback = gradient[0], feedback[0]
    core = lax.axis_index("core")
    rep = ("z", "y")
    chips = ("z", "y", "x")
    left = left_terms(gradient, feedback, right_prior)
    left = lax.all_to_all(left, rep, 0, 0, tiled=True).sum(0) * (1.0 / 32)
    left_mean = spread(left, rep, 32)
    right, gram = right_terms(gradient, feedback, left_mean)
    pick = lambda x, i: lax.dynamic_index_in_dim(x, i, 0, False)
    gram = pick(gram, core) + swap(pick(gram, 1 - core))
    own = pick(right, core) + swap(pick(right, 1 - core))
    own = lax.all_to_all(own.reshape(128, 8, 128), chips, 0, 0, tiled=True).sum(0)
    inverse = inverse_factor(spread(gram, "x", 4))
    inverse = jnp.stack([inverse, swap(inverse)])
    own = spread(own, chips, 128).reshape(16, 8, 8, 128)
    total = jnp.stack([own, swap(own)])
    renewed, basis, factor = finish(core[None], gradient, feedback, left_mean, inverse, total)
    return renewed[None], basis, factor


def solution(mesh):
    chips = Mesh(mesh.devices.reshape(8, 4, 4, 2), ("z", "y", "x", "core"))
    rep, fsdp = ("z", "y"), ("x", "core")
    in_specs = (P(rep, None, fsdp, None), P(rep, None, fsdp, None), P())
    out_specs = (P(rep, None, fsdp, None), P(None, fsdp, None), P())
    return jax.shard_map(shards, mesh=chips, in_specs=in_specs, out_specs=out_specs, check_vma=False)
```

time: 561 us -> 156 us (0.28)
  waiting for transfers between devices: 464 us -> 32.5 us
  blocking collectives: 0 us -> 64.2 us
  other arithmetic: 49.4 us -> 1.39 us
  matrix products: 28.6 us -> 0 us
  starting transfers between devices: 0.12 us -> 23.6 us
  Pallas kernels: 0 us -> 19.5 us
  between operations: 13.8 us -> 0.75 us
  local copies, waits for them, and re-layouts: 4.12 us -> 12.9 us
    psum x3 -> x0, waiting for transfers between devices: 464 us -> none  [the longest x1 254 us: wide_sum(): return lax.psum((pieces[0],), ('rep', 'fsdp'))]
    all_to_all x0 -> x3, blocking collectives: none -> 64.2 us  [the longest x1 28.1 us: shards(): left = lax.all_to_all(left, rep, 0, 0, tiled=True).sum(0) * (1.0 / 32)]
    another operation x7 -> x2, other arithmetic: 44.4 us -> 0.09 us  [the longest x1 0.08 us: shards(): total = jnp.stack([own, swap(own)])]
    all_to_all x0 -> x2, waiting for transfers between devices: none -> 29.8 us  [spread(): lax.all_to_all(jnp.broadcast_to(x[None], (size,) + x.shape), axes, 0, 0,...]
    dot_general x4 -> x0, matrix products: 26.9 us -> none  [the longest x1 9.82 us: shards(): jnp.einsum('mdk,mdr->mkr', merged, left_basis, precision=highest)]
    pallas_call x0 -> x4, Pallas kernels: none -> 19.5 us  [the longest x1 10.8 us: inverse_factor(): pl.pallas_call(inverse_kernel, out_shape=jax.ShapeDtypeStruct((RANK, RANK...]
    all_to_all x0 -> x2, starting transfers between devices: none -> 11.9 us  [spread(): lax.all_to_all(jnp.broadcast_to(x[None], (size,) + x.shape), axes, 0, 0,...]
    ppermute x0 -> x4, starting transfers between devices: none -> 11.7 us  [swap(): return lax.ppermute(x, 'core', [(0, 1), (1, 0)])]
  transfers between devices with their start and end apart: 3 -> 6, of which waited for: 3 -> 4; matrix products, arithmetic and copies ran while one was open for 0% -> 0% of each run, Pallas kernels for 0% -> 7%
where the time goes in v1:
time: 156 us; the launch traced here: 155 us
  blocking collectives  64.2 us (41%)
  waiting for transfers between devices  32.5 us (21%)
  starting transfers between devices  23.6 us (15%)
  Pallas kernels  19.5 us (12%)
  local copies, waits for them, and re-layouts  12.9 us (8%)
    all_to_all x2, waiting for transfers between devices, spread(): lax.all_to_all(jnp.broadcast_to(x[None], (size,) + x.shape), axes, 0, 0,...  29.8 us
    all_to_all x1, blocking collectives, shards(): left = lax.all_to_all(left, rep, 0, 0, tiled=True).sum(0) * (1.0 / 32)  28.1 us
    all_to_all x1, blocking collectives, shards(): lax.all_to_all(own.reshape(128, 8, 128), chips, 0, 0, tiled=True).sum(0)  27.2 us
    all_to_all x2, starting transfers between devices, spread(): lax.all_to_all(jnp.broadcast_to(x[None], (size,) + x.shape), axes, 0, 0,...  11.9 us
    ppermute x4, starting transfers between devices, swap(): return lax.ppermute(x, 'core', [(0, 1), (1, 0)])  11.7 us
    pallas_call x1, Pallas kernels, inverse_factor(): pl.pallas_call(inverse_kernel, out_shape=jax.ShapeDtypeStruct((RANK, RANK...  10.8 us
    unnamed x14, local copies, waits for them, and re-layouts  10.3 us
    all_to_all x1, blocking collectives, spread(): lax.all_to_all(jnp.broadcast_to(x[None], (size,) + x.shape), axes, 0, 0,...  8.93 us
  transfers between devices with their start and end apart: 6, of which 4 were waited for; matrix products, arithmetic and copies ran while one was open for 0% of the time, Pallas kernels for 7%

profile of v1, /device:TPU:1, one launch (start us, length us, event | category | flops | bytes accessed | tf_op | source)
XLA Modules:
  0.0 154.9 jit_solution(5644390992341466107)
XLA Ops:
  0.6 0.0 copy-start
  0.6 2.2 %copy-done = f32[1,2,512,1024]{3,2,1,0:T(8,128)S(1)} copy-done((f32[1,2,512,1024]{3,2,1,0:T(8,128)S(1)}, f32[1,2,512,1024]{3,2,1,0:T(8,128)}, u32[]{:S(2)}) %copy-start) | copy-done | bytes 4194328
  2.8 0.0 copy-start.3
  2.8 1.6 %copy-done.3 = bf16[1,2,512,1024]{3,2,1,0:T(8,128)(2,1)S(1)} copy-done((bf16[1,2,512,1024]{3,2,1,0:T(8,128)(2,1)S(1)}, bf16[1,2,512,1024]{3,2,1,0:T(8,128)(2,1)}, u32[]{:S(2)}) %copy-start.3) | copy-done | bytes 2097176
  4.4 0.0 copy-start.5
  4.4 1.2 copy-done.5
  5.6 0.0 copy-start.4
  5.6 1.9 %left_terms.1 = f32[32,2,16,128]{3,2,1,0:T(8,128)S(1)} custom-call(bf16[2,512,1024]{2,1,0:T(8,128)(2,1)S(1)} %bitcast.21, f32[2,512,1024]{2,1,0:T(8,128)S(1)} %bitcast.18, f32[2,1024,128]{2,1,0:T(8,128)S(1)} %copy-done.5), custom_call_target="tpu_custom_call" | custom-call | tf_op jit(solution)/shard_map/left_terms/pallas_call | solution.py:58
  7.5 28.1 %all_to_all.25 = f32[32,2,16,128]{3,2,1,0:T(8,128)S(1)} all-to-all(f32[32,2,16,128]{3,2,1,0:T(8,128)S(1)} %left_terms.1), channel_id=1, replica_groups=mesh['z'=8,'y'=4,'x'=4,'core'=2] {'z','y'}, dimensions={0} | all-to-all | bytes 1048576 | tf_op jit(solution)/shard_map/all_to_all | solution.py:204
  35.7 0.9 broadcast_in_dim.11
  36.5 5.2 %all-to-all-start.1 = ((f32[32,2,16,128]{3,2,1,0:T(8,128)}), f32[32,2,16,128]{3,2,1,0:T(8,128)S(1)}, u32[]{:S(2)}, u32[]{:S(2)}) async-start(f32[32,2,16,128]{3,2,1,0:T(8,128)} %broadcast_in_dim.11), calls=%async_computation.1 | async-start | bytes 1048576 | tf_op jit(solution)/shard_map/all_to_all | solution.py:191
  41.7 15.1 %all-to-all-done.1.left_mean = f32[32,2,16,128]{3,2,1,0:T(8,128)S(1)} async-done(((f32[32,2,16,128]{3,2,1,0:T(8,128)}), f32[32,2,16,128]{3,2,1,0:T(8,128)S(1)}, u32[]{:S(2)}, u32[]{:S(2)}) %all-to-all-start.1) | async-done | bytes 524320 | tf_op jit(solution)/shard_map/all_to_all | solution.py:191
  56.8 0.0 copy-done.4
  56.8 0.0 copy-start.1
  56.8 2.2 %copy-done.1 = f32[1,2,512,1024]{3,2,1,0:T(8,128)S(1)} copy-done((f32[1,2,512,1024]{3,2,1,0:T(8,128)S(1)}, f32[1,2,512,1024]{3,2,1,0:T(8,128)}, u32[]{:S(2)}) %copy-start.1) | copy-done | bytes 4194328
  59.0 3.0 %right_terms.1 = (f32[2,16,8,8,128]{4,3,2,1,0:T(8,128)S(1)}, f32[2,128,128]{2,1,0:T(8,128)S(1)}) custom-call(bf16[2,512,1024]{2,1,0:T(8,128)(2,1)S(1)} %bitcast.22, f32[2,512,1024]{2,1,0:T(8,128)S(1)} %bitcast.19, f32[32,2,16,128]{3,2,1,0:T(8,128)S(1)} %all-to-all-done.1.left_mean), custom_call_target="tpu_custom_call" | custom-call | tf_op jit(solution)/shard_map/right_terms/pallas_call | solution.py:93
  62.0 0.0 copy-start.6
  62.0 1.0 copy-done.6
  63.0 0.8 dynamic-slice_bitcast_fusion
  63.8 3.8 %collective-permute-start.2 = (f32[16,8,8,128]{3,2,1,0:T(8,128)}, f32[16,8,8,128]{3,2,1,0:T(8,128)S(1)}, u32[]{:S(2)}, u32[]{:S(2)}) collective-permute-start(f32[16,8,8,128]{3,2,1,0:T(8,128)} %dynamic-slice_bitcast_fusion), channel_id=1, source_target_pairs={{0,1},{1,0},{2,3},{3,2},{4,5},{5,4},{6,7},{7,6},{8,9},{9,8},{10,11... | collective-permute-start | bytes 1572872 | tf_op jit(solution)/shard_map/ppermute | solution.py:195
  67.6 1.7 %collective-permute-done.2 = f32[16,8,8,128]{3,2,1,0:T(8,128)S(1)} collective-permute-done((f32[16,8,8,128]{3,2,1,0:T(8,128)}, f32[16,8,8,128]{3,2,1,0:T(8,128)S(1)}, u32[]{:S(2)}, u32[]{:S(2)}) %collective-permute-start.2) | collective-permute-done | bytes 524320 | tf_op jit(solution)/shard_map/ppermute | solution.py:195
  69.3 1.1 bitcast_add_fusion
  70.4 27.2 %all_to_all.26 = f32[128,8,128]{2,1,0:T(8,128)S(1)} all-to-all(f32[128,8,128]{2,1,0:T(8,128)S(1)} %bitcast.25), channel_id=1, replica_groups=mesh['z'=8,'y'=4,'x'=4,'core'=2] {'z','y','x'}, dimensions={0} | all-to-all | bytes 1048576 | tf_op jit(solution)/shard_map/all_to_all | solution.py:210
  97.6 0.1 reduce_sum.19
  97.7 0.8 broadcast_in_dim.13
  98.6 6.7 %all-to-all-start.4 = ((f32[128,8,128]{2,1,0:T(8,128)}), f32[128,8,128]{2,1,0:T(8,128)S(1)}, u32[]{:S(2)}, u32[]{:S(2)}) async-start(f32[128,8,128]{2,1,0:T(8,128)} %broadcast_in_dim.13), calls=%async_computation.4 | async-start | bytes 1048576 | tf_op jit(solution)/shard_map/all_to_all | solution.py:191
  105.3 2.3 %collective-permute-start = (f32[128,128]{1,0:T(8,128)S(1)}, f32[128,128]{1,0:T(8,128)S(1)}, u32[]{:S(2)}, u32[]{:S(2)}) collective-permute-start(f32[128,128]{1,0:T(8,128)S(1)} %dynamic-slice_bitcast_fusion.1), channel_id=1, source_target_pairs={{0,1},{1,0},{2,3},{3,2},{4,5},{5,4},{6,7},{7,6},{8,9},{9,8},{10,11... | collective-permute-start | bytes 196616 | tf_op jit(solution)/shard_map/ppermute | solution.py:195
  107.7 14.8 %all-to-all-done.4 = f32[128,8,128]{2,1,0:T(8,128)S(1)} async-done(((f32[128,8,128]{2,1,0:T(8,128)}), f32[128,8,128]{2,1,0:T(8,128)S(1)}, u32[]{:S(2)}, u32[]{:S(2)}) %all-to-all-start.4) | async-done | bytes 524320 | tf_op jit(solution)/shard_map/all_to_all | solution.py:191
  122.4 4.5 %collective-permute-start.3 = (f32[16,8,8,128]{3,2,1,0:T(8,128)S(1)}, f32[16,8,8,128]{3,2,1,0:T(8,128)S(1)}, u32[]{:S(2)}, u32[]{:S(2)}) collective-permute-start(f32[16,8,8,128]{3,2,1,0:T(8,128)S(1)} %bitcast.26), channel_id=1, source_target_pairs={{0,1},{1,0},{2,3},{3,2},{4,5},{5,4},{6,7},{7,6},{8,9},{9,8},{10,11... | collective-permute-start | bytes 1572872 | tf_op jit(solution)/shard_map/ppermute | solution.py:195
  126.9 0.0 collective-permute-done
  127.0 8.9 %all_to_all.27.parts = f32[4,128,128]{2,1,0:T(8,128)S(1)} all-to-all(f32[4,128,128]{2,1,0:T(8,128)S(1)} %broadcast_in_dim.12), channel_id=1, replica_groups=mesh['z'=8,'y'=4,'x'=4,'core'=2] {'x'}, dimensions={0} | all-to-all | bytes 524288 | tf_op jit(solution)/shard_map/all_to_all | solution.py:191
  135.9 10.8 %inverse_factor.1 = f32[128,128]{1,0:T(8,128)S(1)} custom-call(f32[4,128,128]{2,1,0:T(8,128)S(1)} %all_to_all.27.parts), custom_call_target="tpu_custom_call" | custom-call | tf_op jit(solution)/shard_map/inverse_factor/pallas_call | solution.py:140
  146.7 1.1 collective-permute-start.1
  147.9 0.9 collective-permute-done.1
  148.8 0.0 collective-permute-done.3
  148.8 0.1 pad_maximum_fusion.right_total
  148.9 0.0 copy-start.2
  148.9 2.2 %copy-done.2 = f32[1,2,512,1024]{3,2,1,0:T(8,128)S(1)} copy-done((f32[1,2,512,1024]{3,2,1,0:T(8,128)S(1)}, f32[1,2,512,1024]{3,2,1,0:T(8,128)}, u32[]{:S(2)}) %copy-start.2) | copy-done | bytes 4194328
  151.1 3.9 %finish.1 = (f32[2,512,1024]{2,1,0:T(8,128)}, f32[2,512,128]{2,1,0:T(8,128)}, f32[2,1024,128]{2,1,0:T(8,128)}) custom-call(s32[1]{0:T(128)} %bitcast.core, bf16[2,512,1024]{2,1,0:T(8,128)(2,1)S(1)} %bitcast.23, f32[2,512,1024]{2,1,0:T(8,128)S(1)} %bitcast.20, f32[32,2,16,128]{3,2,1,0:T(8,128)S(1)} %all-to-all-done.1.left_mean, ...), custom_call_target="tpu_custom_call" | custom-call | tf_op jit(solution)/shard_map/finish/pallas_call | solution.py:162
  (6 shorter events, 0.1 us)
Async XLA Ops:
  0.6 2.2 %copy-start = (f32[1,2,512,1024]{3,2,1,0:T(8,128)S(1)}, f32[1,2,512,1024]{3,2,1,0:T(8,128)}, u32[]{:S(2)}) copy-start(f32[1,2,512,1024]{3,2,1,0:T(8,128)} %param.4) | copy-start | bytes 12582916
  2.8 1.6 %copy-start.3 = (bf16[1,2,512,1024]{3,2,1,0:T(8,128)(2,1)S(1)}, bf16[1,2,512,1024]{3,2,1,0:T(8,128)(2,1)}, u32[]{:S(2)}) copy-start(bf16[1,2,512,1024]{3,2,1,0:T(8,128)(2,1)} %param.3) | copy-start | bytes 6291460
  4.4 1.2 copy-start.5
  5.6 51.2 %copy-start.4 = (bf16[1,2,512,1024]{3,2,1,0:T(8,128)(2,1)S(1)}, bf16[1,2,512,1024]{3,2,1,0:T(8,128)(2,1)}, u32[]{:S(2)}) copy-start(bf16[1,2,512,1024]{3,2,1,0:T(8,128)(2,1)} %param.3) | copy-start | bytes 6291460
  36.5 20.3 %all-to-all-start.1 = ((f32[32,2,16,128]{3,2,1,0:T(8,128)}), f32[32,2,16,128]{3,2,1,0:T(8,128)S(1)}, u32[]{:S(2)}, u32[]{:S(2)}) async-start(f32[32,2,16,128]{3,2,1,0:T(8,128)} %broadcast_in_dim.11), calls=%async_computation.1 | async-start | bytes 1048576 | tf_op jit(solution)/shard_map/all_to_all | solution.py:191
  56.8 2.2 %copy-start.1 = (f32[1,2,512,1024]{3,2,1,0:T(8,128)S(1)}, f32[1,2,512,1024]{3,2,1,0:T(8,128)}, u32[]{:S(2)}) copy-start(f32[1,2,512,1024]{3,2,1,0:T(8,128)} %param.4) | copy-start | bytes 12582916
  62.0 1.0 copy-start.6
  63.8 5.5 %collective-permute-start.2 = (f32[16,8,8,128]{3,2,1,0:T(8,128)}, f32[16,8,8,128]{3,2,1,0:T(8,128)S(1)}, u32[]{:S(2)}, u32[]{:S(2)}) collective-permute-start(f32[16,8,8,128]{3,2,1,0:T(8,128)} %dynamic-slice_bitcast_fusion), channel_id=1, source_target_pairs={{0,1},{1,0},{2,3},{3,2},{4,5},{5,4},{6,7},{7,6},{8,9},{9,8},{10,11... | collective-permute-start | bytes 1572872 | tf_op jit(solution)/shard_map/ppermute | solution.py:195
  98.6 23.9 %all-to-all-start.4 = ((f32[128,8,128]{2,1,0:T(8,128)}), f32[128,8,128]{2,1,0:T(8,128)S(1)}, u32[]{:S(2)}, u32[]{:S(2)}) async-start(f32[128,8,128]{2,1,0:T(8,128)} %broadcast_in_dim.13), calls=%async_computation.4 | async-start | bytes 1048576 | tf_op jit(solution)/shard_map/all_to_all | solution.py:191
  105.3 21.6 %collective-permute-start = (f32[128,128]{1,0:T(8,128)S(1)}, f32[128,128]{1,0:T(8,128)S(1)}, u32[]{:S(2)}, u32[]{:S(2)}) collective-permute-start(f32[128,128]{1,0:T(8,128)S(1)} %dynamic-slice_bitcast_fusion.1), channel_id=1, source_target_pairs={{0,1},{1,0},{2,3},{3,2},{4,5},{5,4},{6,7},{7,6},{8,9},{9,8},{10,11... | collective-permute-start | bytes 196616 | tf_op jit(solution)/shard_map/ppermute | solution.py:195
  122.4 26.3 %collective-permute-start.3 = (f32[16,8,8,128]{3,2,1,0:T(8,128)S(1)}, f32[16,8,8,128]{3,2,1,0:T(8,128)S(1)}, u32[]{:S(2)}, u32[]{:S(2)}) collective-permute-start(f32[16,8,8,128]{3,2,1,0:T(8,128)S(1)} %bitcast.26), channel_id=1, source_target_pairs={{0,1},{1,0},{2,3},{3,2},{4,5},{5,4},{6,7},{7,6},{8,9},{9,8},{10,11... | collective-permute-start | bytes 1572872 | tf_op jit(solution)/shard_map/ppermute | solution.py:195
  146.7 2.0 %collective-permute-start.1 = (f32[128,128]{1,0:T(8,128)S(1)}, f32[128,128]{1,0:T(8,128)S(1)}, u32[]{:S(2)}, u32[]{:S(2)}) collective-permute-start(f32[128,128]{1,0:T(8,128)S(1)} %inverse_factor.1), channel_id=1, source_target_pairs={{0,1},{1,0},{2,3},{3,2},{4,5},{5,4},{6,7},{7,6},{8,9},{9,8},{10,11... | collective-permute-start | bytes 196616 | tf_op jit(solution)/shard_map/ppermute | solution.py:195
  148.9 2.2 %copy-start.2 = (f32[1,2,512,1024]{3,2,1,0:T(8,128)S(1)}, f32[1,2,512,1024]{3,2,1,0:T(8,128)}, u32[]{:S(2)}) copy-start(f32[1,2,512,1024]{3,2,1,0:T(8,128)} %param.4) | copy-start | bytes 12582916

commit v2 on v0

v2 whole, which is shorter than its diff:
```python
import functools
import math

import jax
import jax.numpy as jnp
from jax import lax
from jax.experimental import pallas as pl
from jax.experimental.pallas import tpu as pltpu
from jax.sharding import Mesh, PartitionSpec as P

FEATURES = 4096
WIDTH = 1024
RANK = 128
MATRICES = 2
ROWS = 512
ridge_relative = 0.001
ridge_absolute = 1e-06
MIB = 1 << 20
f32 = jnp.float32
bf16 = jnp.bfloat16


def halves(x):
    high = x.astype(bf16)
    return high, (x - high.astype(f32)).astype(bf16)


def dot(a, b, dims):
    return lax.dot_general(a, b, (dims, ((), ())), preferred_element_type=f32)


def in_vmem(x):
    return pltpu.with_memory_space_constraint(x, pltpu.VMEM)


def in_hbm(x):
    return pltpu.with_memory_space_constraint(x, pltpu.HBM)


NN = ((1,), (0,))
NT = ((1,), (1,))
TN = ((0,), (0,))


def dot_wide(a, b):
    a_high, a_low = halves(a)
    b_high, b_low = halves(b)
    both = dot(a_high, jnp.concatenate([b_high, b_low], axis=1), NN)
    return both[:, :RANK] + (both[:, RANK:] + dot(a_low, b_high, NN))


def dot_deep(a, b):
    a_high, a_low = halves(a)
    b_high, b_low = halves(b)
    both = jnp.concatenate([a_high, a_low], axis=1)
    return dot(both, jnp.concatenate([b_high, b_high], axis=1), NT) + dot(a_high, b_low, NT)


def left_kernel(which, gradient, feedback, prior, left, merged, gradient_in, feedback_in, prior_in, sems, prior_sem):
    del which
    steps = gradient_in.shape[0]
    rows = ROWS * MATRICES // steps
    per = steps // MATRICES

    def fetch(i):
        m, at = i // per, i % per * rows
        return (
            pltpu.make_async_copy(gradient.at[m, pl.ds(at, rows)], gradient_in.at[i], sems.at[0, i]),
            pltpu.make_async_copy(feedback.at[m, pl.ds(at, rows)], feedback_in.at[i], sems.at[1, i]),
        )

    def fetch_prior(m):
        return pltpu.make_async_copy(prior.at[m], prior_in.at[m], prior_sem.at[m])

    for i in range(steps):
        if i % per == 0:
            fetch_prior(i // per).start()
        for copy in fetch(i):
            copy.start()
    for i in range(steps):
        m, at = i // per, i % per * rows
        if at == 0:
            fetch_prior(m).wait()
        for copy in fetch(i):
            copy.wait()
        total = gradient_in[i].astype(f32) + feedback_in[i]
        merged[m, at : at + rows] = total
        left[at // 16 : (at + rows) // 16, m] = dot_wide(total, prior_in[m]).reshape(rows // 16, 16, RANK)


def left_terms(which, gradient, feedback, right_prior, steps=4):
    rows = ROWS * MATRICES // steps
    return pl.pallas_call(
        left_kernel,
        in_specs=[pl.BlockSpec(memory_space=pltpu.SMEM)] + [pl.BlockSpec(memory_space=pltpu.HBM)] * 3,
        out_specs=[pl.BlockSpec(memory_space=pltpu.VMEM)] * 2,
        out_shape=[
            jax.ShapeDtypeStruct((ROWS // 16, MATRICES, 16, RANK), f32),
            jax.ShapeDtypeStruct((MATRICES, ROWS, WIDTH), f32),
        ],
        scratch_shapes=[
            pltpu.VMEM((steps, rows, WIDTH), bf16),
            pltpu.VMEM((steps, rows, WIDTH), f32),
            pltpu.VMEM((MATRICES, WIDTH, RANK), f32),
            pltpu.SemaphoreType.DMA((2, steps)),
            pltpu.SemaphoreType.DMA((MATRICES,)),
        ],
        compiler_params=pltpu.CompilerParams(vmem_limit_bytes=24 * MIB),
        name="left_terms",
    )(which, gradient, feedback, right_prior)


def stacked(left):
    return jnp.concatenate(halves(left), axis=1)


def gram_of(both):
    square = dot(both, both, TN)
    return square[:RANK, :RANK] + (square[RANK:, :RANK] + square[:RANK, RANK:] + square[RANK:, RANK:])


def right_kernel(which, merged, left_mean, right, *grams):
    i = which[0]
    both = stacked(left_mean[:, i].reshape(ROWS, RANK))
    if grams:
        grams[0][...] = gram_of(both)
        grams[1][...] = gram_of(stacked(left_mean[:, 1 - i].reshape(ROWS, RANK)))
    cols = WIDTH // 2
    for at in range(0, WIDTH, cols):
        merged_high, merged_low = halves(merged[i, :, at : at + cols])
        double = dot(both, merged_high, TN)
        total = double[:RANK] + (double[RANK:] + dot(both[:, :RANK], merged_low, TN))
        right[at : at + cols] = total.T


def right_terms(which, merged, left_mean, with_gram):
    square = jax.ShapeDtypeStruct((RANK, RANK), f32)
    return pl.pallas_call(
        right_kernel,
        in_specs=[pl.BlockSpec(memory_space=pltpu.SMEM)] + [pl.BlockSpec(memory_space=pltpu.VMEM)] * 2,
        out_shape=[jax.ShapeDtypeStruct((WIDTH, RANK), f32)] + [square] * (2 * with_gram),
        compiler_params=pltpu.CompilerParams(vmem_limit_bytes=24 * MIB),
        cost_estimate=pl.CostEstimate(flops=8 * 10**8, bytes_accessed=4 * 10**6, transcendentals=0),
        name="right_terms",
    )(which, merged, left_mean)


def tree_sum(terms):
    while len(terms) > 1:
        terms = [a + b for a, b in zip(terms[::2], terms[1::2])]
    return terms[0]


def inverse_kernel(gram, one, two, three, out):
    rows = lax.broadcasted_iota(jnp.int32, (RANK, RANK), 0)
    cols = lax.broadcasted_iota(jnp.int32, (RANK, RANK), 1)
    diagonal = rows == cols
    matrix = (gram[...] + one[...] + (two[...] + three[...])) * (1.0 / FEATURES)
    trace = jnp.sum(jnp.where(diagonal, matrix, 0.0))
    ridge = ridge_relative * (trace / RANK) + ridge_absolute
    matrix = jnp.where(diagonal, matrix + ridge, matrix)
    unit = jnp.where(diagonal, 1.0, 0.0)
    panels = RANK // 8
    left = [matrix[8 * q : 8 * q + 8] for q in range(panels)]
    right = [unit[8 * q : 8 * q + 8] for q in range(panels)]
    row = lax.broadcasted_iota(jnp.int32, (8, RANK), 0)

    def wide(x):
        return jnp.broadcast_to(x, (8, RANK))

    for p in range(panels):
        at = 8 * p
        col = [wide(left[p][:, at + j : at + j + 1]) for j in range(8)]
        solved_left, solved_right, reduced = left[p], right[p], right[p]
        pivots = scales = jnp.ones((8, RANK), f32)
        for j in range(8):
            pivot = wide(col[j][j : j + 1])
            scale = 1.0 / pivot
            factor = col[j] * scale
            below = jnp.where(row > j, factor, 0.0)
            beside = jnp.where(row != j, factor, 0.0)
            pivots = jnp.where(row == j, pivot, pivots)
            scales = jnp.where(row == j, scale, scales)
            row_left, row_right = wide(solved_left[j : j + 1]), wide(reduced[j : j + 1])
            for t in range(j + 1, 8):
                col[t] = col[t] - beside * wide(col[t][j : j + 1])
            solved_left = solved_left - beside * row_left
            solved_right = solved_right - beside * row_right
            reduced = reduced - below * row_right
        out[at : at + 8] = reduced * lax.rsqrt(pivots)
        solved_left, solved_right = solved_left * scales, solved_right * scales
        row_left = [wide(solved_left[j : j + 1]) for j in range(8)]
        row_right = [wide(solved_right[j : j + 1]) for j in range(8)]
        for q in range(p + 1, panels):
            col = [wide(left[q][:, at + j : at + j + 1]) for j in range(8)]
            left[q] = left[q] - tree_sum([c * r for c, r in zip(col, row_left)])
            right[q] = right[q] - tree_sum([c * r for c, r in zip(col, row_right)])


def inverse_factor(*grams):
    return pl.pallas_call(
        inverse_kernel,
        out_shape=jax.ShapeDtypeStruct((RANK, RANK), f32),
        compiler_params=pltpu.CompilerParams(vmem_limit_bytes=16 * MIB),
        cost_estimate=pl.CostEstimate(flops=3 * 10**9, bytes_accessed=10**5, transcendentals=0),
        name="inverse_factor",
    )(*grams)


def basis_kernel(core, left_mean, own, other, basis, operand, token):
    token[...] = jnp.zeros(token.shape, f32)
    for i, inverse in ((core[0], own), (1 - core[0], other)):
        rows = dot_wide(left_mean[:, i].reshape(ROWS, RANK), inverse[...].T)
        basis[i] = rows
        operand[i] = stacked(rows * (1.0 / math.sqrt(FEATURES)))


def basis_rows(core, left_mean, own, other):
    return pl.pallas_call(
        basis_kernel,
        in_specs=[pl.BlockSpec(memory_space=pltpu.SMEM)] + [pl.BlockSpec(memory_space=pltpu.VMEM)] * 3,
        out_shape=[
            jax.ShapeDtypeStruct((MATRICES, ROWS, RANK), f32),
            jax.ShapeDtypeStruct((MATRICES, ROWS, 2 * RANK), bf16),
            jax.ShapeDtypeStruct((8, RANK), f32),
        ],
        compiler_params=pltpu.CompilerParams(vmem_limit_bytes=16 * MIB),
        cost_estimate=pl.CostEstimate(flops=8 * 10**8, bytes_accessed=2 * 10**6, transcendentals=0),
        name="basis_rows",
    )(core, left_mean, own, other)


def factor_kernel(parts, inverse, out):
    total = tree_sum([parts[i] for i in range(parts.shape[0])])
    rows = dot_wide(total, inverse[...].T) * (1.0 / (32 * math.sqrt(FEATURES)))
    for i in range(out.shape[0]):
        out[i] = rows


def factor_rows(parts, inverse, copies):
    return pl.pallas_call(
        factor_kernel,
        out_shape=jax.ShapeDtypeStruct((copies,) + parts.shape[1:], f32),
        compiler_params=pltpu.CompilerParams(vmem_limit_bytes=16 * MIB),
        cost_estimate=pl.CostEstimate(flops=10**8, bytes_accessed=4 * 10**5, transcendentals=0),
        name="factor_rows",
    )(parts, inverse)


def tie_kernel(x, after, out):
    del x, after, out


def tie(x, after):
    return pl.pallas_call(
        tie_kernel,
        in_specs=[pl.BlockSpec(memory_space=pl.ANY), pl.BlockSpec(memory_space=pltpu.VMEM)],
        out_specs=pl.BlockSpec(memory_space=pl.ANY),
        out_shape=pltpu.VMEM(x.shape, x.dtype),
        input_output_aliases={0: 0},
        compiler_params=pltpu.CompilerParams(vmem_limit_bytes=MIB),
        name="tie",
    )(in_vmem(x), after)


def finish_kernel(which, gradient, feedback, operand, right, *rest):
    renewed, factor, gradient_in, feedback_in, renewed_out, turned, sems = rest[-7:]
    w = which[0]
    steps = gradient_in.shape[0]
    rows = ROWS // steps

    def fetch(i):
        at = pl.ds(i * rows, rows)
        return (
            pltpu.make_async_copy(gradient.at[w, at], gradient_in.at[i], sems.at[0, i]),
            pltpu.make_async_copy(feedback.at[w, at], feedback_in.at[i], sems.at[1, i]),
        )

    def store(i):
        return pltpu.make_async_copy(renewed_out.at[i], renewed.at[w, pl.ds(i * rows, rows)], sems.at[2, i])

    for i in range(steps):
        for copy in fetch(i):
            copy.start()
    store_factor = pltpu.make_async_copy(right, factor.at[w], sems.at[2, steps])
    store_factor.start()
    high, low = halves(right[...])
    turned[:, :RANK] = high
    turned[:, RANK : 2 * RANK] = high
    turned[:, 2 * RANK :] = low
    for i in range(steps):
        both = operand[w, i * rows : (i + 1) * rows]
        approx = dot(both, turned[:, : 2 * RANK], NT) + dot(both[:, :RANK], turned[:, 2 * RANK :], NT)
        for copy in fetch(i):
            copy.wait()
        renewed_out[i] = gradient_in[i].astype(f32) + feedback_in[i] - approx
        store(i).start()
    store_factor.wait()
    for i in range(steps):
        store(i).wait()


def finish(which, gradient, feedback, operand, right, before=(), steps=2):
    rows = ROWS // steps
    return pl.pallas_call(
        finish_kernel,
        in_specs=[pl.BlockSpec(memory_space=pltpu.SMEM)]
        + [pl.BlockSpec(memory_space=pltpu.HBM)] * 2
        + [pl.BlockSpec(memory_space=pltpu.VMEM)] * 2
        + [pl.BlockSpec(memory_space=pl.ANY)] * len(before),
        out_specs=[pl.BlockSpec(memory_space=pl.ANY)] * 2,
        out_shape=[
            jax.ShapeDtypeStruct((MATRICES, ROWS, WIDTH), f32),
            jax.ShapeDtypeStruct((MATRICES, WIDTH, RANK), f32),
        ],
        scratch_shapes=[
            pltpu.VMEM((steps, rows, WIDTH), bf16),
            pltpu.VMEM((steps, rows, WIDTH), f32),
            pltpu.VMEM((steps, rows, WIDTH), f32),
            pltpu.VMEM((WIDTH, 3 * RANK), bf16),
            pltpu.SemaphoreType.DMA((3, steps + 1)),
        ],
        input_output_aliases={5: 0, 6: 1} if before else {},
        compiler_params=pltpu.CompilerParams(vmem_limit_bytes=24 * MIB),
        cost_estimate=pl.CostEstimate(flops=8 * 10**8, bytes_accessed=6 * 10**6, transcendentals=0),
        name="finish",
    )(which, gradient, feedback, operand, right, *before)


def share_kernel(parts, *rest, scale):
    total = tree_sum([parts[i] for i in range(parts.shape[0])]) * scale
    out = rest[-1]
    for i in range(out.shape[0]):
        out[i] = total


def share(parts, copies, scale, after=()):
    return pl.pallas_call(
        functools.partial(share_kernel, scale=scale),
        out_shape=jax.ShapeDtypeStruct((copies,) + parts.shape[1:], f32),
        compiler_params=pltpu.CompilerParams(vmem_limit_bytes=8 * MIB),
        name="share",
    )(parts, *after)


def add_kernel(*refs):
    pairs = len(refs) // 3
    for i in range(pairs):
        refs[2 * pairs + i][...] = refs[2 * i][...] + refs[2 * i + 1][...]


def add_pairs(*arrays):
    return pl.pallas_call(
        add_kernel,
        out_shape=[jax.ShapeDtypeStruct(x.shape, f32) for x in arrays[::2]],
        compiler_params=pltpu.CompilerParams(vmem_limit_bytes=8 * MIB),
        name="add_pairs",
    )(*arrays)


def exchange(x, axes):
    return lax.all_to_all(x, axes, 0, 0, tiled=True)


def swap(x):
    return lax.ppermute(x, "core", [(0, 1), (1, 0)])


def shards(gradient, feedback, right_prior):
    own = lax.axis_index("core")[None]
    other = 1 - own
    rep, plane = ("z", "y"), ("y", "x")
    gradient, feedback, right_prior = in_hbm(gradient[0]), in_hbm(feedback[0]), in_hbm(right_prior)
    left, merged = left_terms(other, gradient, feedback, right_prior)
    left_mean = exchange(share(exchange(left, rep), 32, 1.0 / 32), rep)

    right_other, gram_other, gram = right_terms(other, merged, left_mean, True)
    right_other, gram_other = swap(right_other), swap(gram_other)
    right = right_terms(own, merged, left_mean, False)[0]
    total, gram = add_pairs(right, right_other, gram, gram_other)

    total = exchange(total.reshape(16, WIDTH // 16, RANK), plane)
    grams = [lax.ppermute(gram, "x", [(i, (i + s) % 4) for i in range(4)]) for s in (1, 3, 2)]
    total = exchange(share(total, 8, 1.0, grams), "z")
    inverse = inverse_factor(gram, *grams)
    right = exchange(factor_rows(total, inverse, 16), plane).reshape(WIDTH, RANK)
    basis, operand, token = basis_rows(own, left_mean, inverse, swap(inverse))
    right = tie(right, token)

    done = finish(own, gradient, feedback, operand, right)
    renewed, factor = finish(other, gradient, feedback, operand, swap(right), tuple(done))
    return renewed[None], basis, factor


def solution(mesh):
    chips = Mesh(mesh.devices.reshape(8, 4, 4, 2), ("z", "y", "x", "core"))
    rep, fsdp = ("z", "y"), ("x", "core")
    in_specs = (P(rep, None, fsdp, None), P(rep, None, fsdp, None), P())
    out_specs = (P(rep, None, fsdp, None), P(None, fsdp, None), P())
    return jax.shard_map(shards, mesh=chips, in_specs=in_specs, out_specs=out_specs, check_vma=False)
```

time: 561 us -> 119 us (0.21)
  waiting for transfers between devices: 464 us -> 17.2 us
  other arithmetic: 49.4 us -> 0 us
  blocking collectives: 0 us -> 48.2 us
  starting transfers between devices: 0.12 us -> 30.7 us
  matrix products: 28.6 us -> 0 us
  Pallas kernels: 0 us -> 21.8 us
  between operations: 13.8 us -> 0.73 us
    psum x3 -> x0, waiting for transfers between devices: 464 us -> none  [the longest x1 254 us: wide_sum(): return lax.psum((pieces[0],), ('rep', 'fsdp'))]
    all_to_all x0 -> x2, blocking collectives: none -> 48.2 us  [exchange(): return lax.all_to_all(x, axes, 0, 0, tiled=True)]
    another operation x7 -> x0, other arithmetic: 44.4 us -> none  [the longest x4 24.4 us: factorize(): return jnp.linalg.cholesky(shifted)]
    dot_general x4 -> x0, matrix products: 26.9 us -> none  [the longest x1 9.82 us: shards(): jnp.einsum('mdk,mdr->mkr', merged, left_basis, precision=highest)]
    pallas_call x0 -> x12, Pallas kernels: none -> 21.8 us  [the longest x2 7.21 us: finish(): pl.pallas_call(finish_kernel, in_specs=[pl.BlockSpec(memory_space=pltpu.S...]
    ppermute x0 -> x7, starting transfers between devices: none -> 15.4 us  [the longest x4 11 us: swap(): return lax.ppermute(x, 'core', [(0, 1), (1, 0)])]
    all_to_all x0 -> x3, starting transfers between devices: none -> 15.3 us  [exchange(): return lax.all_to_all(x, axes, 0, 0, tiled=True)]
    ppermute x0 -> x7, waiting for transfers between devices: none -> 8.96 us  [the longest x3 7.3 us: shards(): lax.ppermute(gram, 'x', [(i, (i + s) % 4) for i in range(4)])]
  transfers between devices with their start and end apart: 3 -> 10, of which waited for: 3 -> 6; matrix products, arithmetic and copies ran while one was open for 0% -> 0% of each run, Pallas kernels for 0% -> 9%
where the time goes in v2:
time: 119 us
  blocking collectives  48.2 us (41%)
  starting transfers between devices  30.7 us (26%)
  Pallas kernels  21.8 us (18%)
  waiting for transfers between devices  17.2 us (14%)
    all_to_all x2, blocking collectives, exchange(): return lax.all_to_all(x, axes, 0, 0, tiled=True)  48.2 us
    all_to_all x3, starting transfers between devices, exchange(): return lax.all_to_all(x, axes, 0, 0, tiled=True)  15.3 us
    ppermute x4, starting transfers between devices, swap(): return lax.ppermute(x, 'core', [(0, 1), (1, 0)])  11 us
    all_to_all x3, waiting for transfers between devices, exchange(): return lax.all_to_all(x, axes, 0, 0, tiled=True)  8.29 us
    ppermute x3, waiting for transfers between devices, shards(): lax.ppermute(gram, 'x', [(i, (i + s) % 4) for i in range(4)])  7.3 us
    pallas_call x2, Pallas kernels, finish(): pl.pallas_call(finish_kernel, in_specs=[pl.BlockSpec(memory_space=pltpu.S...  7.21 us
    pallas_call x1, Pallas kernels, inverse_factor(): pl.pallas_call(inverse_kernel, out_shape=jax.ShapeDtypeStruct((RANK, RANK...  4.63 us
    pallas_call x1, Pallas kernels, left_terms(): pl.pallas_call(left_kernel, in_specs=[pl.BlockSpec(memory_space=pltpu.SME...  4.36 us
  transfers between devices with their start and end apart: 10, of which 6 were waited for; matrix products, arithmetic and copies ran while one was open for 0% of the time, Pallas kernels for 9%

profile of v2, /device:TPU:1, one launch (start us, length us, event | category | flops | bytes accessed | tf_op | source)
XLA Modules:
  0.0 118.7 jit_solution(17453472553186800282)
XLA Ops:
  0.6 4.4 %left_terms.1 = (f32[32,2,16,128]{3,2,1,0:T(8,128)S(1)}, f32[2,512,1024]{2,1,0:T(8,128)S(1)}) custom-call(s32[1]{0:T(128)S(6)} %sub.3.which, bf16[2,512,1024]{2,1,0:T(8,128)(2,1)} %bitcast.10, f32[2,512,1024]{2,1,0:T(8,128)} %bitcast.7, f32[2,1024,128]{2,1,0:T(8,128)} %prior.1), custom_call_target="tpu_custom_call" | custom-call | tf_op jit(solution)/shard_map/left_terms/pallas_call | solution.py:93
  5.0 28.1 %all_to_all.25.parts = f32[32,2,16,128]{3,2,1,0:T(8,128)S(1)} all-to-all(f32[32,2,16,128]{3,2,1,0:T(8,128)S(1)} %get-tuple-element.17), channel_id=1, replica_groups=mesh['z'=8,'y'=4,'x'=4,'core'=2] {'z','y'}, dimensions={0} | all-to-all | bytes 1048576 | tf_op jit(solution)/shard_map/all_to_all | solution.py:362
  33.1 0.1 share.2
  33.2 20.1 %all_to_all.26.left_mean = f32[32,2,16,128]{3,2,1,0:T(8,128)S(1)} all-to-all(f32[32,2,16,128]{3,2,1,0:T(8,128)S(1)} %share.2), channel_id=1, replica_groups=mesh['z'=8,'y'=4,'x'=4,'core'=2] {'z','y'}, dimensions={0} | all-to-all | bytes 1048576 | tf_op jit(solution)/shard_map/all_to_all | solution.py:362
  53.3 0.9 right_terms.3
  54.2 3.8 %collective-permute-start = (f32[1024,128]{1,0:T(8,128)S(1)}, f32[1024,128]{1,0:T(8,128)S(1)}, u32[]{:S(2)}, u32[]{:S(2)}) collective-permute-start(f32[1024,128]{1,0:T(8,128)S(1)} %get-tuple-element.19), channel_id=1, source_target_pairs={{0,1},{1,0},{2,3},{3,2},{4,5},{5,4},{6,7},{7,6},{8,9},{9,8},{10,11... | collective-permute-start | bytes 1572872 | tf_op jit(solution)/shard_map/ppermute | solution.py:366
  58.0 0.1 collective-permute-start.1
  58.1 0.8 right_terms.2.refs_0_
  58.9 0.8 collective-permute-done.1.refs_3_
  59.6 0.0 collective-permute-done.refs_1_
  59.6 0.9 add_pairs.1
  60.5 5.8 %all-to-all-start.2 = ((f32[16,64,128]{2,1,0:T(8,128)}), f32[16,64,128]{2,1,0:T(8,128)S(1)}, u32[]{:S(2)}, u32[]{:S(2)}) async-start(f32[16,64,128]{2,1,0:T(8,128)} %bitcast.3), calls=%async_computation.2 | async-start | bytes 1048576 | tf_op jit(solution)/shard_map/all_to_all | solution.py:362
  66.3 2.9 %collective-permute-start.4 = (f32[128,128]{1,0:T(8,128)S(1)}, f32[128,128]{1,0:T(8,128)S(1)}, u32[]{:S(2)}, u32[]{:S(2)}) collective-permute-start(f32[128,128]{1,0:T(8,128)S(1)} %get-tuple-element.22.gram), channel_id=1, source_target_pairs={{0,4},{2,6},{4,0},{6,2},{1,5},{3,7},{5,1},{7,3},{8,12},{10,14},{12... | collective-permute-start | bytes 196616 | tf_op jit(solution)/shard_map/ppermute | solution.py:383
  69.2 0.9 collective-permute-start.3
  70.1 0.6 collective-permute-start.2
  70.7 6.0 %collective-permute-done.4.three.rest_2_ = f32[128,128]{1,0:T(8,128)S(1)} collective-permute-done((f32[128,128]{1,0:T(8,128)S(1)}, f32[128,128]{1,0:T(8,128)S(1)}, u32[]{:S(2)}, u32[]{:S(2)}) %collective-permute-start.4) | collective-permute-done | bytes 65568 | tf_op jit(solution)/shard_map/ppermute | solution.py:383
  76.6 0.0 collective-permute-done.3.two.rest_1_
  76.6 1.3 %collective-permute-done.2.one.rest_0_ = f32[128,128]{1,0:T(8,128)S(1)} collective-permute-done((f32[128,128]{1,0:T(8,128)S(1)}, f32[128,128]{1,0:T(8,128)S(1)}, u32[]{:S(2)}, u32[]{:S(2)}) %collective-permute-start.2) | collective-permute-done | bytes 65568 | tf_op jit(solution)/shard_map/ppermute | solution.py:383
  78.0 0.0 all-to-all-done.2.parts
  78.0 0.7 share.3
  78.7 3.4 %all-to-all-start.3 = ((f32[8,64,128]{2,1,0:T(8,128)}), f32[8,64,128]{2,1,0:T(8,128)S(1)}, u32[]{:S(2)}, u32[]{:S(2)}) async-start(f32[8,64,128]{2,1,0:T(8,128)} %share.3), calls=%async_computation.3 | async-start | bytes 524288 | tf_op jit(solution)/shard_map/all_to_all | solution.py:362
  82.1 4.6 %inverse_factor.1.own.inverse = f32[128,128]{1,0:T(8,128)S(1)} custom-call(f32[128,128]{1,0:T(8,128)S(1)} %get-tuple-element.22.gram, f32[128,128]{1,0:T(8,128)S(1)} %collective-permute-done.2.one.rest_0_, f32[128,128]{1,0:T(8,128)S(1)} %collective-permute-done.3.two.rest_1_, f32[128,128]{1,0:T(8,128)S(1)} %collective-permute-done.4.three.rest_2_), custom_call_target="tpu_custom_call" | custom-call | flops 3000000000 | bytes 100000 | tf_op jit(solution)/shard_map/inverse_factor/pallas_call | solution.py:201
  86.8 4.5 %all-to-all-done.3.parts = f32[8,64,128]{2,1,0:T(8,128)S(1)} async-done(((f32[8,64,128]{2,1,0:T(8,128)}), f32[8,64,128]{2,1,0:T(8,128)S(1)}, u32[]{:S(2)}, u32[]{:S(2)}) %all-to-all-start.3) | async-done | bytes 262176 | tf_op jit(solution)/shard_map/all_to_all | solution.py:362
  91.2 1.1 factor_rows.1
  92.3 6.1 %all-to-all-start.4 = ((f32[16,64,128]{2,1,0:T(8,128)}), f32[16,64,128]{2,1,0:T(8,128)S(1)}, u32[]{:S(2)}, u32[]{:S(2)}) async-start(f32[16,64,128]{2,1,0:T(8,128)} %factor_rows.1), calls=%async_computation.4 | async-start | bytes 1048576 | tf_op jit(solution)/shard_map/all_to_all | solution.py:362
  98.4 3.0 %collective-permute-start.5 = (f32[128,128]{1,0:T(8,128)S(1)}, f32[128,128]{1,0:T(8,128)S(1)}, u32[]{:S(2)}, u32[]{:S(2)}) collective-permute-start(f32[128,128]{1,0:T(8,128)S(1)} %inverse_factor.1.own.inverse), channel_id=1, source_target_pairs={{0,1},{1,0},{2,3},{3,2},{4,5},{5,4},{6,7},{7,6},{8,9},{9,8},{10,11... | collective-permute-start | bytes 196616 | tf_op jit(solution)/shard_map/ppermute | solution.py:366
  101.4 0.9 collective-permute-done.5.other
  102.3 1.2 %basis_rows.1 = (f32[2,512,128]{2,1,0:T(8,128)}, bf16[2,512,256]{2,1,0:T(8,128)(2,1)S(1)}, f32[8,128]{1,0:T(8,128)S(1)}) custom-call(s32[1]{0:T(128)} %bitcast.which.core, f32[32,2,16,128]{3,2,1,0:T(8,128)S(1)} %all_to_all.26.left_mean, f32[128,128]{1,0:T(8,128)S(1)} %inverse_factor.1.own.inverse, f32[128,128]{1,0:T(8,128)S(1)} %collective-permute-done.5.other), custom_call_target="tpu_custom_call" | custom-call | flops 800000000 | bytes 2000000 | tf_op jit(solution)/shard_map/basis_rows/pallas_call | solution.py:219
  103.6 3.8 %all-to-all-done.4 = f32[16,64,128]{2,1,0:T(8,128)S(1)} async-done(((f32[16,64,128]{2,1,0:T(8,128)}), f32[16,64,128]{2,1,0:T(8,128)S(1)}, u32[]{:S(2)}, u32[]{:S(2)}) %all-to-all-start.4) | async-done | bytes 524320 | tf_op jit(solution)/shard_map/all_to_all | solution.py:362
  107.4 4.1 %collective-permute-start.6 = (f32[1024,128]{1,0:T(8,128)S(1)}, f32[1024,128]{1,0:T(8,128)S(1)}, u32[]{:S(2)}, u32[]{:S(2)}) collective-permute-start(f32[1024,128]{1,0:T(8,128)S(1)} %tie.1.right), channel_id=1, source_target_pairs={{0,1},{1,0},{2,3},{3,2},{4,5},{5,4},{6,7},{7,6},{8,9},{9,8},{10,11... | collective-permute-start | bytes 1572872 | tf_op jit(solution)/shard_map/ppermute | solution.py:366
  111.5 3.6 %finish.2 = (f32[2,512,1024]{2,1,0:T(8,128)}, f32[2,1024,128]{2,1,0:T(8,128)}) custom-call(s32[1]{0:T(128)} %bitcast.which.core, bf16[2,512,1024]{2,1,0:T(8,128)(2,1)} %bitcast.11, f32[2,512,1024]{2,1,0:T(8,128)} %bitcast.8, bf16[2,512,256]{2,1,0:T(8,128)(2,1)S(1)} %get-tuple-element.23.operand, f32[1024,128]{1,0:T(8,128)S(1)} %tie.1.right), custom_call_target="tpu_custom_call" | custom-call | flops 800000000 | bytes 6000000 | tf_op jit(solution)/shard_map/finish/pallas_call | solution.py:305
  115.1 0.0 collective-permute-done.6.right
  115.1 3.6 %finish.3 = (f32[2,512,1024]{2,1,0:T(8,128)}, f32[2,1024,128]{2,1,0:T(8,128)}) custom-call(s32[1]{0:T(128)S(6)} %sub.3.which, bf16[2,512,1024]{2,1,0:T(8,128)(2,1)} %bitcast.12, f32[2,512,1024]{2,1,0:T(8,128)} %bitcast.9, bf16[2,512,256]{2,1,0:T(8,128)(2,1)S(1)} %get-tuple-element.23.operand, ...), custom_call_target="tpu_custom_call", output_to_operand_aliasing={{0}: (5, {}), {1}: (6, {})} | custom-call | flops 800000000 | bytes 6000000 | tf_op jit(solution)/shard_map/finish/pallas_call | solution.py:305
  (1 shorter events, 0.0 us)
Async XLA Ops:
  54.2 5.5 %collective-permute-start = (f32[1024,128]{1,0:T(8,128)S(1)}, f32[1024,128]{1,0:T(8,128)S(1)}, u32[]{:S(2)}, u32[]{:S(2)}) collective-permute-start(f32[1024,128]{1,0:T(8,128)S(1)} %get-tuple-element.19), channel_id=1, source_target_pairs={{0,1},{1,0},{2,3},{3,2},{4,5},{5,4},{6,7},{7,6},{8,9},{9,8},{10,11... | collective-permute-start | bytes 1572872 | tf_op jit(solution)/shard_map/ppermute | solution.py:366
  58.0 1.6 %collective-permute-start.1 = (f32[128,128]{1,0:T(8,128)S(1)}, f32[128,128]{1,0:T(8,128)S(1)}, u32[]{:S(2)}, u32[]{:S(2)}) collective-permute-start(f32[128,128]{1,0:T(8,128)S(1)} %get-tuple-element.21), channel_id=1, source_target_pairs={{0,1},{1,0},{2,3},{3,2},{4,5},{5,4},{6,7},{7,6},{8,9},{9,8},{10,11... | collective-permute-start | bytes 196616 | tf_op jit(solution)/shard_map/ppermute | solution.py:366
  60.5 17.5 %all-to-all-start.2 = ((f32[16,64,128]{2,1,0:T(8,128)}), f32[16,64,128]{2,1,0:T(8,128)S(1)}, u32[]{:S(2)}, u32[]{:S(2)}) async-start(f32[16,64,128]{2,1,0:T(8,128)} %bitcast.3), calls=%async_computation.2 | async-start | bytes 1048576 | tf_op jit(solution)/shard_map/all_to_all | solution.py:362
  66.3 10.3 %collective-permute-start.4 = (f32[128,128]{1,0:T(8,128)S(1)}, f32[128,128]{1,0:T(8,128)S(1)}, u32[]{:S(2)}, u32[]{:S(2)}) collective-permute-start(f32[128,128]{1,0:T(8,128)S(1)} %get-tuple-element.22.gram), channel_id=1, source_target_pairs={{0,4},{2,6},{4,0},{6,2},{1,5},{3,7},{5,1},{7,3},{8,12},{10,14},{12... | collective-permute-start | bytes 196616 | tf_op jit(solution)/shard_map/ppermute | solution.py:383
  69.2 7.4 %collective-permute-start.3 = (f32[128,128]{1,0:T(8,128)S(1)}, f32[128,128]{1,0:T(8,128)S(1)}, u32[]{:S(2)}, u32[]{:S(2)}) collective-permute-start(f32[128,128]{1,0:T(8,128)S(1)} %get-tuple-element.22.gram), channel_id=1, source_target_pairs={{0,6},{2,0},{4,2},{6,4},{1,7},{3,1},{5,3},{7,5},{8,14},{10,8},{12,... | collective-permute-start | bytes 196616 | tf_op jit(solution)/shard_map/ppermute | solution.py:383
  70.1 7.9 %collective-permute-start.2 = (f32[128,128]{1,0:T(8,128)S(1)}, f32[128,128]{1,0:T(8,128)S(1)}, u32[]{:S(2)}, u32[]{:S(2)}) collective-permute-start(f32[128,128]{1,0:T(8,128)S(1)} %get-tuple-element.22.gram), channel_id=1, source_target_pairs={{0,2},{2,4},{4,6},{6,0},{1,3},{3,5},{5,7},{7,1},{8,10},{10,12},{12... | collective-permute-start | bytes 196616 | tf_op jit(solution)/shard_map/ppermute | solution.py:383
  78.7 12.5 %all-to-all-start.3 = ((f32[8,64,128]{2,1,0:T(8,128)}), f32[8,64,128]{2,1,0:T(8,128)S(1)}, u32[]{:S(2)}, u32[]{:S(2)}) async-start(f32[8,64,128]{2,1,0:T(8,128)} %share.3), calls=%async_computation.3 | async-start | bytes 524288 | tf_op jit(solution)/shard_map/all_to_all | solution.py:362
  92.3 15.1 %all-to-all-start.4 = ((f32[16,64,128]{2,1,0:T(8,128)}), f32[16,64,128]{2,1,0:T(8,128)S(1)}, u32[]{:S(2)}, u32[]{:S(2)}) async-start(f32[16,64,128]{2,1,0:T(8,128)} %factor_rows.1), calls=%async_computation.4 | async-start | bytes 1048576 | tf_op jit(solution)/shard_map/all_to_all | solution.py:362
  98.4 3.9 %collective-permute-start.5 = (f32[128,128]{1,0:T(8,128)S(1)}, f32[128,128]{1,0:T(8,128)S(1)}, u32[]{:S(2)}, u32[]{:S(2)}) collective-permute-start(f32[128,128]{1,0:T(8,128)S(1)} %inverse_factor.1.own.inverse), channel_id=1, source_target_pairs={{0,1},{1,0},{2,3},{3,2},{4,5},{5,4},{6,7},{7,6},{8,9},{9,8},{10,11... | collective-permute-start | bytes 196616 | tf_op jit(solution)/shard_map/ppermute | solution.py:366
  107.4 7.7 %collective-permute-start.6 = (f32[1024,128]{1,0:T(8,128)S(1)}, f32[1024,128]{1,0:T(8,128)S(1)}, u32[]{:S(2)}, u32[]{:S(2)}) collective-permute-start(f32[1024,128]{1,0:T(8,128)S(1)} %tie.1.right), channel_id=1, source_target_pairs={{0,1},{1,0},{2,3},{3,2},{4,5},{5,4},{6,7},{7,6},{8,9},{9,8},{10,11... | collective-permute-start | bytes 1572872 | tf_op jit(solution)/shard_map/ppermute | solution.py:366

commit v3 on v2

--- a/solution.py
+++ b/solution.py
@@ -13,6 +13,10 @@
 RANK = 128
 MATRICES = 2
 ROWS = 512
+CHUNK = 64
+BOX = 32
+SHARE = WIDTH // BOX
+PIECE = 16
 ridge_relative = 0.001
 ridge_absolute = 1e-06
 MIB = 1 << 20
@@ -56,8 +60,8 @@
     return dot(both, jnp.concatenate([b_high, b_high], axis=1), NT) + dot(a_high, b_low, NT)
 
 
-def left_kernel(which, gradient, feedback, prior, left, merged, gradient_in, feedback_in, prior_in, sems, prior_sem):
-    del which
+def left_kernel(other, place, gradient, feedback, prior, left, merged, gradient_in, feedback_in, prior_in, sems, prior_sem):
+    del other, place
     steps = gradient_in.shape[0]
     rows = ROWS * MATRICES // steps
     per = steps // MATRICES
@@ -85,17 +89,17 @@
             copy.wait()
         total = gradient_in[i].astype(f32) + feedback_in[i]
         merged[m, at : at + rows] = total
-        left[at // 16 : (at + rows) // 16, m] = dot_wide(total, prior_in[m]).reshape(rows // 16, 16, RANK)
-
-
-def left_terms(which, gradient, feedback, right_prior, steps=4):
+        left[at // CHUNK : (at + rows) // CHUNK, m] = dot_wide(total, prior_in[m]).reshape(rows // CHUNK, CHUNK, RANK)
+
+
+def left_terms(other, place, gradient, feedback, right_prior, steps=4):
     rows = ROWS * MATRICES // steps
     return pl.pallas_call(
         left_kernel,
-        in_specs=[pl.BlockSpec(memory_space=pltpu.SMEM)] + [pl.BlockSpec(memory_space=pltpu.HBM)] * 3,
+        in_specs=[pl.BlockSpec(memory_space=pltpu.SMEM)] * 2 + [pl.BlockSpec(memory_space=pltpu.HBM)] * 3,
         out_specs=[pl.BlockSpec(memory_space=pltpu.VMEM)] * 2,
         out_shape=[
-            jax.ShapeDtypeStruct((ROWS // 16, MATRICES, 16, RANK), f32),
+            jax.ShapeDtypeStruct((ROWS // CHUNK, MATRICES, CHUNK, RANK), f32),
             jax.ShapeDtypeStruct((MATRICES, ROWS, WIDTH), f32),
         ],
         scratch_shapes=[
@@ -107,7 +111,7 @@
         ],
         compiler_params=pltpu.CompilerParams(vmem_limit_bytes=24 * MIB),
         name="left_terms",
-    )(which, gradient, feedback, right_prior)
+    )(other, place, gradient, feedback, right_prior)
 
 
 def stacked(left):
@@ -151,11 +155,11 @@
     return terms[0]
 
 
-def inverse_kernel(gram, one, two, three, out):
+def inverse_kernel(gram, out):
     rows = lax.broadcasted_iota(jnp.int32, (RANK, RANK), 0)
     cols = lax.broadcasted_iota(jnp.int32, (RANK, RANK), 1)
     diagonal = rows == cols
-    matrix = (gram[...] + one[...] + (two[...] + three[...])) * (1.0 / FEATURES)
+    matrix = gram[...] * (1.0 / FEATURES)
     trace = jnp.sum(jnp.where(diagonal, matrix, 0.0))
     ridge = ridge_relative * (trace / RANK) + ridge_absolute
     matrix = jnp.where(diagonal, matrix + ridge, matrix)
@@ -197,14 +201,14 @@
             right[q] = right[q] - tree_sum([c * r for c, r in zip(col, row_right)])
 
 
-def inverse_factor(*grams):
+def inverse_factor(gram):
     return pl.pallas_call(
         inverse_kernel,
         out_shape=jax.ShapeDtypeStruct((RANK, RANK), f32),
         compiler_params=pltpu.CompilerParams(vmem_limit_bytes=16 * MIB),
         cost_estimate=pl.CostEstimate(flops=3 * 10**9, bytes_accessed=10**5, transcendentals=0),
         name="inverse_factor",
-    )(*grams)
+    )(gram)
 
 
 def basis_kernel(core, left_mean, own, other, basis, operand, token):
@@ -230,8 +234,9 @@
     )(core, left_mean, own, other)
 
 
-def factor_kernel(parts, inverse, out):
-    total = tree_sum([parts[i] for i in range(parts.shape[0])])
+def factor_kernel(*refs):
+    *parts, inverse, out = refs
+    total = tree_sum([part[...] for part in parts])
     rows = dot_wide(total, inverse[...].T) * (1.0 / (32 * math.sqrt(FEATURES)))
     for i in range(out.shape[0]):
         out[i] = rows
@@ -240,11 +245,11 @@
 def factor_rows(parts, inverse, copies):
     return pl.pallas_call(
         factor_kernel,
-        out_shape=jax.ShapeDtypeStruct((copies,) + parts.shape[1:], f32),
+        out_shape=jax.ShapeDtypeStruct((copies,) + parts[0].shape, f32),
         compiler_params=pltpu.CompilerParams(vmem_limit_bytes=16 * MIB),
         cost_estimate=pl.CostEstimate(flops=10**8, bytes_accessed=4 * 10**5, transcendentals=0),
         name="factor_rows",
-    )(parts, inverse)
+    )(*parts, inverse)
 
 
 def tie_kernel(x, after, out):
@@ -263,99 +268,172 @@
     )(in_vmem(x), after)
 
 
-def finish_kernel(which, gradient, feedback, operand, right, *rest):
-    renewed, factor, gradient_in, feedback_in, renewed_out, turned, sems = rest[-7:]
+def fetches(which, gradient, feedback, gradient_in, feedback_in, sems, i):
+    rows = gradient_in.shape[1]
+    at = pl.ds(i * rows, rows)
+    return (
+        pltpu.make_async_copy(gradient.at[which, at], gradient_in.at[i], sems.at[0, i]),
+        pltpu.make_async_copy(feedback.at[which, at], feedback_in.at[i], sems.at[1, i]),
+    )
+
+
+def merge_arrived(which, gradient, feedback, gradient_in, feedback_in, sems, merged):
+    steps, rows, _ = gradient_in.shape
+    for i in range(steps):
+        for copy in fetches(which, gradient, feedback, gradient_in, feedback_in, sems, i):
+            copy.wait()
+        merged[i * rows : (i + 1) * rows] = gradient_in[i].astype(f32) + feedback_in[i]
+
+
+def fetch_scratch(steps):
+    rows = ROWS // steps
+    return [
+        pltpu.VMEM((steps, rows, WIDTH), bf16),
+        pltpu.VMEM((steps, rows, WIDTH), f32),
+        pltpu.SemaphoreType.DMA((2, steps)),
+    ]
+
+
+def merge_kernel(which, gradient, feedback, after, merged, token, *scratch):
+    del after
+    token[...] = jnp.zeros(token.shape, f32)
+    arrays = (which[0], gradient, feedback, *scratch)
+    for i in range(scratch[0].shape[0]):
+        for copy in fetches(*arrays, i):
+            copy.start()
+    merge_arrived(*arrays, merged)
+
+
+def merge(which, gradient, feedback, after):
+    return pl.pallas_call(
+        merge_kernel,
+        in_specs=[pl.BlockSpec(memory_space=pltpu.SMEM)]
+        + [pl.BlockSpec(memory_space=pltpu.HBM)] * 2
+        + [pl.BlockSpec(memory_space=pltpu.VMEM)],
+        out_shape=[jax.ShapeDtypeStruct((ROWS, WIDTH), f32), jax.ShapeDtypeStruct((8, RANK), f32)],
+        scratch_shapes=fetch_scratch(2),
+        compiler_params=pltpu.CompilerParams(vmem_limit_bytes=16 * MIB),
+        cost_estimate=pl.CostEstimate(flops=10**8, bytes_accessed=5 * 10**6, transcendentals=0),
+        name="merge",
+    )(which, gradient, feedback, after)
+
+
+def finish_kernel(which, merged, operand, right, *rest):
+    *rest, renewed_out, turned, sems = rest
     w = which[0]
-    steps = gradient_in.shape[0]
-    rows = ROWS // steps
-
-    def fetch(i):
-        at = pl.ds(i * rows, rows)
-        return (
-            pltpu.make_async_copy(gradient.at[w, at], gradient_in.at[i], sems.at[0, i]),
-            pltpu.make_async_copy(feedback.at[w, at], feedback_in.at[i], sems.at[1, i]),
-        )
+    steps, rows, _ = renewed_out.shape
+    if len(rest) > 4:
+        gradient, feedback, renewed, factor, merged_next, *scratch = rest
+        arrays = (1 - w, gradient, feedback, *scratch)
+        for i in range(scratch[0].shape[0]):
+            for copy in fetches(*arrays, i):
+                copy.start()
+    else:
+        renewed, factor = rest[-2:]
 
     def store(i):
-        return pltpu.make_async_copy(renewed_out.at[i], renewed.at[w, pl.ds(i * rows, rows)], sems.at[2, i])
-
-    for i in range(steps):
-        for copy in fetch(i):
-            copy.start()
-    store_factor = pltpu.make_async_copy(right, factor.at[w], sems.at[2, steps])
-    store_factor.start()
+        return pltpu.make_async_copy(renewed_out.at[i], renewed.at[w, pl.ds(i * rows, rows)], sems.at[i])
+
+    store_factor = pltpu.make_async_copy(right, factor.at[w], sems.at[steps])
     high, low = halves(right[...])
     turned[:, :RANK] = high
     turned[:, RANK : 2 * RANK] = high
     turned[:, 2 * RANK :] = low
     for i in range(steps):
-        both = operand[w, i * rows : (i + 1) * rows]
+        at = slice(i * rows, (i + 1) * rows)
+        both = operand[w, at]
         approx = dot(both, turned[:, : 2 * RANK], NT) + dot(both[:, :RANK], turned[:, 2 * RANK :], NT)
-        for copy in fetch(i):
-            copy.wait()
-        renewed_out[i] = gradient_in[i].astype(f32) + feedback_in[i] - approx
+        renewed_out[i] = merged[at] - approx
         store(i).start()
-    store_factor.wait()
+    store_factor.start()
+    if len(rest) > 4:
+        merge_arrived(*arrays, merged_next)
     for i in range(steps):
         store(i).wait()
-
-
-def finish(which, gradient, feedback, operand, right, before=(), steps=2):
+    store_factor.wait()
+
+
+def finish(which, merged, operand, right, ahead=(), before=(), steps=2):
     rows = ROWS // steps
+    outs = [
+        jax.ShapeDtypeStruct((MATRICES, ROWS, WIDTH), f32),
+        jax.ShapeDtypeStruct((MATRICES, WIDTH, RANK), f32),
+    ]
     return pl.pallas_call(
         finish_kernel,
         in_specs=[pl.BlockSpec(memory_space=pltpu.SMEM)]
-        + [pl.BlockSpec(memory_space=pltpu.HBM)] * 2
-        + [pl.BlockSpec(memory_space=pltpu.VMEM)] * 2
+        + [pl.BlockSpec(memory_space=pltpu.VMEM)] * 3
+        + [pl.BlockSpec(memory_space=pltpu.HBM)] * len(ahead)
         + [pl.BlockSpec(memory_space=pl.ANY)] * len(before),
-        out_specs=[pl.BlockSpec(memory_space=pl.ANY)] * 2,
-        out_shape=[
-            jax.ShapeDtypeStruct((MATRICES, ROWS, WIDTH), f32),
-            jax.ShapeDtypeStruct((MATRICES, WIDTH, RANK), f32),
-        ],
-        scratch_shapes=[
-            pltpu.VMEM((steps, rows, WIDTH), bf16),
-            pltpu.VMEM((steps, rows, WIDTH), f32),
+        out_specs=[pl.BlockSpec(memory_space=pl.ANY)] * 2 + [pl.BlockSpec(memory_space=pltpu.VMEM)] * bool(ahead),
+        out_shape=outs + [jax.ShapeDtypeStruct((ROWS, WIDTH), f32)] * bool(ahead),
+        scratch_shapes=fetch_scratch(2) * bool(ahead)
+        + [
             pltpu.VMEM((steps, rows, WIDTH), f32),
             pltpu.VMEM((WIDTH, 3 * RANK), bf16),
-            pltpu.SemaphoreType.DMA((3, steps + 1)),
+            pltpu.SemaphoreType.DMA((steps + 1,)),
         ],
-        input_output_aliases={5: 0, 6: 1} if before else {},
+        input_output_aliases={4: 0, 5: 1} if before else {},
         compiler_params=pltpu.CompilerParams(vmem_limit_bytes=24 * MIB),
         cost_estimate=pl.CostEstimate(flops=8 * 10**8, bytes_accessed=6 * 10**6, transcendentals=0),
         name="finish",
-    )(which, gradient, feedback, operand, right, *before)
-
-
-def share_kernel(parts, *rest, scale):
-    total = tree_sum([parts[i] for i in range(parts.shape[0])]) * scale
-    out = rest[-1]
+    )(which, merged, operand, right, *ahead, *before)
+
+
+def share_kernel(*refs, scale, count):
+    parts, out = refs[:count], refs[-1]
+    if count == 1:
+        parts = [parts[0][i] for i in range(parts[0].shape[0])]
+    else:
+        parts = [part[0] for part in parts]
+    total = tree_sum(parts) * scale
     for i in range(out.shape[0]):
         out[i] = total
 
 
 def share(parts, copies, scale, after=()):
-    return pl.pallas_call(
-        functools.partial(share_kernel, scale=scale),
-        out_shape=jax.ShapeDtypeStruct((copies,) + parts.shape[1:], f32),
+    parts = parts if isinstance(parts, list) else [parts]
+    return pl.pallas_call(
+        functools.partial(share_kernel, scale=scale, count=len(parts)),
+        out_shape=jax.ShapeDtypeStruct((copies,) + parts[0].shape[1:], f32),
         compiler_params=pltpu.CompilerParams(vmem_limit_bytes=8 * MIB),
         name="share",
-    )(parts, *after)
-
-
-def add_kernel(*refs):
-    pairs = len(refs) // 3
-    for i in range(pairs):
-        refs[2 * pairs + i][...] = refs[2 * i][...] + refs[2 * i + 1][...]
-
-
-def add_pairs(*arrays):
-    return pl.pallas_call(
-        add_kernel,
-        out_shape=[jax.ShapeDtypeStruct(x.shape, f32) for x in arrays[::2]],
+    )(*parts, *after)
+
+
+def parcel_kernel(place, right, right_other, gram, gram_other, out, gram_sum):
+    gram_sum[...] = gram[...] + gram_other[...]
+    piece = gram_sum[pl.ds(pl.multiple_of(place[0] * PIECE, PIECE), PIECE)]
+    for i in range(BOX):
+        at = slice(i * SHARE, (i + 1) * SHARE)
+        out[i, :SHARE] = right[at] + right_other[at]
+        out[i, SHARE:] = piece
+
+
+def parcels(place, right, right_other, gram, gram_other):
+    return pl.pallas_call(
+        parcel_kernel,
+        in_specs=[pl.BlockSpec(memory_space=pltpu.SMEM)] + [pl.BlockSpec(memory_space=pltpu.VMEM)] * 4,
+        out_shape=jax.ShapeDtypeStruct((BOX, SHARE + PIECE, RANK), f32),
+        scratch_shapes=[pltpu.VMEM((RANK, RANK), f32)],
         compiler_params=pltpu.CompilerParams(vmem_limit_bytes=8 * MIB),
-        name="add_pairs",
-    )(*arrays)
+        name="parcels",
+    )(place, right, right_other, gram, gram_other)
+
+
+def unpack_kernel(parts, total, gram):
+    total[...] = tree_sum([parts[i, :SHARE] for i in range(BOX)])
+    for k in range(RANK // PIECE):
+        gram[k * PIECE : (k + 1) * PIECE] = tree_sum([parts[4 * k + x, SHARE:] for x in range(4)])
+
+
+def unpack(parts):
+    return pl.pallas_call(
+        unpack_kernel,
+        out_shape=[jax.ShapeDtypeStruct((SHARE, RANK), f32), jax.ShapeDtypeStruct((RANK, RANK), f32)],
+        compiler_params=pltpu.CompilerParams(vmem_limit_bytes=8 * MIB),
+        name="unpack",
+    )(parts)
 
 
 def exchange(x, axes):
@@ -364,37 +442,42 @@
 
 def swap(x):
     return lax.ppermute(x, "core", [(0, 1), (1, 0)])
+
+
+def rounds(x, axis):
+    return [x] + [lax.ppermute(x, axis, [(i, (i + s) % 4) for i in range(4)]) for s in (1, 3, 2)]
 
 
 def shards(gradient, feedback, right_prior):
     own = lax.axis_index("core")[None]
     other = 1 - own
-    rep, plane = ("z", "y"), ("y", "x")
+    place = lax.axis_index(("zl", "y"))[None]
+    column, box = ("zl", "y"), ("zl", "y", "x")
     gradient, feedback, right_prior = in_hbm(gradient[0]), in_hbm(feedback[0]), in_hbm(right_prior)
-    left, merged = left_terms(other, gradient, feedback, right_prior)
-    left_mean = exchange(share(exchange(left, rep), 32, 1.0 / 32), rep)
+    left, merged = left_terms(other, place, gradient, feedback, right_prior)
+    left = rounds(share(exchange(left, column), 1, 1.0 / 32), "zh")
+    left_mean = exchange(share(left, 8, 1.0), column)
 
     right_other, gram_other, gram = right_terms(other, merged, left_mean, True)
     right_other, gram_other = swap(right_other), swap(gram_other)
     right = right_terms(own, merged, left_mean, False)[0]
-    total, gram = add_pairs(right, right_other, gram, gram_other)
-
-    total = exchange(total.reshape(16, WIDTH // 16, RANK), plane)
-    grams = [lax.ppermute(gram, "x", [(i, (i + s) % 4) for i in range(4)]) for s in (1, 3, 2)]
-    total = exchange(share(total, 8, 1.0, grams), "z")
-    inverse = inverse_factor(gram, *grams)
-    right = exchange(factor_rows(total, inverse, 16), plane).reshape(WIDTH, RANK)
+    parts = exchange(parcels(place, right, right_other, gram, gram_other), box)
+    total, gram = unpack(parts)
+    totals = rounds(total, "zh")
+    inverse = inverse_factor(gram)
+    right = exchange(factor_rows(totals, inverse, 32), box).reshape(WIDTH, RANK)
     basis, operand, token = basis_rows(own, left_mean, inverse, swap(inverse))
+    merged, token = merge(own, gradient, feedback, token)
     right = tie(right, token)
 
-    done = finish(own, gradient, feedback, operand, right)
-    renewed, factor = finish(other, gradient, feedback, operand, swap(right), tuple(done))
+    *done, merged = finish(own, merged, operand, right, (gradient, feedback))
+    renewed, factor = finish(other, merged, operand, swap(right), (), tuple(done))
     return renewed[None], basis, factor
 
 
 def solution(mesh):
-    chips = Mesh(mesh.devices.reshape(8, 4, 4, 2), ("z", "y", "x", "core"))
-    rep, fsdp = ("z", "y"), ("x", "core")
+    chips = Mesh(mesh.devices.reshape(4, 2, 4, 4, 2), ("zh", "zl", "y", "x", "core"))
+    rep, fsdp = ("zh", "zl", "y"), ("x", "core")
     in_specs = (P(rep, None, fsdp, None), P(rep, None, fsdp, None), P())
     out_specs = (P(rep, None, fsdp, None), P(None, fsdp, None), P())
     return jax.shard_map(shards, mesh=chips, in_specs=in_specs, out_specs=out_specs, check_vma=False)

time: 119 us -> 104 us (0.87)
  waiting for transfers between devices: 17.2 us -> 8.42 us
  blocking collectives: 48.2 us -> 43.6 us
  Pallas kernels: 21.8 us -> 20.5 us
    ppermute x3 -> x6, starting transfers between devices: 4.34 us -> 14.9 us  [rounds(): lax.ppermute(x, axis, [(i, (i + s) % 4) for i in range(4)])]
    all_to_all x3 -> x1, starting transfers between devices: 15.3 us -> 6.03 us  [exchange(): return lax.all_to_all(x, axes, 0, 0, tiled=True)]
    all_to_all x3 -> x1, waiting for transfers between devices: 8.29 us -> 3.22 us  [exchange(): return lax.all_to_all(x, axes, 0, 0, tiled=True)]
    all_to_all x2 -> x3, blocking collectives: 48.2 us -> 43.6 us  [exchange(): return lax.all_to_all(x, axes, 0, 0, tiled=True)]
    ppermute x3 -> x6, waiting for transfers between devices: 7.3 us -> 3.53 us  [rounds(): lax.ppermute(x, axis, [(i, (i + s) % 4) for i in range(4)])]
    pallas_call x2, Pallas kernels: 7.21 us -> 5.34 us  [finish(): pl.pallas_call(finish_kernel, in_specs=[pl.BlockSpec(memory_space=pltpu.S...]
    ppermute x4, starting transfers between devices: 11 us -> 9.77 us  [swap(): return lax.ppermute(x, 'core', [(0, 1), (1, 0)])]
  transfers between devices with their start and end apart: 10 -> 11, of which waited for: 6 -> 4; matrix products, arithmetic and copies ran while one was open for 0% -> 0% of each run, Pallas kernels for 9% -> 11%
where the time goes in v3:
time: 104 us
  blocking collectives  43.6 us (42%)
  starting transfers between devices  30.7 us (30%)
  Pallas kernels  20.5 us (20%)
  waiting for transfers between devices  8.42 us (8%)
    all_to_all x3, blocking collectives, exchange(): return lax.all_to_all(x, axes, 0, 0, tiled=True)  43.6 us
    ppermute x6, starting transfers between devices, rounds(): lax.ppermute(x, axis, [(i, (i + s) % 4) for i in range(4)])  14.9 us
    ppermute x4, starting transfers between devices, swap(): return lax.ppermute(x, 'core', [(0, 1), (1, 0)])  9.77 us
    all_to_all x1, starting transfers between devices, exchange(): return lax.all_to_all(x, axes, 0, 0, tiled=True)  6.03 us
    pallas_call x2, Pallas kernels, finish(): pl.pallas_call(finish_kernel, in_specs=[pl.BlockSpec(memory_space=pltpu.S...  5.34 us
    pallas_call x1, Pallas kernels, inverse_factor(): pl.pallas_call(inverse_kernel, out_shape=jax.ShapeDtypeStruct((RANK, RANK...  4.62 us
    pallas_call x1, Pallas kernels, left_terms(): pl.pallas_call(left_kernel, in_specs=[pl.BlockSpec(memory_space=pltpu.SME...  4.35 us
    ppermute x6, waiting for transfers between devices, rounds(): lax.ppermute(x, axis, [(i, (i + s) % 4) for i in range(4)])  3.53 us
  transfers between devices with their start and end apart: 11, of which 4 were waited for; matrix products, arithmetic and copies ran while one was open for 0% of the time, Pallas kernels for 11%

profile of v3, /device:TPU:1, one launch (start us, length us, event | category | flops | bytes accessed | tf_op | source)
XLA Modules:
  0.0 104.1 jit_solution(650233885778393902)
XLA Ops:
  0.6 4.4 %left_terms.1 = (f32[8,2,64,128]{3,2,1,0:T(8,128)S(1)}, f32[2,512,1024]{2,1,0:T(8,128)S(1)}) custom-call(s32[1]{0:T(128)S(6)} %sub.3.other.which, s32[1]{0:T(128)} %bitcast.3.place, bf16[2,512,1024]{2,1,0:T(8,128)(2,1)} %bitcast.10, f32[2,512,1024]{2,1,0:T(8,128)} %bitcast.7, f32[2,1024,128]{2,1,0:T(8,128)} %prior.1), custom_call_target="tpu_custom_call" | custom-call | tf_op jit(solution)/shard_map/left_terms/pallas_call | solution.py:97
  5.0 14.8 %all_to_all.20.refs_0_ = f32[8,2,64,128]{3,2,1,0:T(8,128)S(1)} all-to-all(f32[8,2,64,128]{3,2,1,0:T(8,128)S(1)} %get-tuple-element.20), channel_id=1, replica_groups=mesh['zh'=4,'zl'=2,'y'=4,'x'=4,'core'=2] {'zl','y'}, dimensions={0} | all-to-all | bytes 1048576 | tf_op jit(solution)/shard_map/all_to_all | solution.py:440
  19.8 6.1 %collective-permute-start.2 = (f32[1,2,64,128]{3,2,1,0:T(8,128)S(1)}, f32[1,2,64,128]{3,2,1,0:T(8,128)S(1)}, u32[]{:S(2)}, u32[]{:S(2)}) collective-permute-start(f32[1,2,64,128]{3,2,1,0:T(8,128)S(1)} %share.2.refs_0_), channel_id=1, source_target_pairs={{0,128},{64,192},{128,0},{192,64},{1,129},{65,193},{129,1},{193,65... | collective-permute-start | bytes 196616 | tf_op jit(solution)/shard_map/ppermute | solution.py:448
  25.9 0.3 collective-permute-start.1
  26.2 2.1 %collective-permute-start = (f32[1,2,64,128]{3,2,1,0:T(8,128)S(1)}, f32[1,2,64,128]{3,2,1,0:T(8,128)S(1)}, u32[]{:S(2)}, u32[]{:S(2)}) collective-permute-start(f32[1,2,64,128]{3,2,1,0:T(8,128)S(1)} %share.2.refs_0_), channel_id=1, source_target_pairs={{0,64},{64,128},{128,192},{192,0},{1,65},{65,129},{129,193},{193,1... | collective-permute-start | bytes 196616 | tf_op jit(solution)/shard_map/ppermute | solution.py:448
  28.3 0.0 collective-permute-done.2.refs_3_
  28.3 3.5 %collective-permute-done.1.refs_2_ = f32[1,2,64,128]{3,2,1,0:T(8,128)S(1)} collective-permute-done((f32[1,2,64,128]{3,2,1,0:T(8,128)S(1)}, f32[1,2,64,128]{3,2,1,0:T(8,128)S(1)}, u32[]{:S(2)}, u32[]{:S(2)}) %collective-permute-start.1) | collective-permute-done | bytes 65568 | tf_op jit(solution)/shard_map/ppermute | solution.py:448
  31.8 0.0 collective-permute-done.refs_1_
  31.9 11.2 %all_to_all.21.left_mean = f32[8,2,64,128]{3,2,1,0:T(8,128)S(1)} all-to-all(f32[8,2,64,128]{3,2,1,0:T(8,128)S(1)} %share.3), channel_id=1, replica_groups=mesh['zh'=4,'zl'=2,'y'=4,'x'=4,'core'=2] {'zl','y'}, dimensions={0} | all-to-all | bytes 1048576 | tf_op jit(solution)/shard_map/all_to_all | solution.py:440
  43.0 0.9 right_terms.3
  43.9 4.5 %collective-permute-start.3 = (f32[1024,128]{1,0:T(8,128)S(1)}, f32[1024,128]{1,0:T(8,128)S(1)}, u32[]{:S(2)}, u32[]{:S(2)}) collective-permute-start(f32[1024,128]{1,0:T(8,128)S(1)} %get-tuple-element.22), channel_id=1, source_target_pairs={{0,1},{1,0},{2,3},{3,2},{4,5},{5,4},{6,7},{7,6},{8,9},{9,8},{10,11... | collective-permute-start | bytes 1572872 | tf_op jit(solution)/shard_map/ppermute | solution.py:444
  48.5 0.1 collective-permute-start.4
  48.6 0.8 right_terms.2.right
  49.3 0.8 collective-permute-done.4.gram_other
  50.1 0.0 collective-permute-done.3.right_other
  50.1 0.1 parcels.1
  50.2 17.6 %all_to_all.22.parts = f32[32,48,128]{2,1,0:T(8,128)S(1)} all-to-all(f32[32,48,128]{2,1,0:T(8,128)S(1)} %parcels.1), channel_id=1, replica_groups=mesh['zh'=4,'zl'=2,'y'=4,'x'=4,'core'=2] {'zl','y','x'}, dimensions={0} | all-to-all | bytes 1572864 | tf_op jit(solution)/shard_map/all_to_all | solution.py:440
  67.8 4.1 %collective-permute-start.8 = (f32[32,128]{1,0:T(8,128)S(1)}, f32[32,128]{1,0:T(8,128)S(1)}, u32[]{:S(2)}, u32[]{:S(2)}) collective-permute-start(f32[32,128]{1,0:T(8,128)S(1)} %get-tuple-element.29.refs_0_), channel_id=1, source_target_pairs={{0,128},{64,192},{128,0},{192,64},{1,129},{65,193},{129,1},{193,65... | collective-permute-start | bytes 49160 | tf_op jit(solution)/shard_map/ppermute | solution.py:448
  71.9 0.3 collective-permute-start.7
  72.2 2.0 %collective-permute-start.6 = (f32[32,128]{1,0:T(8,128)S(1)}, f32[32,128]{1,0:T(8,128)S(1)}, u32[]{:S(2)}, u32[]{:S(2)}) collective-permute-start(f32[32,128]{1,0:T(8,128)S(1)} %get-tuple-element.29.refs_0_), channel_id=1, source_target_pairs={{0,64},{64,128},{128,192},{192,0},{1,65},{65,129},{129,193},{193,1... | collective-permute-start | bytes 49160 | tf_op jit(solution)/shard_map/ppermute | solution.py:448
  74.2 4.6 %inverse_factor.1.own.refs_4_ = f32[128,128]{1,0:T(8,128)S(1)} custom-call(f32[128,128]{1,0:T(8,128)S(1)} %get-tuple-element.25.gram), custom_call_target="tpu_custom_call" | custom-call | flops 3000000000 | bytes 100000 | tf_op jit(solution)/shard_map/inverse_factor/pallas_call | solution.py:205
  78.9 0.0 collective-permute-done.8.refs_3_
  78.9 0.0 collective-permute-done.7.refs_2_
  78.9 0.0 collective-permute-done.6.refs_1_
  78.9 1.1 %factor_rows.1 = f32[32,32,128]{2,1,0:T(8,128)} custom-call(f32[32,128]{1,0:T(8,128)S(1)} %get-tuple-element.29.refs_0_, f32[32,128]{1,0:T(8,128)S(1)} %collective-permute-done.6.refs_1_, f32[32,128]{1,0:T(8,128)S(1)} %collective-permute-done.7.refs_2_, f32[32,128]{1,0:T(8,128)S(1)} %collective-permute-done.8.refs_3_, f32[128,128]{1,0:T(8,128)S(1)} %inverse_factor.1.own.refs_4_), custom_call_target="tpu_custom_call" | custom-call | flops 100000000 | bytes 400000 | tf_op jit(solution)/shard_map/factor_rows/pallas_call | solution.py:246
  80.0 6.0 %all-to-all-start.3 = ((f32[32,32,128]{2,1,0:T(8,128)}), f32[32,32,128]{2,1,0:T(8,128)S(1)}, u32[]{:S(2)}, u32[]{:S(2)}) async-start(f32[32,32,128]{2,1,0:T(8,128)} %factor_rows.1), calls=%async_computation.3 | async-start | bytes 1048576 | tf_op jit(solution)/shard_map/all_to_all | solution.py:440
  86.0 2.0 %collective-permute-start.5 = (f32[128,128]{1,0:T(8,128)S(1)}, f32[128,128]{1,0:T(8,128)S(1)}, u32[]{:S(2)}, u32[]{:S(2)}) collective-permute-start(f32[128,128]{1,0:T(8,128)S(1)} %inverse_factor.1.own.refs_4_), channel_id=1, source_target_pairs={{0,1},{1,0},{2,3},{3,2},{4,5},{5,4},{6,7},{7,6},{8,9},{9,8},{10,11... | collective-permute-start | bytes 196616 | tf_op jit(solution)/shard_map/ppermute | solution.py:444
  88.0 0.9 collective-permute-done.5.other
  88.9 1.2 %basis_rows.1 = (f32[2,512,128]{2,1,0:T(8,128)}, bf16[2,512,256]{2,1,0:T(8,128)(2,1)S(1)}, f32[8,128]{1,0:T(8,128)S(1)}) custom-call(s32[1]{0:T(128)} %bitcast.which.core, f32[8,2,64,128]{3,2,1,0:T(8,128)S(1)} %all_to_all.21.left_mean, f32[128,128]{1,0:T(8,128)S(1)} %inverse_factor.1.own.refs_4_, f32[128,128]{1,0:T(8,128)S(1)} %collective-permute-done.5.other), custom_call_target="tpu_custom_call" | custom-call | flops 800000000 | bytes 2000000 | tf_op jit(solution)/shard_map/basis_rows/pallas_call | solution.py:223
  90.2 2.0 %merge.1 = (f32[512,1024]{1,0:T(8,128)S(1)}, f32[8,128]{1,0:T(8,128)S(1)}) custom-call(s32[1]{0:T(128)} %bitcast.which.core, bf16[2,512,1024]{2,1,0:T(8,128)(2,1)} %bitcast.11, f32[2,512,1024]{2,1,0:T(8,128)} %bitcast.8, f32[8,128]{1,0:T(8,128)S(1)} %get-tuple-element.26.after), custom_call_target="tpu_custom_call" | custom-call | flops 100000000 | bytes 5000000 | tf_op jit(solution)/shard_map/merge/pallas_call | solution.py:308
  92.2 3.2 %all-to-all-done.3 = f32[32,32,128]{2,1,0:T(8,128)S(1)} async-done(((f32[32,32,128]{2,1,0:T(8,128)}), f32[32,32,128]{2,1,0:T(8,128)S(1)}, u32[]{:S(2)}, u32[]{:S(2)}) %all-to-all-start.3) | async-done | bytes 524320 | tf_op jit(solution)/shard_map/all_to_all | solution.py:440
  95.4 3.2 %collective-permute-start.9 = (f32[1024,128]{1,0:T(8,128)S(1)}, f32[1024,128]{1,0:T(8,128)S(1)}, u32[]{:S(2)}, u32[]{:S(2)}) collective-permute-start(f32[1024,128]{1,0:T(8,128)S(1)} %tie.1.right), channel_id=1, source_target_pairs={{0,1},{1,0},{2,3},{3,2},{4,5},{5,4},{6,7},{7,6},{8,9},{9,8},{10,11... | collective-permute-start | bytes 1572872 | tf_op jit(solution)/shard_map/ppermute | solution.py:444
  98.5 3.3 %finish.2 = (f32[2,512,1024]{2,1,0:T(8,128)}, f32[2,1024,128]{2,1,0:T(8,128)}, f32[512,1024]{1,0:T(8,128)S(1)}) custom-call(s32[1]{0:T(128)} %bitcast.which.core, f32[512,1024]{1,0:T(8,128)S(1)} %get-tuple-element.27.merged, bf16[2,512,256]{2,1,0:T(8,128)(2,1)S(1)} %get-tuple-element.28.operand, f32[1024,128]{1,0:T(8,128)S(1)} %tie.1.right, ...), custom_call_target="tpu_custom_call" | custom-call | flops 800000000 | bytes 6000000 | tf_op jit(solution)/shard_map/finish/pallas_call | solution.py:362
  101.9 0.0 collective-permute-done.9.right
  101.9 2.0 %finish.3 = (f32[2,512,1024]{2,1,0:T(8,128)}, f32[2,1024,128]{2,1,0:T(8,128)}) custom-call(s32[1]{0:T(128)S(6)} %sub.3.other.which, f32[512,1024]{1,0:T(8,128)S(1)} %get-tuple-element.31.merged, bf16[2,512,256]{2,1,0:T(8,128)(2,1)S(1)} %get-tuple-element.28.operand, ...), custom_call_target="tpu_custom_call", output_to_operand_aliasing={{0}: (4, {}), {1}: (5, {})} | custom-call | flops 800000000 | bytes 6000000 | tf_op jit(solution)/shard_map/finish/pallas_call | solution.py:362
  (4 shorter events, 0.1 us)
Async XLA Ops:
  19.8 8.5 %collective-permute-start.2 = (f32[1,2,64,128]{3,2,1,0:T(8,128)S(1)}, f32[1,2,64,128]{3,2,1,0:T(8,128)S(1)}, u32[]{:S(2)}, u32[]{:S(2)}) collective-permute-start(f32[1,2,64,128]{3,2,1,0:T(8,128)S(1)} %share.2.refs_0_), channel_id=1, source_target_pairs={{0,128},{64,192},{128,0},{192,64},{1,129},{65,193},{129,1},{193,65... | collective-permute-start | bytes 196616 | tf_op jit(solution)/shard_map/ppermute | solution.py:448
  25.9 5.9 %collective-permute-start.1 = (f32[1,2,64,128]{3,2,1,0:T(8,128)S(1)}, f32[1,2,64,128]{3,2,1,0:T(8,128)S(1)}, u32[]{:S(2)}, u32[]{:S(2)}) collective-permute-start(f32[1,2,64,128]{3,2,1,0:T(8,128)S(1)} %share.2.refs_0_), channel_id=1, source_target_pairs={{0,192},{64,0},{128,64},{192,128},{1,193},{65,1},{129,65},{193,129... | collective-permute-start | bytes 196616 | tf_op jit(solution)/shard_map/ppermute | solution.py:448
  26.2 5.6 %collective-permute-start = (f32[1,2,64,128]{3,2,1,0:T(8,128)S(1)}, f32[1,2,64,128]{3,2,1,0:T(8,128)S(1)}, u32[]{:S(2)}, u32[]{:S(2)}) collective-permute-start(f32[1,2,64,128]{3,2,1,0:T(8,128)S(1)} %share.2.refs_0_), channel_id=1, source_target_pairs={{0,64},{64,128},{128,192},{192,0},{1,65},{65,129},{129,193},{193,1... | collective-permute-start | bytes 196616 | tf_op jit(solution)/shard_map/ppermute | solution.py:448
  43.9 6.1 %collective-permute-start.3 = (f32[1024,128]{1,0:T(8,128)S(1)}, f32[1024,128]{1,0:T(8,128)S(1)}, u32[]{:S(2)}, u32[]{:S(2)}) collective-permute-start(f32[1024,128]{1,0:T(8,128)S(1)} %get-tuple-element.22), channel_id=1, source_target_pairs={{0,1},{1,0},{2,3},{3,2},{4,5},{5,4},{6,7},{7,6},{8,9},{9,8},{10,11... | collective-permute-start | bytes 1572872 | tf_op jit(solution)/shard_map/ppermute | solution.py:444
  48.5 1.6 %collective-permute-start.4 = (f32[128,128]{1,0:T(8,128)S(1)}, f32[128,128]{1,0:T(8,128)S(1)}, u32[]{:S(2)}, u32[]{:S(2)}) collective-permute-start(f32[128,128]{1,0:T(8,128)S(1)} %get-tuple-element.24), channel_id=1, source_target_pairs={{0,1},{1,0},{2,3},{3,2},{4,5},{5,4},{6,7},{7,6},{8,9},{9,8},{10,11... | collective-permute-start | bytes 196616 | tf_op jit(solution)/shard_map/ppermute | solution.py:444
  67.8 11.1 %collective-permute-start.8 = (f32[32,128]{1,0:T(8,128)S(1)}, f32[32,128]{1,0:T(8,128)S(1)}, u32[]{:S(2)}, u32[]{:S(2)}) collective-permute-start(f32[32,128]{1,0:T(8,128)S(1)} %get-tuple-element.29.refs_0_), channel_id=1, source_target_pairs={{0,128},{64,192},{128,0},{192,64},{1,129},{65,193},{129,1},{193,65... | collective-permute-start | bytes 49160 | tf_op jit(solution)/shard_map/ppermute | solution.py:448
  71.9 7.0 %collective-permute-start.7 = (f32[32,128]{1,0:T(8,128)S(1)}, f32[32,128]{1,0:T(8,128)S(1)}, u32[]{:S(2)}, u32[]{:S(2)}) collective-permute-start(f32[32,128]{1,0:T(8,128)S(1)} %get-tuple-element.29.refs_0_), channel_id=1, source_target_pairs={{0,192},{64,0},{128,64},{192,128},{1,193},{65,1},{129,65},{193,129... | collective-permute-start | bytes 49160 | tf_op jit(solution)/shard_map/ppermute | solution.py:448
  72.2 6.7 %collective-permute-start.6 = (f32[32,128]{1,0:T(8,128)S(1)}, f32[32,128]{1,0:T(8,128)S(1)}, u32[]{:S(2)}, u32[]{:S(2)}) collective-permute-start(f32[32,128]{1,0:T(8,128)S(1)} %get-tuple-element.29.refs_0_), channel_id=1, source_target_pairs={{0,64},{64,128},{128,192},{192,0},{1,65},{65,129},{129,193},{193,1... | collective-permute-start | bytes 49160 | tf_op jit(solution)/shard_map/ppermute | solution.py:448
  80.0 15.4 %all-to-all-start.3 = ((f32[32,32,128]{2,1,0:T(8,128)}), f32[32,32,128]{2,1,0:T(8,128)S(1)}, u32[]{:S(2)}, u32[]{:S(2)}) async-start(f32[32,32,128]{2,1,0:T(8,128)} %factor_rows.1), calls=%async_computation.3 | async-start | bytes 1048576 | tf_op jit(solution)/shard_map/all_to_all | solution.py:440
  86.0 2.9 %collective-permute-start.5 = (f32[128,128]{1,0:T(8,128)S(1)}, f32[128,128]{1,0:T(8,128)S(1)}, u32[]{:S(2)}, u32[]{:S(2)}) collective-permute-start(f32[128,128]{1,0:T(8,128)S(1)} %inverse_factor.1.own.refs_4_), channel_id=1, source_target_pairs={{0,1},{1,0},{2,3},{3,2},{4,5},{5,4},{6,7},{7,6},{8,9},{9,8},{10,11... | collective-permute-start | bytes 196616 | tf_op jit(solution)/shard_map/ppermute | solution.py:444
  95.4 6.5 %collective-permute-start.9 = (f32[1024,128]{1,0:T(8,128)S(1)}, f32[1024,128]{1,0:T(8,128)S(1)}, u32[]{:S(2)}, u32[]{:S(2)}) collective-permute-start(f32[1024,128]{1,0:T(8,128)S(1)} %tie.1.right), channel_id=1, source_target_pairs={{0,1},{1,0},{2,3},{3,2},{4,5},{5,4},{6,7},{7,6},{8,9},{9,8},{10,11... | collective-permute-start | bytes 1572872 | tf_op jit(solution)/shard_map/ppermute | solution.py:444

commit v4 on v3

--- a/solution.py
+++ b/solution.py
@@ -163,42 +163,51 @@
     trace = jnp.sum(jnp.where(diagonal, matrix, 0.0))
     ridge = ridge_relative * (trace / RANK) + ridge_absolute
     matrix = jnp.where(diagonal, matrix + ridge, matrix)
-    unit = jnp.where(diagonal, 1.0, 0.0)
     panels = RANK // 8
     left = [matrix[8 * q : 8 * q + 8] for q in range(panels)]
-    right = [unit[8 * q : 8 * q + 8] for q in range(panels)]
     row = lax.broadcasted_iota(jnp.int32, (8, RANK), 0)
+    lane = lax.broadcasted_iota(jnp.int32, (8, RANK), 1)
 
     def wide(x):
         return jnp.broadcast_to(x, (8, RANK))
 
     for p in range(panels):
         at = 8 * p
+        here = (lane >= at) & (lane < at + 8)
         col = [wide(left[p][:, at + j : at + j + 1]) for j in range(8)]
-        solved_left, solved_right, reduced = left[p], right[p], right[p]
-        pivots = scales = jnp.ones((8, RANK), f32)
-        for j in range(8):
-            pivot = wide(col[j][j : j + 1])
-            scale = 1.0 / pivot
-            factor = col[j] * scale
-            below = jnp.where(row > j, factor, 0.0)
-            beside = jnp.where(row != j, factor, 0.0)
-            pivots = jnp.where(row == j, pivot, pivots)
-            scales = jnp.where(row == j, scale, scales)
-            row_left, row_right = wide(solved_left[j : j + 1]), wide(reduced[j : j + 1])
-            for t in range(j + 1, 8):
-                col[t] = col[t] - beside * wide(col[t][j : j + 1])
-            solved_left = solved_left - beside * row_left
-            solved_right = solved_right - beside * row_right
-            reduced = reduced - below * row_right
-        out[at : at + 8] = reduced * lax.rsqrt(pivots)
-        solved_left, solved_right = solved_left * scales, solved_right * scales
-        row_left = [wide(solved_left[j : j + 1]) for j in range(8)]
-        row_right = [wide(solved_right[j : j + 1]) for j in range(8)]
+        solved = reduced = jnp.where(here, jnp.where(lane - at == row, 1.0, 0.0), left[p])
+        pivots = same = beside = jnp.ones((8, RANK), f32)
+        for j in range(0, 8, 2):
+            a, b, d = wide(col[j][j : j + 1]), wide(col[j + 1][j : j + 1]), wide(col[j + 1][j + 1 : j + 2])
+            det = a * d - b * b
+            scale = 1.0 / det
+            first, second = row == j, row == j + 1
+            away = (row < j) | (row > j + 1)
+            factor_0 = jnp.where(away, col[j] * d - col[j + 1] * b, 0.0) * scale
+            factor_1 = jnp.where(away, col[j + 1] * a - col[j] * b, 0.0) * scale
+            for t in range(j + 2, 8):
+                col[t] = col[t] - (factor_0 * wide(col[t][j : j + 1]) + factor_1 * wide(col[t][j + 1 : j + 2]))
+            row_0, row_1 = wide(reduced[j : j + 1]), wide(reduced[j + 1 : j + 2])
+            scale_a = 1.0 / a
+            change = factor_0 * row_0 + factor_1 * row_1
+            solved = solved - change
+            reduced = reduced - jnp.where(row > j + 1, change, jnp.where(second, (b * scale_a) * row_0, 0.0))
+            pivots = jnp.where(first, a, jnp.where(second, det * scale_a, pivots))
+            same = jnp.where(first, d * scale, jnp.where(second, a * scale, same))
+            beside = jnp.where(first | second, -(b * scale), beside)
+        out[at : at + 8] = jnp.where(lane < at + 8, reduced * lax.rsqrt(pivots), 0.0)
+        if p + 1 == panels:
+            break
+        partner = jnp.where(
+            row % 2 == 0,
+            jnp.concatenate([solved[1:], solved[:1]], axis=0),
+            jnp.concatenate([solved[7:], solved[:7]], axis=0),
+        )
+        solved = same * solved + beside * partner
+        pieces = [wide(solved[j : j + 1]) for j in range(8)]
         for q in range(p + 1, panels):
-            col = [wide(left[q][:, at + j : at + j + 1]) for j in range(8)]
-            left[q] = left[q] - tree_sum([c * r for c, r in zip(col, row_left)])
-            right[q] = right[q] - tree_sum([c * r for c, r in zip(col, row_right)])
+            terms = [wide(left[q][:, at + j : at + j + 1]) * pieces[j] for j in range(8)]
+            left[q] = jnp.where(here, 0.0, left[q]) - tree_sum(terms)
 
 
 def inverse_factor(gram):
@@ -335,6 +344,7 @@
         return pltpu.make_async_copy(renewed_out.at[i], renewed.at[w, pl.ds(i * rows, rows)], sems.at[i])
 
     store_factor = pltpu.make_async_copy(right, factor.at[w], sems.at[steps])
+    store_factor.start()
     high, low = halves(right[...])
     turned[:, :RANK] = high
     turned[:, RANK : 2 * RANK] = high
@@ -345,7 +355,6 @@
         approx = dot(both, turned[:, : 2 * RANK], NT) + dot(both[:, :RANK], turned[:, 2 * RANK :], NT)
         renewed_out[i] = merged[at] - approx
         store(i).start()
-    store_factor.start()
     if len(rest) > 4:
         merge_arrived(*arrays, merged_next)
     for i in range(steps):

time: 104 us -> 103 us (level)
  Pallas kernels: 20.5 us -> 19.4 us
where the time goes in v4:
time: 103 us
  blocking collectives  43.6 us (42%)
  starting transfers between devices  30.9 us (30%)
  Pallas kernels  19.4 us (19%)
  waiting for transfers between devices  8.42 us (8%)
    all_to_all x3, blocking collectives, exchange(): return lax.all_to_all(x, axes, 0, 0, tiled=True)  43.6 us
    ppermute x6, starting transfers between devices, rounds(): lax.ppermute(x, axis, [(i, (i + s) % 4) for i in range(4)])  14.9 us
    ppermute x4, starting transfers between devices, swap(): return lax.ppermute(x, 'core', [(0, 1), (1, 0)])  9.77 us
    all_to_all x1, starting transfers between devices, exchange(): return lax.all_to_all(x, axes, 0, 0, tiled=True)  6.22 us
    pallas_call x2, Pallas kernels, finish(): pl.pallas_call(finish_kernel, in_specs=[pl.BlockSpec(memory_space=pltpu.S...  4.81 us
    pallas_call x1, Pallas kernels, left_terms(): pl.pallas_call(left_kernel, in_specs=[pl.BlockSpec(memory_space=pltpu.SME...  4.35 us
    pallas_call x1, Pallas kernels, inverse_factor(): pl.pallas_call(inverse_kernel, out_shape=jax.ShapeDtypeStruct((RANK, RANK...  4.06 us
    ppermute x6, waiting for transfers between devices, rounds(): lax.ppermute(x, axis, [(i, (i + s) % 4) for i in range(4)])  3.53 us
  transfers between devices with their start and end apart: 11, of which 4 were waited for; matrix products, arithmetic and copies ran while one was open for 0% of the time, Pallas kernels for 11%

profile of v4, /device:TPU:1, one launch (start us, length us, event | category | flops | bytes accessed | tf_op | source)
XLA Modules:
  0.0 103.1 jit_solution(380515433619704760)
XLA Ops:
  0.6 4.4 %left_terms.1 = (f32[8,2,64,128]{3,2,1,0:T(8,128)S(1)}, f32[2,512,1024]{2,1,0:T(8,128)S(1)}) custom-call(s32[1]{0:T(128)S(6)} %sub.3.other.which, s32[1]{0:T(128)} %bitcast.3.place, bf16[2,512,1024]{2,1,0:T(8,128)(2,1)} %bitcast.10, f32[2,512,1024]{2,1,0:T(8,128)} %bitcast.7, f32[2,1024,128]{2,1,0:T(8,128)} %prior.1), custom_call_target="tpu_custom_call" | custom-call | tf_op jit(solution)/shard_map/left_terms/pallas_call | solution.py:97
  5.0 14.8 %all_to_all.20.refs_0_ = f32[8,2,64,128]{3,2,1,0:T(8,128)S(1)} all-to-all(f32[8,2,64,128]{3,2,1,0:T(8,128)S(1)} %get-tuple-element.20), channel_id=1, replica_groups=mesh['zh'=4,'zl'=2,'y'=4,'x'=4,'core'=2] {'zl','y'}, dimensions={0} | all-to-all | bytes 1048576 | tf_op jit(solution)/shard_map/all_to_all | solution.py:449
  19.8 6.1 %collective-permute-start.2 = (f32[1,2,64,128]{3,2,1,0:T(8,128)S(1)}, f32[1,2,64,128]{3,2,1,0:T(8,128)S(1)}, u32[]{:S(2)}, u32[]{:S(2)}) collective-permute-start(f32[1,2,64,128]{3,2,1,0:T(8,128)S(1)} %share.2.refs_0_), channel_id=1, source_target_pairs={{0,128},{64,192},{128,0},{192,64},{1,129},{65,193},{129,1},{193,65... | collective-permute-start | bytes 196616 | tf_op jit(solution)/shard_map/ppermute | solution.py:457
  25.9 0.3 collective-permute-start.1
  26.2 2.1 %collective-permute-start = (f32[1,2,64,128]{3,2,1,0:T(8,128)S(1)}, f32[1,2,64,128]{3,2,1,0:T(8,128)S(1)}, u32[]{:S(2)}, u32[]{:S(2)}) collective-permute-start(f32[1,2,64,128]{3,2,1,0:T(8,128)S(1)} %share.2.refs_0_), channel_id=1, source_target_pairs={{0,64},{64,128},{128,192},{192,0},{1,65},{65,129},{129,193},{193,1... | collective-permute-start | bytes 196616 | tf_op jit(solution)/shard_map/ppermute | solution.py:457
  28.3 0.0 collective-permute-done.2.refs_3_
  28.3 3.5 %collective-permute-done.1.refs_2_ = f32[1,2,64,128]{3,2,1,0:T(8,128)S(1)} collective-permute-done((f32[1,2,64,128]{3,2,1,0:T(8,128)S(1)}, f32[1,2,64,128]{3,2,1,0:T(8,128)S(1)}, u32[]{:S(2)}, u32[]{:S(2)}) %collective-permute-start.1) | collective-permute-done | bytes 65568 | tf_op jit(solution)/shard_map/ppermute | solution.py:457
  31.8 0.0 collective-permute-done.refs_1_
  31.9 11.2 %all_to_all.21.left_mean = f32[8,2,64,128]{3,2,1,0:T(8,128)S(1)} all-to-all(f32[8,2,64,128]{3,2,1,0:T(8,128)S(1)} %share.3), channel_id=1, replica_groups=mesh['zh'=4,'zl'=2,'y'=4,'x'=4,'core'=2] {'zl','y'}, dimensions={0} | all-to-all | bytes 1048576 | tf_op jit(solution)/shard_map/all_to_all | solution.py:449
  43.0 0.9 right_terms.3
  43.9 4.5 %collective-permute-start.3 = (f32[1024,128]{1,0:T(8,128)S(1)}, f32[1024,128]{1,0:T(8,128)S(1)}, u32[]{:S(2)}, u32[]{:S(2)}) collective-permute-start(f32[1024,128]{1,0:T(8,128)S(1)} %get-tuple-element.22), channel_id=1, source_target_pairs={{0,1},{1,0},{2,3},{3,2},{4,5},{5,4},{6,7},{7,6},{8,9},{9,8},{10,11... | collective-permute-start | bytes 1572872 | tf_op jit(solution)/shard_map/ppermute | solution.py:453
  48.5 0.1 collective-permute-start.4
  48.6 0.8 right_terms.2.right
  49.3 0.8 collective-permute-done.4.gram_other
  50.1 0.0 collective-permute-done.3.right_other
  50.1 0.1 parcels.1
  50.2 17.6 %all_to_all.22.parts = f32[32,48,128]{2,1,0:T(8,128)S(1)} all-to-all(f32[32,48,128]{2,1,0:T(8,128)S(1)} %parcels.1), channel_id=1, replica_groups=mesh['zh'=4,'zl'=2,'y'=4,'x'=4,'core'=2] {'zl','y','x'}, dimensions={0} | all-to-all | bytes 1572864 | tf_op jit(solution)/shard_map/all_to_all | solution.py:449
  67.8 4.1 %collective-permute-start.8 = (f32[32,128]{1,0:T(8,128)S(1)}, f32[32,128]{1,0:T(8,128)S(1)}, u32[]{:S(2)}, u32[]{:S(2)}) collective-permute-start(f32[32,128]{1,0:T(8,128)S(1)} %get-tuple-element.29.refs_0_), channel_id=1, source_target_pairs={{0,128},{64,192},{128,0},{192,64},{1,129},{65,193},{129,1},{193,65... | collective-permute-start | bytes 49160 | tf_op jit(solution)/shard_map/ppermute | solution.py:457
  71.9 0.3 collective-permute-start.7
  72.2 2.0 %collective-permute-start.6 = (f32[32,128]{1,0:T(8,128)S(1)}, f32[32,128]{1,0:T(8,128)S(1)}, u32[]{:S(2)}, u32[]{:S(2)}) collective-permute-start(f32[32,128]{1,0:T(8,128)S(1)} %get-tuple-element.29.refs_0_), channel_id=1, source_target_pairs={{0,64},{64,128},{128,192},{192,0},{1,65},{65,129},{129,193},{193,1... | collective-permute-start | bytes 49160 | tf_op jit(solution)/shard_map/ppermute | solution.py:457
  74.2 4.1 %inverse_factor.1.own.refs_4_ = f32[128,128]{1,0:T(8,128)S(1)} custom-call(f32[128,128]{1,0:T(8,128)S(1)} %get-tuple-element.25.gram), custom_call_target="tpu_custom_call" | custom-call | flops 3000000000 | bytes 100000 | tf_op jit(solution)/shard_map/inverse_factor/pallas_call | solution.py:214
  78.3 0.0 collective-permute-done.8.refs_3_
  78.3 0.0 collective-permute-done.7.refs_2_
  78.3 0.0 collective-permute-done.6.refs_1_
  78.3 1.1 %factor_rows.1 = f32[32,32,128]{2,1,0:T(8,128)} custom-call(f32[32,128]{1,0:T(8,128)S(1)} %get-tuple-element.29.refs_0_, f32[32,128]{1,0:T(8,128)S(1)} %collective-permute-done.6.refs_1_, f32[32,128]{1,0:T(8,128)S(1)} %collective-permute-done.7.refs_2_, f32[32,128]{1,0:T(8,128)S(1)} %collective-permute-done.8.refs_3_, f32[128,128]{1,0:T(8,128)S(1)} %inverse_factor.1.own.refs_4_), custom_call_target="tpu_custom_call" | custom-call | flops 100000000 | bytes 400000 | tf_op jit(solution)/shard_map/factor_rows/pallas_call | solution.py:255
  79.4 6.2 %all-to-all-start.3 = ((f32[32,32,128]{2,1,0:T(8,128)}), f32[32,32,128]{2,1,0:T(8,128)S(1)}, u32[]{:S(2)}, u32[]{:S(2)}) async-start(f32[32,32,128]{2,1,0:T(8,128)} %factor_rows.1), calls=%async_computation.3 | async-start | bytes 1048576 | tf_op jit(solution)/shard_map/all_to_all | solution.py:449
  85.6 2.0 %collective-permute-start.5 = (f32[128,128]{1,0:T(8,128)S(1)}, f32[128,128]{1,0:T(8,128)S(1)}, u32[]{:S(2)}, u32[]{:S(2)}) collective-permute-start(f32[128,128]{1,0:T(8,128)S(1)} %inverse_factor.1.own.refs_4_), channel_id=1, source_target_pairs={{0,1},{1,0},{2,3},{3,2},{4,5},{5,4},{6,7},{7,6},{8,9},{9,8},{10,11... | collective-permute-start | bytes 196616 | tf_op jit(solution)/shard_map/ppermute | solution.py:453
  87.6 0.9 collective-permute-done.5.other
  88.5 1.2 %basis_rows.1 = (f32[2,512,128]{2,1,0:T(8,128)}, bf16[2,512,256]{2,1,0:T(8,128)(2,1)S(1)}, f32[8,128]{1,0:T(8,128)S(1)}) custom-call(s32[1]{0:T(128)} %bitcast.which.core, f32[8,2,64,128]{3,2,1,0:T(8,128)S(1)} %all_to_all.21.left_mean, f32[128,128]{1,0:T(8,128)S(1)} %inverse_factor.1.own.refs_4_, f32[128,128]{1,0:T(8,128)S(1)} %collective-permute-done.5.other), custom_call_target="tpu_custom_call" | custom-call | flops 800000000 | bytes 2000000 | tf_op jit(solution)/shard_map/basis_rows/pallas_call | solution.py:232
  89.8 2.0 %merge.1 = (f32[512,1024]{1,0:T(8,128)S(1)}, f32[8,128]{1,0:T(8,128)S(1)}) custom-call(s32[1]{0:T(128)} %bitcast.which.core, bf16[2,512,1024]{2,1,0:T(8,128)(2,1)} %bitcast.11, f32[2,512,1024]{2,1,0:T(8,128)} %bitcast.8, f32[8,128]{1,0:T(8,128)S(1)} %get-tuple-element.26.after), custom_call_target="tpu_custom_call" | custom-call | flops 100000000 | bytes 5000000 | tf_op jit(solution)/shard_map/merge/pallas_call | solution.py:317
  91.8 3.2 %all-to-all-done.3 = f32[32,32,128]{2,1,0:T(8,128)S(1)} async-done(((f32[32,32,128]{2,1,0:T(8,128)}), f32[32,32,128]{2,1,0:T(8,128)S(1)}, u32[]{:S(2)}, u32[]{:S(2)}) %all-to-all-start.3) | async-done | bytes 524320 | tf_op jit(solution)/shard_map/all_to_all | solution.py:449
  95.0 3.2 %collective-permute-start.9 = (f32[1024,128]{1,0:T(8,128)S(1)}, f32[1024,128]{1,0:T(8,128)S(1)}, u32[]{:S(2)}, u32[]{:S(2)}) collective-permute-start(f32[1024,128]{1,0:T(8,128)S(1)} %tie.1.right), channel_id=1, source_target_pairs={{0,1},{1,0},{2,3},{3,2},{4,5},{5,4},{6,7},{7,6},{8,9},{9,8},{10,11... | collective-permute-start | bytes 1572872 | tf_op jit(solution)/shard_map/ppermute | solution.py:453
  98.2 3.0 %finish.2 = (f32[2,512,1024]{2,1,0:T(8,128)}, f32[2,1024,128]{2,1,0:T(8,128)}, f32[512,1024]{1,0:T(8,128)S(1)}) custom-call(s32[1]{0:T(128)} %bitcast.which.core, f32[512,1024]{1,0:T(8,128)S(1)} %get-tuple-element.27.merged, bf16[2,512,256]{2,1,0:T(8,128)(2,1)S(1)} %get-tuple-element.28.operand, f32[1024,128]{1,0:T(8,128)S(1)} %tie.1.right, ...), custom_call_target="tpu_custom_call" | custom-call | flops 800000000 | bytes 6000000 | tf_op jit(solution)/shard_map/finish/pallas_call | solution.py:371
  101.1 0.0 collective-permute-done.9.right
  101.1 1.8 %finish.3 = (f32[2,512,1024]{2,1,0:T(8,128)}, f32[2,1024,128]{2,1,0:T(8,128)}) custom-call(s32[1]{0:T(128)S(6)} %sub.3.other.which, f32[512,1024]{1,0:T(8,128)S(1)} %get-tuple-element.31.merged, bf16[2,512,256]{2,1,0:T(8,128)(2,1)S(1)} %get-tuple-element.28.operand, ...), custom_call_target="tpu_custom_call", output_to_operand_aliasing={{0}: (4, {}), {1}: (5, {})} | custom-call | flops 800000000 | bytes 6000000 | tf_op jit(solution)/shard_map/finish/pallas_call | solution.py:371
  (4 shorter events, 0.1 us)
Async XLA Ops:
  19.8 8.5 %collective-permute-start.2 = (f32[1,2,64,128]{3,2,1,0:T(8,128)S(1)}, f32[1,2,64,128]{3,2,1,0:T(8,128)S(1)}, u32[]{:S(2)}, u32[]{:S(2)}) collective-permute-start(f32[1,2,64,128]{3,2,1,0:T(8,128)S(1)} %share.2.refs_0_), channel_id=1, source_target_pairs={{0,128},{64,192},{128,0},{192,64},{1,129},{65,193},{129,1},{193,65... | collective-permute-start | bytes 196616 | tf_op jit(solution)/shard_map/ppermute | solution.py:457
  25.9 5.9 %collective-permute-start.1 = (f32[1,2,64,128]{3,2,1,0:T(8,128)S(1)}, f32[1,2,64,128]{3,2,1,0:T(8,128)S(1)}, u32[]{:S(2)}, u32[]{:S(2)}) collective-permute-start(f32[1,2,64,128]{3,2,1,0:T(8,128)S(1)} %share.2.refs_0_), channel_id=1, source_target_pairs={{0,192},{64,0},{128,64},{192,128},{1,193},{65,1},{129,65},{193,129... | collective-permute-start | bytes 196616 | tf_op jit(solution)/shard_map/ppermute | solution.py:457
  26.2 5.6 %collective-permute-start = (f32[1,2,64,128]{3,2,1,0:T(8,128)S(1)}, f32[1,2,64,128]{3,2,1,0:T(8,128)S(1)}, u32[]{:S(2)}, u32[]{:S(2)}) collective-permute-start(f32[1,2,64,128]{3,2,1,0:T(8,128)S(1)} %share.2.refs_0_), channel_id=1, source_target_pairs={{0,64},{64,128},{128,192},{192,0},{1,65},{65,129},{129,193},{193,1... | collective-permute-start | bytes 196616 | tf_op jit(solution)/shard_map/ppermute | solution.py:457
  43.9 6.1 %collective-permute-start.3 = (f32[1024,128]{1,0:T(8,128)S(1)}, f32[1024,128]{1,0:T(8,128)S(1)}, u32[]{:S(2)}, u32[]{:S(2)}) collective-permute-start(f32[1024,128]{1,0:T(8,128)S(1)} %get-tuple-element.22), channel_id=1, source_target_pairs={{0,1},{1,0},{2,3},{3,2},{4,5},{5,4},{6,7},{7,6},{8,9},{9,8},{10,11... | collective-permute-start | bytes 1572872 | tf_op jit(solution)/shard_map/ppermute | solution.py:453
  48.5 1.6 %collective-permute-start.4 = (f32[128,128]{1,0:T(8,128)S(1)}, f32[128,128]{1,0:T(8,128)S(1)}, u32[]{:S(2)}, u32[]{:S(2)}) collective-permute-start(f32[128,128]{1,0:T(8,128)S(1)} %get-tuple-element.24), channel_id=1, source_target_pairs={{0,1},{1,0},{2,3},{3,2},{4,5},{5,4},{6,7},{7,6},{8,9},{9,8},{10,11... | collective-permute-start | bytes 196616 | tf_op jit(solution)/shard_map/ppermute | solution.py:453
  67.8 10.5 %collective-permute-start.8 = (f32[32,128]{1,0:T(8,128)S(1)}, f32[32,128]{1,0:T(8,128)S(1)}, u32[]{:S(2)}, u32[]{:S(2)}) collective-permute-start(f32[32,128]{1,0:T(8,128)S(1)} %get-tuple-element.29.refs_0_), channel_id=1, source_target_pairs={{0,128},{64,192},{128,0},{192,64},{1,129},{65,193},{129,1},{193,65... | collective-permute-start | bytes 49160 | tf_op jit(solution)/shard_map/ppermute | solution.py:457
  71.9 6.5 %collective-permute-start.7 = (f32[32,128]{1,0:T(8,128)S(1)}, f32[32,128]{1,0:T(8,128)S(1)}, u32[]{:S(2)}, u32[]{:S(2)}) collective-permute-start(f32[32,128]{1,0:T(8,128)S(1)} %get-tuple-element.29.refs_0_), channel_id=1, source_target_pairs={{0,192},{64,0},{128,64},{192,128},{1,193},{65,1},{129,65},{193,129... | collective-permute-start | bytes 49160 | tf_op jit(solution)/shard_map/ppermute | solution.py:457
  72.2 6.1 %collective-permute-start.6 = (f32[32,128]{1,0:T(8,128)S(1)}, f32[32,128]{1,0:T(8,128)S(1)}, u32[]{:S(2)}, u32[]{:S(2)}) collective-permute-start(f32[32,128]{1,0:T(8,128)S(1)} %get-tuple-element.29.refs_0_), channel_id=1, source_target_pairs={{0,64},{64,128},{128,192},{192,0},{1,65},{65,129},{129,193},{193,1... | collective-permute-start | bytes 49160 | tf_op jit(solution)/shard_map/ppermute | solution.py:457
  79.4 15.6 %all-to-all-start.3 = ((f32[32,32,128]{2,1,0:T(8,128)}), f32[32,32,128]{2,1,0:T(8,128)S(1)}, u32[]{:S(2)}, u32[]{:S(2)}) async-start(f32[32,32,128]{2,1,0:T(8,128)} %factor_rows.1), calls=%async_computation.3 | async-start | bytes 1048576 | tf_op jit(solution)/shard_map/all_to_all | solution.py:449
  85.6 2.9 %collective-permute-start.5 = (f32[128,128]{1,0:T(8,128)S(1)}, f32[128,128]{1,0:T(8,128)S(1)}, u32[]{:S(2)}, u32[]{:S(2)}) collective-permute-start(f32[128,128]{1,0:T(8,128)S(1)} %inverse_factor.1.own.refs_4_), channel_id=1, source_target_pairs={{0,1},{1,0},{2,3},{3,2},{4,5},{5,4},{6,7},{7,6},{8,9},{9,8},{10,11... | collective-permute-start | bytes 196616 | tf_op jit(solution)/shard_map/ppermute | solution.py:453
  95.0 6.1 %collective-permute-start.9 = (f32[1024,128]{1,0:T(8,128)S(1)}, f32[1024,128]{1,0:T(8,128)S(1)}, u32[]{:S(2)}, u32[]{:S(2)}) collective-permute-start(f32[1024,128]{1,0:T(8,128)S(1)} %tie.1.right), channel_id=1, source_target_pairs={{0,1},{1,0},{2,3},{3,2},{4,5},{5,4},{6,7},{7,6},{8,9},{9,8},{10,11... | collective-permute-start | bytes 1572872 | tf_op jit(solution)/shard_map/ppermute | solution.py:453

commit v5 on v4

--- a/solution.py
+++ b/solution.py
@@ -92,7 +92,7 @@
         left[at // CHUNK : (at + rows) // CHUNK, m] = dot_wide(total, prior_in[m]).reshape(rows // CHUNK, CHUNK, RANK)
 
 
-def left_terms(other, place, gradient, feedback, right_prior, steps=4):
+def left_terms(other, place, gradient, feedback, right_prior, steps=2):
     rows = ROWS * MATRICES // steps
     return pl.pallas_call(
         left_kernel,
@@ -123,12 +123,12 @@
     return square[:RANK, :RANK] + (square[RANK:, :RANK] + square[:RANK, RANK:] + square[RANK:, RANK:])
 
 
-def right_kernel(which, merged, left_mean, right, *grams):
+def right_kernel(which, merged, left_mean, right, *gram):
     i = which[0]
     both = stacked(left_mean[:, i].reshape(ROWS, RANK))
-    if grams:
-        grams[0][...] = gram_of(both)
-        grams[1][...] = gram_of(stacked(left_mean[:, 1 - i].reshape(ROWS, RANK)))
+    if gram:
+        right[WIDTH:] = gram_of(both)
+        gram[0][...] = gram_of(stacked(left_mean[:, 1 - i].reshape(ROWS, RANK)))
     cols = WIDTH // 2
     for at in range(0, WIDTH, cols):
         merged_high, merged_low = halves(merged[i, :, at : at + cols])
@@ -138,11 +138,11 @@
 
 
 def right_terms(which, merged, left_mean, with_gram):
-    square = jax.ShapeDtypeStruct((RANK, RANK), f32)
     return pl.pallas_call(
         right_kernel,
         in_specs=[pl.BlockSpec(memory_space=pltpu.SMEM)] + [pl.BlockSpec(memory_space=pltpu.VMEM)] * 2,
-        out_shape=[jax.ShapeDtypeStruct((WIDTH, RANK), f32)] + [square] * (2 * with_gram),
+        out_shape=[jax.ShapeDtypeStruct((WIDTH + RANK * with_gram, RANK), f32)]
+        + [jax.ShapeDtypeStruct((RANK, RANK), f32)] * with_gram,
         compiler_params=pltpu.CompilerParams(vmem_limit_bytes=24 * MIB),
         cost_estimate=pl.CostEstimate(flops=8 * 10**8, bytes_accessed=4 * 10**6, transcendentals=0),
         name="right_terms",
@@ -410,30 +410,30 @@
     )(*parts, *after)
 
 
-def parcel_kernel(place, right, right_other, gram, gram_other, out, gram_sum):
-    gram_sum[...] = gram[...] + gram_other[...]
+def parcel_kernel(place, right, gram, arrived, out, gram_sum):
+    gram_sum[...] = gram[...] + arrived[WIDTH:]
     piece = gram_sum[pl.ds(pl.multiple_of(place[0] * PIECE, PIECE), PIECE)]
     for i in range(BOX):
         at = slice(i * SHARE, (i + 1) * SHARE)
-        out[i, :SHARE] = right[at] + right_other[at]
+        out[i, :SHARE] = right[at] + arrived[at]
         out[i, SHARE:] = piece
 
 
-def parcels(place, right, right_other, gram, gram_other):
+def parcels(place, right, gram, arrived):
     return pl.pallas_call(
         parcel_kernel,
-        in_specs=[pl.BlockSpec(memory_space=pltpu.SMEM)] + [pl.BlockSpec(memory_space=pltpu.VMEM)] * 4,
+        in_specs=[pl.BlockSpec(memory_space=pltpu.SMEM)] + [pl.BlockSpec(memory_space=pltpu.VMEM)] * 3,
         out_shape=jax.ShapeDtypeStruct((BOX, SHARE + PIECE, RANK), f32),
         scratch_shapes=[pltpu.VMEM((RANK, RANK), f32)],
         compiler_params=pltpu.CompilerParams(vmem_limit_bytes=8 * MIB),
         name="parcels",
-    )(place, right, right_other, gram, gram_other)
+    )(place, right, gram, arrived)
 
 
 def unpack_kernel(parts, total, gram):
     total[...] = tree_sum([parts[i, :SHARE] for i in range(BOX)])
     for k in range(RANK // PIECE):
-        gram[k * PIECE : (k + 1) * PIECE] = tree_sum([parts[4 * k + x, SHARE:] for x in range(4)])
+        gram[k * PIECE : (k + 1) * PIECE] = tree_sum([parts[8 * x + k, SHARE:] for x in range(4)])
 
 
 def unpack(parts):
@@ -454,23 +454,23 @@
 
 
 def rounds(x, axis):
-    return [x] + [lax.ppermute(x, axis, [(i, (i + s) % 4) for i in range(4)]) for s in (1, 3, 2)]
+    return [x] + [lax.ppermute(x, axis, [(i, i ^ s) for i in range(4)]) for s in (1, 3, 2)]
 
 
 def shards(gradient, feedback, right_prior):
     own = lax.axis_index("core")[None]
     other = 1 - own
-    place = lax.axis_index(("zl", "y"))[None]
-    column, box = ("zl", "y"), ("zl", "y", "x")
+    place = lax.axis_index(('zl', 'y'))[None]
+    column, box = ('zl', 'y'), ('x', 'zl', 'y')
     gradient, feedback, right_prior = in_hbm(gradient[0]), in_hbm(feedback[0]), in_hbm(right_prior)
     left, merged = left_terms(other, place, gradient, feedback, right_prior)
     left = rounds(share(exchange(left, column), 1, 1.0 / 32), "zh")
     left_mean = exchange(share(left, 8, 1.0), column)
 
-    right_other, gram_other, gram = right_terms(other, merged, left_mean, True)
-    right_other, gram_other = swap(right_other), swap(gram_other)
+    right_other, gram = right_terms(other, merged, left_mean, True)
+    arrived = swap(right_other)
     right = right_terms(own, merged, left_mean, False)[0]
-    parts = exchange(parcels(place, right, right_other, gram, gram_other), box)
+    parts = exchange(parcels(place, right, gram, arrived), box)
     total, gram = unpack(parts)
     totals = rounds(total, "zh")
     inverse = inverse_factor(gram)

time: 103 us -> 101 us (0.981)
  starting transfers between devices: 30.9 us -> 28.5 us
    ppermute x6, starting transfers between devices: 14.9 us -> 13 us  [rounds(): lax.ppermute(x, axis, [(i, i ^ s) for i in range(4)])]
    all_to_all x1, starting transfers between devices: 6.22 us -> 4.55 us  [exchange(): return lax.all_to_all(x, axes, 0, 0, tiled=True)]
    ppermute x4 -> x3, starting transfers between devices: 9.77 us -> 10.9 us  [swap(): return lax.ppermute(x, 'core', [(0, 1), (1, 0)])]
    ppermute x6, waiting for transfers between devices: 3.53 us -> 4.58 us  [rounds(): lax.ppermute(x, axis, [(i, i ^ s) for i in range(4)])]
  transfers between devices with their start and end apart: 11 -> 10, of which waited for: 4 -> 5; matrix products, arithmetic and copies ran while one was open for 0% -> 0% of each run, Pallas kernels for 11% -> 11%
where the time goes in v5:
time: 101 us; the launch traced here: 100 us
  blocking collectives  43.7 us (43%)
  starting transfers between devices  28.5 us (28%)
  Pallas kernels  19 us (19%)
  waiting for transfers between devices  8.61 us (9%)
    all_to_all x3, blocking collectives, exchange(): return lax.all_to_all(x, axes, 0, 0, tiled=True)  43.7 us
    ppermute x6, starting transfers between devices, rounds(): lax.ppermute(x, axis, [(i, i ^ s) for i in range(4)])  13 us
    ppermute x3, starting transfers between devices, swap(): return lax.ppermute(x, 'core', [(0, 1), (1, 0)])  10.9 us
    pallas_call x2, Pallas kernels, finish(): pl.pallas_call(finish_kernel, in_specs=[pl.BlockSpec(memory_space=pltpu.S...  4.81 us
    ppermute x6, waiting for transfers between devices, rounds(): lax.ppermute(x, axis, [(i, i ^ s) for i in range(4)])  4.58 us
    all_to_all x1, starting transfers between devices, exchange(): return lax.all_to_all(x, axes, 0, 0, tiled=True)  4.55 us
    pallas_call x1, Pallas kernels, inverse_factor(): pl.pallas_call(inverse_kernel, out_shape=jax.ShapeDtypeStruct((RANK, RANK...  4.06 us
    pallas_call x1, Pallas kernels, left_terms(): pl.pallas_call(left_kernel, in_specs=[pl.BlockSpec(memory_space=pltpu.SME...  3.97 us
  transfers between devices with their start and end apart: 10, of which 5 were waited for; matrix products, arithmetic and copies ran while one was open for 0% of the time, Pallas kernels for 11%

profile of v5, /device:TPU:1, one launch (start us, length us, event | category | flops | bytes accessed | tf_op | source)
XLA Modules:
  0.0 100.5 jit_solution(9899790373879994503)
XLA Ops:
  0.6 4.0 %left_terms.1 = (f32[8,2,64,128]{3,2,1,0:T(8,128)S(1)}, f32[2,512,1024]{2,1,0:T(8,128)S(1)}) custom-call(s32[1]{0:T(128)S(6)} %sub.3.other.which, s32[1]{0:T(128)} %bitcast.3.place, bf16[2,512,1024]{2,1,0:T(8,128)(2,1)} %bitcast.10, f32[2,512,1024]{2,1,0:T(8,128)} %bitcast.7, f32[2,1024,128]{2,1,0:T(8,128)} %prior.1), custom_call_target="tpu_custom_call" | custom-call | tf_op jit(solution)/shard_map/left_terms/pallas_call | solution.py:97
  4.6 14.8 %all_to_all.20.refs_0_ = f32[8,2,64,128]{3,2,1,0:T(8,128)S(1)} all-to-all(f32[8,2,64,128]{3,2,1,0:T(8,128)S(1)} %get-tuple-element.19), channel_id=1, replica_groups=mesh['zh'=4,'zl'=2,'y'=4,'x'=4,'core'=2] {'zl','y'}, dimensions={0} | all-to-all | bytes 1048576 | tf_op jit(solution)/shard_map/all_to_all | solution.py:449
  19.4 6.1 %collective-permute-start.2 = (f32[1,2,64,128]{3,2,1,0:T(8,128)S(1)}, f32[1,2,64,128]{3,2,1,0:T(8,128)S(1)}, u32[]{:S(2)}, u32[]{:S(2)}) collective-permute-start(f32[1,2,64,128]{3,2,1,0:T(8,128)S(1)} %share.2.refs_0_), channel_id=1, source_target_pairs={{0,128},{64,192},{128,0},{192,64},{1,129},{65,193},{129,1},{193,65... | collective-permute-start | bytes 196616 | tf_op jit(solution)/shard_map/ppermute | solution.py:457
  25.5 0.3 collective-permute-start.1
  25.8 0.9 collective-permute-start
  26.7 0.5 collective-permute-done.2.refs_3_
  27.2 4.0 %collective-permute-done.1.refs_2_ = f32[1,2,64,128]{3,2,1,0:T(8,128)S(1)} collective-permute-done((f32[1,2,64,128]{3,2,1,0:T(8,128)S(1)}, f32[1,2,64,128]{3,2,1,0:T(8,128)S(1)}, u32[]{:S(2)}, u32[]{:S(2)}) %collective-permute-start.1) | collective-permute-done | bytes 65568 | tf_op jit(solution)/shard_map/ppermute | solution.py:457
  31.3 0.0 collective-permute-done.refs_1_
  31.3 10.8 %all_to_all.21.left_mean = f32[8,2,64,128]{3,2,1,0:T(8,128)S(1)} all-to-all(f32[8,2,64,128]{3,2,1,0:T(8,128)S(1)} %share.3), channel_id=1, replica_groups=mesh['zh'=4,'zl'=2,'y'=4,'x'=4,'core'=2] {'zl','y'}, dimensions={0} | all-to-all | bytes 1048576 | tf_op jit(solution)/shard_map/all_to_all | solution.py:449
  42.1 0.9 right_terms.3
  43.0 4.5 %collective-permute-start.3 = (f32[1152,128]{1,0:T(8,128)S(1)}, f32[1152,128]{1,0:T(8,128)S(1)}, u32[]{:S(2)}, u32[]{:S(2)}) collective-permute-start(f32[1152,128]{1,0:T(8,128)S(1)} %get-tuple-element.22), channel_id=1, source_target_pairs={{0,1},{1,0},{2,3},{3,2},{4,5},{5,4},{6,7},{7,6},{8,9},{9,8},{10,11... | collective-permute-start | bytes 1769480 | tf_op jit(solution)/shard_map/ppermute | solution.py:453
  47.5 0.8 right_terms.2.right
  48.3 0.9 collective-permute-done.3.arrived
  49.2 0.1 parcels.1
  49.2 18.1 %all_to_all.22.parts = f32[32,48,128]{2,1,0:T(8,128)S(1)} all-to-all(f32[32,48,128]{2,1,0:T(8,128)S(1)} %parcels.1), channel_id=1, replica_groups=mesh['zh'=4,'zl'=2,'y'=4,'x'=4,'core'=2] {'x','zl','y'}, dimensions={0} | all-to-all | bytes 1572864 | tf_op jit(solution)/shard_map/all_to_all | solution.py:449
  67.4 4.0 %collective-permute-start.7 = (f32[32,128]{1,0:T(8,128)S(1)}, f32[32,128]{1,0:T(8,128)S(1)}, u32[]{:S(2)}, u32[]{:S(2)}) collective-permute-start(f32[32,128]{1,0:T(8,128)S(1)} %get-tuple-element.27.refs_0_), channel_id=1, source_target_pairs={{0,128},{64,192},{128,0},{192,64},{1,129},{65,193},{129,1},{193,65... | collective-permute-start | bytes 49160 | tf_op jit(solution)/shard_map/ppermute | solution.py:457
  71.4 1.5 %collective-permute-start.6 = (f32[32,128]{1,0:T(8,128)S(1)}, f32[32,128]{1,0:T(8,128)S(1)}, u32[]{:S(2)}, u32[]{:S(2)}) collective-permute-start(f32[32,128]{1,0:T(8,128)S(1)} %get-tuple-element.27.refs_0_), channel_id=1, source_target_pairs={{0,192},{64,128},{128,64},{192,0},{1,193},{65,129},{129,65},{193,1... | collective-permute-start | bytes 49160 | tf_op jit(solution)/shard_map/ppermute | solution.py:457
  72.9 0.2 collective-permute-start.5
  73.1 4.1 %inverse_factor.1.own.refs_4_ = f32[128,128]{1,0:T(8,128)S(1)} custom-call(f32[128,128]{1,0:T(8,128)S(1)} %get-tuple-element.23.gram), custom_call_target="tpu_custom_call" | custom-call | flops 3000000000 | bytes 100000 | tf_op jit(solution)/shard_map/inverse_factor/pallas_call | solution.py:214
  77.2 0.0 collective-permute-done.7.refs_3_
  77.2 0.0 collective-permute-done.6.refs_2_
  77.2 0.0 collective-permute-done.5.refs_1_
  77.2 1.1 %factor_rows.1 = f32[32,32,128]{2,1,0:T(8,128)} custom-call(f32[32,128]{1,0:T(8,128)S(1)} %get-tuple-element.27.refs_0_, f32[32,128]{1,0:T(8,128)S(1)} %collective-permute-done.5.refs_1_, f32[32,128]{1,0:T(8,128)S(1)} %collective-permute-done.6.refs_2_, f32[32,128]{1,0:T(8,128)S(1)} %collective-permute-done.7.refs_3_, f32[128,128]{1,0:T(8,128)S(1)} %inverse_factor.1.own.refs_4_), custom_call_target="tpu_custom_call" | custom-call | flops 100000000 | bytes 400000 | tf_op jit(solution)/shard_map/factor_rows/pallas_call | solution.py:255
  78.3 4.6 %all-to-all-start.3 = ((f32[32,32,128]{2,1,0:T(8,128)}), f32[32,32,128]{2,1,0:T(8,128)S(1)}, u32[]{:S(2)}, u32[]{:S(2)}) async-start(f32[32,32,128]{2,1,0:T(8,128)} %factor_rows.1), calls=%async_computation.3 | async-start | bytes 1048576 | tf_op jit(solution)/shard_map/all_to_all | solution.py:449
  82.8 2.7 %collective-permute-start.4 = (f32[128,128]{1,0:T(8,128)S(1)}, f32[128,128]{1,0:T(8,128)S(1)}, u32[]{:S(2)}, u32[]{:S(2)}) collective-permute-start(f32[128,128]{1,0:T(8,128)S(1)} %inverse_factor.1.own.refs_4_), channel_id=1, source_target_pairs={{0,1},{1,0},{2,3},{3,2},{4,5},{5,4},{6,7},{7,6},{8,9},{9,8},{10,11... | collective-permute-start | bytes 196616 | tf_op jit(solution)/shard_map/ppermute | solution.py:453
  85.6 0.9 collective-permute-done.4.other
  86.5 1.2 %basis_rows.1 = (f32[2,512,128]{2,1,0:T(8,128)}, bf16[2,512,256]{2,1,0:T(8,128)(2,1)S(1)}, f32[8,128]{1,0:T(8,128)S(1)}) custom-call(s32[1]{0:T(128)} %bitcast.which.core, f32[8,2,64,128]{3,2,1,0:T(8,128)S(1)} %all_to_all.21.left_mean, f32[128,128]{1,0:T(8,128)S(1)} %inverse_factor.1.own.refs_4_, f32[128,128]{1,0:T(8,128)S(1)} %collective-permute-done.4.other), custom_call_target="tpu_custom_call" | custom-call | flops 800000000 | bytes 2000000 | tf_op jit(solution)/shard_map/basis_rows/pallas_call | solution.py:232
  87.7 2.0 %merge.1 = (f32[512,1024]{1,0:T(8,128)S(1)}, f32[8,128]{1,0:T(8,128)S(1)}) custom-call(s32[1]{0:T(128)} %bitcast.which.core, bf16[2,512,1024]{2,1,0:T(8,128)(2,1)} %bitcast.11, f32[2,512,1024]{2,1,0:T(8,128)} %bitcast.8, f32[8,128]{1,0:T(8,128)S(1)} %get-tuple-element.24.after), custom_call_target="tpu_custom_call" | custom-call | flops 100000000 | bytes 5000000 | tf_op jit(solution)/shard_map/merge/pallas_call | solution.py:317
  89.7 2.3 %all-to-all-done.3 = f32[32,32,128]{2,1,0:T(8,128)S(1)} async-done(((f32[32,32,128]{2,1,0:T(8,128)}), f32[32,32,128]{2,1,0:T(8,128)S(1)}, u32[]{:S(2)}, u32[]{:S(2)}) %all-to-all-start.3) | async-done | bytes 524320 | tf_op jit(solution)/shard_map/all_to_all | solution.py:449
  92.0 3.6 %collective-permute-start.8 = (f32[1024,128]{1,0:T(8,128)S(1)}, f32[1024,128]{1,0:T(8,128)S(1)}, u32[]{:S(2)}, u32[]{:S(2)}) collective-permute-start(f32[1024,128]{1,0:T(8,128)S(1)} %tie.1.right), channel_id=1, source_target_pairs={{0,1},{1,0},{2,3},{3,2},{4,5},{5,4},{6,7},{7,6},{8,9},{9,8},{10,11... | collective-permute-start | bytes 1572872 | tf_op jit(solution)/shard_map/ppermute | solution.py:453
  95.6 3.0 %finish.2 = (f32[2,512,1024]{2,1,0:T(8,128)}, f32[2,1024,128]{2,1,0:T(8,128)}, f32[512,1024]{1,0:T(8,128)S(1)}) custom-call(s32[1]{0:T(128)} %bitcast.which.core, f32[512,1024]{1,0:T(8,128)S(1)} %get-tuple-element.25.merged, bf16[2,512,256]{2,1,0:T(8,128)(2,1)S(1)} %get-tuple-element.26.operand, f32[1024,128]{1,0:T(8,128)S(1)} %tie.1.right, ...), custom_call_target="tpu_custom_call" | custom-call | flops 800000000 | bytes 6000000 | tf_op jit(solution)/shard_map/finish/pallas_call | solution.py:371
  98.6 0.0 collective-permute-done.8.right
  98.6 1.8 %finish.3 = (f32[2,512,1024]{2,1,0:T(8,128)}, f32[2,1024,128]{2,1,0:T(8,128)}) custom-call(s32[1]{0:T(128)S(6)} %sub.3.other.which, f32[512,1024]{1,0:T(8,128)S(1)} %get-tuple-element.29.merged, bf16[2,512,256]{2,1,0:T(8,128)(2,1)S(1)} %get-tuple-element.26.operand, ...), custom_call_target="tpu_custom_call", output_to_operand_aliasing={{0}: (4, {}), {1}: (5, {})} | custom-call | flops 800000000 | bytes 6000000 | tf_op jit(solution)/shard_map/finish/pallas_call | solution.py:371
  (4 shorter events, 0.1 us)
Async XLA Ops:
  19.4 7.8 %collective-permute-start.2 = (f32[1,2,64,128]{3,2,1,0:T(8,128)S(1)}, f32[1,2,64,128]{3,2,1,0:T(8,128)S(1)}, u32[]{:S(2)}, u32[]{:S(2)}) collective-permute-start(f32[1,2,64,128]{3,2,1,0:T(8,128)S(1)} %share.2.refs_0_), channel_id=1, source_target_pairs={{0,128},{64,192},{128,0},{192,64},{1,129},{65,193},{129,1},{193,65... | collective-permute-start | bytes 196616 | tf_op jit(solution)/shard_map/ppermute | solution.py:457
  25.5 5.7 %collective-permute-start.1 = (f32[1,2,64,128]{3,2,1,0:T(8,128)S(1)}, f32[1,2,64,128]{3,2,1,0:T(8,128)S(1)}, u32[]{:S(2)}, u32[]{:S(2)}) collective-permute-start(f32[1,2,64,128]{3,2,1,0:T(8,128)S(1)} %share.2.refs_0_), channel_id=1, source_target_pairs={{0,192},{64,128},{128,64},{192,0},{1,193},{65,129},{129,65},{193,1... | collective-permute-start | bytes 196616 | tf_op jit(solution)/shard_map/ppermute | solution.py:457
  25.8 5.5 %collective-permute-start = (f32[1,2,64,128]{3,2,1,0:T(8,128)S(1)}, f32[1,2,64,128]{3,2,1,0:T(8,128)S(1)}, u32[]{:S(2)}, u32[]{:S(2)}) collective-permute-start(f32[1,2,64,128]{3,2,1,0:T(8,128)S(1)} %share.2.refs_0_), channel_id=1, source_target_pairs={{0,64},{64,0},{128,192},{192,128},{1,65},{65,1},{129,193},{193,129... | collective-permute-start | bytes 196616 | tf_op jit(solution)/shard_map/ppermute | solution.py:457
  43.0 6.1 %collective-permute-start.3 = (f32[1152,128]{1,0:T(8,128)S(1)}, f32[1152,128]{1,0:T(8,128)S(1)}, u32[]{:S(2)}, u32[]{:S(2)}) collective-permute-start(f32[1152,128]{1,0:T(8,128)S(1)} %get-tuple-element.22), channel_id=1, source_target_pairs={{0,1},{1,0},{2,3},{3,2},{4,5},{5,4},{6,7},{7,6},{8,9},{9,8},{10,11... | collective-permute-start | bytes 1769480 | tf_op jit(solution)/shard_map/ppermute | solution.py:453
  67.4 9.8 %collective-permute-start.7 = (f32[32,128]{1,0:T(8,128)S(1)}, f32[32,128]{1,0:T(8,128)S(1)}, u32[]{:S(2)}, u32[]{:S(2)}) collective-permute-start(f32[32,128]{1,0:T(8,128)S(1)} %get-tuple-element.27.refs_0_), channel_id=1, source_target_pairs={{0,128},{64,192},{128,0},{192,64},{1,129},{65,193},{129,1},{193,65... | collective-permute-start | bytes 49160 | tf_op jit(solution)/shard_map/ppermute | solution.py:457
  71.4 5.8 %collective-permute-start.6 = (f32[32,128]{1,0:T(8,128)S(1)}, f32[32,128]{1,0:T(8,128)S(1)}, u32[]{:S(2)}, u32[]{:S(2)}) collective-permute-start(f32[32,128]{1,0:T(8,128)S(1)} %get-tuple-element.27.refs_0_), channel_id=1, source_target_pairs={{0,192},{64,128},{128,64},{192,0},{1,193},{65,129},{129,65},{193,1... | collective-permute-start | bytes 49160 | tf_op jit(solution)/shard_map/ppermute | solution.py:457
  72.9 4.3 %collective-permute-start.5 = (f32[32,128]{1,0:T(8,128)S(1)}, f32[32,128]{1,0:T(8,128)S(1)}, u32[]{:S(2)}, u32[]{:S(2)}) collective-permute-start(f32[32,128]{1,0:T(8,128)S(1)} %get-tuple-element.27.refs_0_), channel_id=1, source_target_pairs={{0,64},{64,0},{128,192},{192,128},{1,65},{65,1},{129,193},{193,129... | collective-permute-start | bytes 49160 | tf_op jit(solution)/shard_map/ppermute | solution.py:457
  78.3 13.7 %all-to-all-start.3 = ((f32[32,32,128]{2,1,0:T(8,128)}), f32[32,32,128]{2,1,0:T(8,128)S(1)}, u32[]{:S(2)}, u32[]{:S(2)}) async-start(f32[32,32,128]{2,1,0:T(8,128)} %factor_rows.1), calls=%async_computation.3 | async-start | bytes 1048576 | tf_op jit(solution)/shard_map/all_to_all | solution.py:449
  82.8 3.6 %collective-permute-start.4 = (f32[128,128]{1,0:T(8,128)S(1)}, f32[128,128]{1,0:T(8,128)S(1)}, u32[]{:S(2)}, u32[]{:S(2)}) collective-permute-start(f32[128,128]{1,0:T(8,128)S(1)} %inverse_factor.1.own.refs_4_), channel_id=1, source_target_pairs={{0,1},{1,0},{2,3},{3,2},{4,5},{5,4},{6,7},{7,6},{8,9},{9,8},{10,11... | collective-permute-start | bytes 196616 | tf_op jit(solution)/shard_map/ppermute | solution.py:453
  92.0 6.6 %collective-permute-start.8 = (f32[1024,128]{1,0:T(8,128)S(1)}, f32[1024,128]{1,0:T(8,128)S(1)}, u32[]{:S(2)}, u32[]{:S(2)}) collective-permute-start(f32[1024,128]{1,0:T(8,128)S(1)} %tie.1.right), channel_id=1, source_target_pairs={{0,1},{1,0},{2,3},{3,2},{4,5},{5,4},{6,7},{7,6},{8,9},{9,8},{10,11... | collective-permute-start | bytes 1572872 | tf_op jit(solution)/shard_map/ppermute | solution.py:453

commit v6 on v5

--- a/solution.py
+++ b/solution.py
@@ -220,29 +220,6 @@
     )(gram)
 
 
-def basis_kernel(core, left_mean, own, other, basis, operand, token):
-    token[...] = jnp.zeros(token.shape, f32)
-    for i, inverse in ((core[0], own), (1 - core[0], other)):
-        rows = dot_wide(left_mean[:, i].reshape(ROWS, RANK), inverse[...].T)
-        basis[i] = rows
-        operand[i] = stacked(rows * (1.0 / math.sqrt(FEATURES)))
-
-
-def basis_rows(core, left_mean, own, other):
-    return pl.pallas_call(
-        basis_kernel,
-        in_specs=[pl.BlockSpec(memory_space=pltpu.SMEM)] + [pl.BlockSpec(memory_space=pltpu.VMEM)] * 3,
-        out_shape=[
-            jax.ShapeDtypeStruct((MATRICES, ROWS, RANK), f32),
-            jax.ShapeDtypeStruct((MATRICES, ROWS, 2 * RANK), bf16),
-            jax.ShapeDtypeStruct((8, RANK), f32),
-        ],
-        compiler_params=pltpu.CompilerParams(vmem_limit_bytes=16 * MIB),
-        cost_estimate=pl.CostEstimate(flops=8 * 10**8, bytes_accessed=2 * 10**6, transcendentals=0),
-        name="basis_rows",
-    )(core, left_mean, own, other)
-
-
 def factor_kernel(*refs):
     *parts, inverse, out = refs
     total = tree_sum([part[...] for part in parts])
@@ -277,116 +254,61 @@
     )(in_vmem(x), after)
 
 
-def fetches(which, gradient, feedback, gradient_in, feedback_in, sems, i):
-    rows = gradient_in.shape[1]
-    at = pl.ds(i * rows, rows)
-    return (
-        pltpu.make_async_copy(gradient.at[which, at], gradient_in.at[i], sems.at[0, i]),
-        pltpu.make_async_copy(feedback.at[which, at], feedback_in.at[i], sems.at[1, i]),
-    )
-
-
-def merge_arrived(which, gradient, feedback, gradient_in, feedback_in, sems, merged):
-    steps, rows, _ = gradient_in.shape
-    for i in range(steps):
-        for copy in fetches(which, gradient, feedback, gradient_in, feedback_in, sems, i):
-            copy.wait()
-        merged[i * rows : (i + 1) * rows] = gradient_in[i].astype(f32) + feedback_in[i]
-
-
-def fetch_scratch(steps):
-    rows = ROWS // steps
-    return [
-        pltpu.VMEM((steps, rows, WIDTH), bf16),
-        pltpu.VMEM((steps, rows, WIDTH), f32),
-        pltpu.SemaphoreType.DMA((2, steps)),
-    ]
-
-
-def merge_kernel(which, gradient, feedback, after, merged, token, *scratch):
-    del after
-    token[...] = jnp.zeros(token.shape, f32)
-    arrays = (which[0], gradient, feedback, *scratch)
-    for i in range(scratch[0].shape[0]):
-        for copy in fetches(*arrays, i):
-            copy.start()
-    merge_arrived(*arrays, merged)
-
-
-def merge(which, gradient, feedback, after):
-    return pl.pallas_call(
-        merge_kernel,
-        in_specs=[pl.BlockSpec(memory_space=pltpu.SMEM)]
-        + [pl.BlockSpec(memory_space=pltpu.HBM)] * 2
-        + [pl.BlockSpec(memory_space=pltpu.VMEM)],
-        out_shape=[jax.ShapeDtypeStruct((ROWS, WIDTH), f32), jax.ShapeDtypeStruct((8, RANK), f32)],
-        scratch_shapes=fetch_scratch(2),
-        compiler_params=pltpu.CompilerParams(vmem_limit_bytes=16 * MIB),
-        cost_estimate=pl.CostEstimate(flops=10**8, bytes_accessed=5 * 10**6, transcendentals=0),
-        name="merge",
-    )(which, gradient, feedback, after)
-
-
-def finish_kernel(which, merged, operand, right, *rest):
-    *rest, renewed_out, turned, sems = rest
+def finish_kernel(which, merged, left_mean, inverse, right, *rest):
+    renewed, basis, factor, renewed_out, basis_out, turned, sems = rest[-7:]
     w = which[0]
     steps, rows, _ = renewed_out.shape
-    if len(rest) > 4:
-        gradient, feedback, renewed, factor, merged_next, *scratch = rest
-        arrays = (1 - w, gradient, feedback, *scratch)
-        for i in range(scratch[0].shape[0]):
-            for copy in fetches(*arrays, i):
-                copy.start()
-    else:
-        renewed, factor = rest[-2:]
 
     def store(i):
         return pltpu.make_async_copy(renewed_out.at[i], renewed.at[w, pl.ds(i * rows, rows)], sems.at[i])
 
     store_factor = pltpu.make_async_copy(right, factor.at[w], sems.at[steps])
+    store_basis = pltpu.make_async_copy(basis_out, basis.at[w], sems.at[steps + 1])
     store_factor.start()
+    left_basis = dot_wide(left_mean[:, w].reshape(ROWS, RANK), inverse[...].T)
+    basis_out[...] = left_basis
+    store_basis.start()
+    operand = stacked(left_basis * (1.0 / math.sqrt(FEATURES)))
     high, low = halves(right[...])
     turned[:, :RANK] = high
     turned[:, RANK : 2 * RANK] = high
     turned[:, 2 * RANK :] = low
     for i in range(steps):
         at = slice(i * rows, (i + 1) * rows)
-        both = operand[w, at]
+        both = operand[at]
         approx = dot(both, turned[:, : 2 * RANK], NT) + dot(both[:, :RANK], turned[:, 2 * RANK :], NT)
-        renewed_out[i] = merged[at] - approx
+        renewed_out[i] = merged[w, at] - approx
         store(i).start()
-    if len(rest) > 4:
-        merge_arrived(*arrays, merged_next)
+    store_factor.wait()
+    store_basis.wait()
     for i in range(steps):
         store(i).wait()
-    store_factor.wait()
-
-
-def finish(which, merged, operand, right, ahead=(), before=(), steps=2):
+
+
+def finish(which, merged, left_mean, inverse, right, before=(), steps=2):
     rows = ROWS // steps
-    outs = [
-        jax.ShapeDtypeStruct((MATRICES, ROWS, WIDTH), f32),
-        jax.ShapeDtypeStruct((MATRICES, WIDTH, RANK), f32),
-    ]
     return pl.pallas_call(
         finish_kernel,
         in_specs=[pl.BlockSpec(memory_space=pltpu.SMEM)]
-        + [pl.BlockSpec(memory_space=pltpu.VMEM)] * 3
-        + [pl.BlockSpec(memory_space=pltpu.HBM)] * len(ahead)
+        + [pl.BlockSpec(memory_space=pltpu.VMEM)] * 4
         + [pl.BlockSpec(memory_space=pl.ANY)] * len(before),
-        out_specs=[pl.BlockSpec(memory_space=pl.ANY)] * 2 + [pl.BlockSpec(memory_space=pltpu.VMEM)] * bool(ahead),
-        out_shape=outs + [jax.ShapeDtypeStruct((ROWS, WIDTH), f32)] * bool(ahead),
-        scratch_shapes=fetch_scratch(2) * bool(ahead)
-        + [
+        out_specs=[pl.BlockSpec(memory_space=pl.ANY)] * 3,
+        out_shape=[
+            jax.ShapeDtypeStruct((MATRICES, ROWS, WIDTH), f32),
+            jax.ShapeDtypeStruct((MATRICES, ROWS, RANK), f32),
+            jax.ShapeDtypeStruct((MATRICES, WIDTH, RANK), f32),
+        ],
+        scratch_shapes=[
             pltpu.VMEM((steps, rows, WIDTH), f32),
+            pltpu.VMEM((ROWS, RANK), f32),
             pltpu.VMEM((WIDTH, 3 * RANK), bf16),
-            pltpu.SemaphoreType.DMA((steps + 1,)),
+            pltpu.SemaphoreType.DMA((steps + 2,)),
         ],
-        input_output_aliases={4: 0, 5: 1} if before else {},
+        input_output_aliases={5: 0, 6: 1, 7: 2} if before else {},
         compiler_params=pltpu.CompilerParams(vmem_limit_bytes=24 * MIB),
         cost_estimate=pl.CostEstimate(flops=8 * 10**8, bytes_accessed=6 * 10**6, transcendentals=0),
         name="finish",
-    )(which, merged, operand, right, *ahead, *before)
+    )(which, merged, left_mean, inverse, right, *before)
 
 
 def share_kernel(*refs, scale, count):
@@ -475,12 +397,10 @@
     totals = rounds(total, "zh")
     inverse = inverse_factor(gram)
     right = exchange(factor_rows(totals, inverse, 32), box).reshape(WIDTH, RANK)
-    basis, operand, token = basis_rows(own, left_mean, inverse, swap(inverse))
-    merged, token = merge(own, gradient, feedback, token)
-    right = tie(right, token)
-
-    *done, merged = finish(own, merged, operand, right, (gradient, feedback))
-    renewed, factor = finish(other, merged, operand, swap(right), (), tuple(done))
+    inverse = tie(inverse, right)
+    arrived = swap(inverse), swap(right)
+    done = finish(own, merged, left_mean, inverse, right)
+    renewed, basis, factor = finish(other, merged, left_mean, *arrived, tuple(done))
     return renewed[None], basis, factor
 
 

time: 101 us -> 99.1 us (0.981)
  blocking collectives: 43.7 us -> 57.2 us
  starting transfers between devices: 28.5 us -> 21.2 us
  Pallas kernels: 19 us -> 14.3 us
  waiting for transfers between devices: 8.61 us -> 5.45 us
    all_to_all x3 -> x4, blocking collectives: 43.7 us -> 57.2 us  [exchange(): return lax.all_to_all(x, axes, 0, 0, tiled=True)]
    all_to_all x1 -> x0, starting transfers between devices: 4.55 us -> none  [exchange(): return lax.all_to_all(x, axes, 0, 0, tiled=True)]
    pallas_call x2 -> x0, Pallas kernels: 3.23 us -> none  [the longest x1 1.98 us: merge(): pl.pallas_call(merge_kernel, in_specs=[pl.BlockSpec(memory_space=pltpu.SM...]
    ppermute x3, starting transfers between devices: 10.9 us -> 8.16 us  [swap(): return lax.ppermute(x, 'core', [(0, 1), (1, 0)])]
    all_to_all x1 -> x0, waiting for transfers between devices: 2.27 us -> none  [exchange(): return lax.all_to_all(x, axes, 0, 0, tiled=True)]
  transfers between devices with their start and end apart: 10 -> 9, of which waited for: 5 -> 3; matrix products, arithmetic and copies ran while one was open for 0% -> 0% of each run, Pallas kernels for 11% -> 7%
where the time goes in v6:
time: 99.1 us; the launch traced here: 98.9 us
  blocking collectives  57.2 us (58%)
  starting transfers between devices  21.2 us (21%)
  Pallas kernels  14.3 us (14%)
  waiting for transfers between devices  5.45 us (5%)
    all_to_all x4, blocking collectives, exchange(): return lax.all_to_all(x, axes, 0, 0, tiled=True)  57.2 us
    ppermute x6, starting transfers between devices, rounds(): lax.ppermute(x, axis, [(i, i ^ s) for i in range(4)])  13 us
    ppermute x3, starting transfers between devices, swap(): return lax.ppermute(x, 'core', [(0, 1), (1, 0)])  8.16 us
    ppermute x6, waiting for transfers between devices, rounds(): lax.ppermute(x, axis, [(i, i ^ s) for i in range(4)])  4.58 us
    pallas_call x2, Pallas kernels, finish(): pl.pallas_call(finish_kernel, in_specs=[pl.BlockSpec(memory_space=pltpu.S...  4.17 us
    pallas_call x1, Pallas kernels, inverse_factor(): pl.pallas_call(inverse_kernel, out_shape=jax.ShapeDtypeStruct((RANK, RANK...  4.06 us
    pallas_call x1, Pallas kernels, left_terms(): pl.pallas_call(left_kernel, in_specs=[pl.BlockSpec(memory_space=pltpu.SME...  3.96 us
  transfers between devices with their start and end apart: 9, of which 3 were waited for; matrix products, arithmetic and copies ran while one was open for 0% of the time, Pallas kernels for 7%

profile of v6, /device:TPU:1, one launch (start us, length us, event | category | flops | bytes accessed | tf_op | source)
XLA Modules:
  0.0 98.9 jit_solution(9779499890253328306)
XLA Ops:
  0.6 4.0 %left_terms.1 = (f32[8,2,64,128]{3,2,1,0:T(8,128)S(1)}, f32[2,512,1024]{2,1,0:T(8,128)S(1)}) custom-call(s32[1]{0:T(128)S(6)} %sub.3.other.which, s32[1]{0:T(128)} %bitcast.1.place, bf16[2,512,1024]{2,1,0:T(8,128)(2,1)} %bitcast.11, f32[2,512,1024]{2,1,0:T(8,128)} %bitcast.9, f32[2,1024,128]{2,1,0:T(8,128)} %prior.1), custom_call_target="tpu_custom_call" | custom-call | tf_op jit(solution)/shard_map/left_terms/pallas_call | solution.py:97
  4.6 14.8 %all_to_all.20.refs_0_ = f32[8,2,64,128]{3,2,1,0:T(8,128)S(1)} all-to-all(f32[8,2,64,128]{3,2,1,0:T(8,128)S(1)} %get-tuple-element.16), channel_id=1, replica_groups=mesh['zh'=4,'zl'=2,'y'=4,'x'=4,'core'=2] {'zl','y'}, dimensions={0} | all-to-all | bytes 1048576 | tf_op jit(solution)/shard_map/all_to_all | solution.py:371
  19.4 6.1 %collective-permute-start.2 = (f32[1,2,64,128]{3,2,1,0:T(8,128)S(1)}, f32[1,2,64,128]{3,2,1,0:T(8,128)S(1)}, u32[]{:S(2)}, u32[]{:S(2)}) collective-permute-start(f32[1,2,64,128]{3,2,1,0:T(8,128)S(1)} %share.2.refs_0_), channel_id=1, source_target_pairs={{0,128},{64,192},{128,0},{192,64},{1,129},{65,193},{129,1},{193,65... | collective-permute-start | bytes 196616 | tf_op jit(solution)/shard_map/ppermute | solution.py:379
  25.5 0.3 collective-permute-start.1
  25.8 0.9 collective-permute-start
  26.7 0.5 collective-permute-done.2.refs_3_
  27.2 4.0 %collective-permute-done.1.refs_2_ = f32[1,2,64,128]{3,2,1,0:T(8,128)S(1)} collective-permute-done((f32[1,2,64,128]{3,2,1,0:T(8,128)S(1)}, f32[1,2,64,128]{3,2,1,0:T(8,128)S(1)}, u32[]{:S(2)}, u32[]{:S(2)}) %collective-permute-start.1) | collective-permute-done | bytes 65568 | tf_op jit(solution)/shard_map/ppermute | solution.py:379
  31.3 0.0 collective-permute-done.refs_1_
  31.3 10.8 %all_to_all.21.left_mean = f32[8,2,64,128]{3,2,1,0:T(8,128)S(1)} all-to-all(f32[8,2,64,128]{3,2,1,0:T(8,128)S(1)} %share.3), channel_id=1, replica_groups=mesh['zh'=4,'zl'=2,'y'=4,'x'=4,'core'=2] {'zl','y'}, dimensions={0} | all-to-all | bytes 1048576 | tf_op jit(solution)/shard_map/all_to_all | solution.py:371
  42.1 0.9 right_terms.3
  43.0 4.5 %collective-permute-start.3 = (f32[1152,128]{1,0:T(8,128)S(1)}, f32[1152,128]{1,0:T(8,128)S(1)}, u32[]{:S(2)}, u32[]{:S(2)}) collective-permute-start(f32[1152,128]{1,0:T(8,128)S(1)} %get-tuple-element.18), channel_id=1, source_target_pairs={{0,1},{1,0},{2,3},{3,2},{4,5},{5,4},{6,7},{7,6},{8,9},{9,8},{10,11... | collective-permute-start | bytes 1769480 | tf_op jit(solution)/shard_map/ppermute | solution.py:375
  47.5 0.8 right_terms.2.right
  48.3 0.9 collective-permute-done.3.arrived
  49.2 0.1 parcels.1
  49.2 18.1 %all_to_all.22.parts = f32[32,48,128]{2,1,0:T(8,128)S(1)} all-to-all(f32[32,48,128]{2,1,0:T(8,128)S(1)} %parcels.1), channel_id=1, replica_groups=mesh['zh'=4,'zl'=2,'y'=4,'x'=4,'core'=2] {'x','zl','y'}, dimensions={0} | all-to-all | bytes 1572864 | tf_op jit(solution)/shard_map/all_to_all | solution.py:371
  67.4 4.0 %collective-permute-start.6 = (f32[32,128]{1,0:T(8,128)S(1)}, f32[32,128]{1,0:T(8,128)S(1)}, u32[]{:S(2)}, u32[]{:S(2)}) collective-permute-start(f32[32,128]{1,0:T(8,128)S(1)} %get-tuple-element.20.refs_0_), channel_id=1, source_target_pairs={{0,128},{64,192},{128,0},{192,64},{1,129},{65,193},{129,1},{193,65... | collective-permute-start | bytes 49160 | tf_op jit(solution)/shard_map/ppermute | solution.py:379
  71.4 1.5 %collective-permute-start.5 = (f32[32,128]{1,0:T(8,128)S(1)}, f32[32,128]{1,0:T(8,128)S(1)}, u32[]{:S(2)}, u32[]{:S(2)}) collective-permute-start(f32[32,128]{1,0:T(8,128)S(1)} %get-tuple-element.20.refs_0_), channel_id=1, source_target_pairs={{0,192},{64,128},{128,64},{192,0},{1,193},{65,129},{129,65},{193,1... | collective-permute-start | bytes 49160 | tf_op jit(solution)/shard_map/ppermute | solution.py:379
  72.9 0.2 collective-permute-start.4
  73.1 4.1 %inverse_factor.1.refs_4_.x = f32[128,128]{1,0:T(8,128)S(1)} custom-call(f32[128,128]{1,0:T(8,128)S(1)} %get-tuple-element.19.gram), custom_call_target="tpu_custom_call" | custom-call | flops 3000000000 | bytes 100000 | tf_op jit(solution)/shard_map/inverse_factor/pallas_call | solution.py:214
  77.2 0.0 collective-permute-done.6.refs_3_
  77.2 0.0 collective-permute-done.5.refs_2_
  77.2 0.0 collective-permute-done.4.refs_1_
  77.2 0.3 factor_rows.1
  77.5 13.5 %all_to_all.23 = f32[32,32,128]{2,1,0:T(8,128)S(1)} all-to-all(f32[32,32,128]{2,1,0:T(8,128)S(1)} %factor_rows.1), channel_id=1, replica_groups=mesh['zh'=4,'zl'=2,'y'=4,'x'=4,'core'=2] {'x','zl','y'}, dimensions={0} | all-to-all | bytes 1048576 | tf_op jit(solution)/shard_map/all_to_all | solution.py:371
  91.0 3.7 %collective-permute-start.8 = (f32[1024,128]{1,0:T(8,128)S(1)}, f32[1024,128]{1,0:T(8,128)S(1)}, u32[]{:S(2)}, u32[]{:S(2)}) collective-permute-start(f32[1024,128]{1,0:T(8,128)S(1)} %bitcast.6), channel_id=1, source_target_pairs={{0,1},{1,0},{2,3},{3,2},{4,5},{5,4},{6,7},{7,6},{8,9},{9,8},{10,11... | collective-permute-start | bytes 1572872 | tf_op jit(solution)/shard_map/ppermute | solution.py:375
  94.7 0.0 collective-permute-start.7
  94.7 2.1 %finish.2 = (f32[2,512,1024]{2,1,0:T(8,128)}, f32[2,512,128]{2,1,0:T(8,128)}, f32[2,1024,128]{2,1,0:T(8,128)}) custom-call(s32[1]{0:T(128)} %bitcast.which, f32[2,512,1024]{2,1,0:T(8,128)S(1)} %get-tuple-element.15.merged, f32[8,2,64,128]{3,2,1,0:T(8,128)S(1)} %all_to_all.21.left_mean, f32[128,128]{1,0:T(8,128)S(1)} %tie.1.inverse, f32[1024,128]{1,0:T(8,128)S(1)} %bitcast.8), custom_call_target="tpu_custom_call" | custom-call | flops 800000000 | bytes 6000000 | tf_op jit(solution)/shard_map/finish/pallas_call | solution.py:290
  96.8 0.0 collective-permute-done.7.inverse
  96.8 0.0 collective-permute-done.8.right
  96.8 2.1 %finish.3 = (f32[2,512,1024]{2,1,0:T(8,128)}, f32[2,512,128]{2,1,0:T(8,128)}, f32[2,1024,128]{2,1,0:T(8,128)}) custom-call(s32[1]{0:T(128)S(6)} %sub.3.other.which, f32[2,512,1024]{2,1,0:T(8,128)S(1)} %get-tuple-element.15.merged, f32[8,2,64,128]{3,2,1,0:T(8,128)S(1)} %all_to_all.21.left_mean, ...), custom_call_target="tpu_custom_call", output_to_operand_aliasing={{0}: (5, {}), {1}: (6, {}), {2}: (7, {})} | custom-call | flops 800000000 | bytes 6000000 | tf_op jit(solution)/shard_map/finish/pallas_call | solution.py:290
  (4 shorter events, 0.1 us)
Async XLA Ops:
  19.4 7.8 %collective-permute-start.2 = (f32[1,2,64,128]{3,2,1,0:T(8,128)S(1)}, f32[1,2,64,128]{3,2,1,0:T(8,128)S(1)}, u32[]{:S(2)}, u32[]{:S(2)}) collective-permute-start(f32[1,2,64,128]{3,2,1,0:T(8,128)S(1)} %share.2.refs_0_), channel_id=1, source_target_pairs={{0,128},{64,192},{128,0},{192,64},{1,129},{65,193},{129,1},{193,65... | collective-permute-start | bytes 196616 | tf_op jit(solution)/shard_map/ppermute | solution.py:379
  25.5 5.7 %collective-permute-start.1 = (f32[1,2,64,128]{3,2,1,0:T(8,128)S(1)}, f32[1,2,64,128]{3,2,1,0:T(8,128)S(1)}, u32[]{:S(2)}, u32[]{:S(2)}) collective-permute-start(f32[1,2,64,128]{3,2,1,0:T(8,128)S(1)} %share.2.refs_0_), channel_id=1, source_target_pairs={{0,192},{64,128},{128,64},{192,0},{1,193},{65,129},{129,65},{193,1... | collective-permute-start | bytes 196616 | tf_op jit(solution)/shard_map/ppermute | solution.py:379
  25.8 5.5 %collective-permute-start = (f32[1,2,64,128]{3,2,1,0:T(8,128)S(1)}, f32[1,2,64,128]{3,2,1,0:T(8,128)S(1)}, u32[]{:S(2)}, u32[]{:S(2)}) collective-permute-start(f32[1,2,64,128]{3,2,1,0:T(8,128)S(1)} %share.2.refs_0_), channel_id=1, source_target_pairs={{0,64},{64,0},{128,192},{192,128},{1,65},{65,1},{129,193},{193,129... | collective-permute-start | bytes 196616 | tf_op jit(solution)/shard_map/ppermute | solution.py:379
  43.0 6.1 %collective-permute-start.3 = (f32[1152,128]{1,0:T(8,128)S(1)}, f32[1152,128]{1,0:T(8,128)S(1)}, u32[]{:S(2)}, u32[]{:S(2)}) collective-permute-start(f32[1152,128]{1,0:T(8,128)S(1)} %get-tuple-element.18), channel_id=1, source_target_pairs={{0,1},{1,0},{2,3},{3,2},{4,5},{5,4},{6,7},{7,6},{8,9},{9,8},{10,11... | collective-permute-start | bytes 1769480 | tf_op jit(solution)/shard_map/ppermute | solution.py:375
  67.4 9.8 %collective-permute-start.6 = (f32[32,128]{1,0:T(8,128)S(1)}, f32[32,128]{1,0:T(8,128)S(1)}, u32[]{:S(2)}, u32[]{:S(2)}) collective-permute-start(f32[32,128]{1,0:T(8,128)S(1)} %get-tuple-element.20.refs_0_), channel_id=1, source_target_pairs={{0,128},{64,192},{128,0},{192,64},{1,129},{65,193},{129,1},{193,65... | collective-permute-start | bytes 49160 | tf_op jit(solution)/shard_map/ppermute | solution.py:379
  71.4 5.8 %collective-permute-start.5 = (f32[32,128]{1,0:T(8,128)S(1)}, f32[32,128]{1,0:T(8,128)S(1)}, u32[]{:S(2)}, u32[]{:S(2)}) collective-permute-start(f32[32,128]{1,0:T(8,128)S(1)} %get-tuple-element.20.refs_0_), channel_id=1, source_target_pairs={{0,192},{64,128},{128,64},{192,0},{1,193},{65,129},{129,65},{193,1... | collective-permute-start | bytes 49160 | tf_op jit(solution)/shard_map/ppermute | solution.py:379
  72.9 4.3 %collective-permute-start.4 = (f32[32,128]{1,0:T(8,128)S(1)}, f32[32,128]{1,0:T(8,128)S(1)}, u32[]{:S(2)}, u32[]{:S(2)}) collective-permute-start(f32[32,128]{1,0:T(8,128)S(1)} %get-tuple-element.20.refs_0_), channel_id=1, source_target_pairs={{0,64},{64,0},{128,192},{192,128},{1,65},{65,1},{129,193},{193,129... | collective-permute-start | bytes 49160 | tf_op jit(solution)/shard_map/ppermute | solution.py:379
  91.0 5.8 %collective-permute-start.8 = (f32[1024,128]{1,0:T(8,128)S(1)}, f32[1024,128]{1,0:T(8,128)S(1)}, u32[]{:S(2)}, u32[]{:S(2)}) collective-permute-start(f32[1024,128]{1,0:T(8,128)S(1)} %bitcast.6), channel_id=1, source_target_pairs={{0,1},{1,0},{2,3},{3,2},{4,5},{5,4},{6,7},{7,6},{8,9},{9,8},{10,11... | collective-permute-start | bytes 1572872 | tf_op jit(solution)/shard_map/ppermute | solution.py:375
  94.7 2.1 %collective-permute-start.7 = (f32[128,128]{1,0:T(8,128)S(1)}, f32[128,128]{1,0:T(8,128)S(1)}, u32[]{:S(2)}, u32[]{:S(2)}) collective-permute-start(f32[128,128]{1,0:T(8,128)S(1)} %tie.1.inverse), channel_id=1, source_target_pairs={{0,1},{1,0},{2,3},{3,2},{4,5},{5,4},{6,7},{7,6},{8,9},{9,8},{10,11... | collective-permute-start | bytes 196616 | tf_op jit(solution)/shard_map/ppermute | solution.py:375

commit v7 on v6

--- a/solution.py
+++ b/solution.py
@@ -238,23 +238,21 @@
     )(*parts, inverse)
 
 
-def tie_kernel(x, after, out):
-    del x, after, out
-
-
-def tie(x, after):
-    return pl.pallas_call(
-        tie_kernel,
-        in_specs=[pl.BlockSpec(memory_space=pl.ANY), pl.BlockSpec(memory_space=pltpu.VMEM)],
-        out_specs=pl.BlockSpec(memory_space=pl.ANY),
-        out_shape=pltpu.VMEM(x.shape, x.dtype),
-        input_output_aliases={0: 0},
-        compiler_params=pltpu.CompilerParams(vmem_limit_bytes=MIB),
-        name="tie",
-    )(in_vmem(x), after)
-
-
-def finish_kernel(which, merged, left_mean, inverse, right, *rest):
+def join_kernel(right, inverse, out):
+    out[:WIDTH] = right[...]
+    out[WIDTH:] = inverse[...]
+
+
+def join(right, inverse):
+    return pl.pallas_call(
+        join_kernel,
+        out_shape=jax.ShapeDtypeStruct((WIDTH + RANK, RANK), f32),
+        compiler_params=pltpu.CompilerParams(vmem_limit_bytes=8 * MIB),
+        name="join",
+    )(right, inverse)
+
+
+def finish_kernel(which, merged, left_mean, joined, *rest):
     renewed, basis, factor, renewed_out, basis_out, turned, sems = rest[-7:]
     w = which[0]
     steps, rows, _ = renewed_out.shape
@@ -262,14 +260,14 @@
     def store(i):
         return pltpu.make_async_copy(renewed_out.at[i], renewed.at[w, pl.ds(i * rows, rows)], sems.at[i])
 
-    store_factor = pltpu.make_async_copy(right, factor.at[w], sems.at[steps])
+    store_factor = pltpu.make_async_copy(joined.at[pl.ds(0, WIDTH)], factor.at[w], sems.at[steps])
     store_basis = pltpu.make_async_copy(basis_out, basis.at[w], sems.at[steps + 1])
     store_factor.start()
-    left_basis = dot_wide(left_mean[:, w].reshape(ROWS, RANK), inverse[...].T)
+    left_basis = dot_wide(left_mean[:, w].reshape(ROWS, RANK), joined[WIDTH:].T)
     basis_out[...] = left_basis
     store_basis.start()
     operand = stacked(left_basis * (1.0 / math.sqrt(FEATURES)))
-    high, low = halves(right[...])
+    high, low = halves(joined[:WIDTH])
     turned[:, :RANK] = high
     turned[:, RANK : 2 * RANK] = high
     turned[:, 2 * RANK :] = low
@@ -285,12 +283,12 @@
         store(i).wait()
 
 
-def finish(which, merged, left_mean, inverse, right, before=(), steps=2):
+def finish(which, merged, left_mean, joined, before=(), steps=2):
     rows = ROWS // steps
     return pl.pallas_call(
         finish_kernel,
         in_specs=[pl.BlockSpec(memory_space=pltpu.SMEM)]
-        + [pl.BlockSpec(memory_space=pltpu.VMEM)] * 4
+        + [pl.BlockSpec(memory_space=pltpu.VMEM)] * 3
         + [pl.BlockSpec(memory_space=pl.ANY)] * len(before),
         out_specs=[pl.BlockSpec(memory_space=pl.ANY)] * 3,
         out_shape=[
@@ -304,11 +302,11 @@
             pltpu.VMEM((WIDTH, 3 * RANK), bf16),
             pltpu.SemaphoreType.DMA((steps + 2,)),
         ],
-        input_output_aliases={5: 0, 6: 1, 7: 2} if before else {},
+        input_output_aliases={4: 0, 5: 1, 6: 2} if before else {},
         compiler_params=pltpu.CompilerParams(vmem_limit_bytes=24 * MIB),
         cost_estimate=pl.CostEstimate(flops=8 * 10**8, bytes_accessed=6 * 10**6, transcendentals=0),
         name="finish",
-    )(which, merged, left_mean, inverse, right, *before)
+    )(which, merged, left_mean, joined, *before)
 
 
 def share_kernel(*refs, scale, count):
@@ -397,10 +395,9 @@
     totals = rounds(total, "zh")
     inverse = inverse_factor(gram)
     right = exchange(factor_rows(totals, inverse, 32), box).reshape(WIDTH, RANK)
-    inverse = tie(inverse, right)
-    arrived = swap(inverse), swap(right)
-    done = finish(own, merged, left_mean, inverse, right)
-    renewed, basis, factor = finish(other, merged, left_mean, *arrived, tuple(done))
+    joined = join(right, inverse)
+    done = finish(own, merged, left_mean, joined)
+    renewed, basis, factor = finish(other, merged, left_mean, swap(joined), tuple(done))
     return renewed[None], basis, factor
 
 

time: 99.1 us -> 99.2 us (level)
    ppermute x3 -> x2, starting transfers between devices: 8.16 us -> 8.24 us  [swap(): return lax.ppermute(x, 'core', [(0, 1), (1, 0)])]
  transfers between devices with their start and end apart: 9 -> 8, of which waited for: 3 -> 3; matrix products, arithmetic and copies ran while one was open for 0% -> 0% of each run, Pallas kernels for 7% -> 7%
where the time goes in v7:
time: 99.2 us; the launch traced here: 99 us
  blocking collectives  57.2 us (58%)
  starting transfers between devices  21.3 us (21%)
  Pallas kernels  14.4 us (15%)
  waiting for transfers between devices  5.45 us (5%)
    all_to_all x4, blocking collectives, exchange(): return lax.all_to_all(x, axes, 0, 0, tiled=True)  57.2 us
    ppermute x6, starting transfers between devices, rounds(): lax.ppermute(x, axis, [(i, i ^ s) for i in range(4)])  13 us
    ppermute x2, starting transfers between devices, swap(): return lax.ppermute(x, 'core', [(0, 1), (1, 0)])  8.24 us
    ppermute x6, waiting for transfers between devices, rounds(): lax.ppermute(x, axis, [(i, i ^ s) for i in range(4)])  4.58 us
    pallas_call x2, Pallas kernels, finish(): pl.pallas_call(finish_kernel, in_specs=[pl.BlockSpec(memory_space=pltpu.S...  4.17 us
    pallas_call x1, Pallas kernels, inverse_factor(): pl.pallas_call(inverse_kernel, out_shape=jax.ShapeDtypeStruct((RANK, RANK...  4.06 us
    pallas_call x1, Pallas kernels, left_terms(): pl.pallas_call(left_kernel, in_specs=[pl.BlockSpec(memory_space=pltpu.SME...  3.96 us
  transfers between devices with their start and end apart: 8, of which 3 were waited for; matrix products, arithmetic and copies ran while one was open for 0% of the time, Pallas kernels for 7%

profile of v7, /device:TPU:1, one launch (start us, length us, event | category | flops | bytes accessed | tf_op | source)
XLA Modules:
  0.0 99.0 jit_solution(17386785524341410077)
XLA Ops:
  0.6 4.0 %left_terms.1 = (f32[8,2,64,128]{3,2,1,0:T(8,128)S(1)}, f32[2,512,1024]{2,1,0:T(8,128)S(1)}) custom-call(s32[1]{0:T(128)S(6)} %sub.3.other.which, s32[1]{0:T(128)} %bitcast.1.place, bf16[2,512,1024]{2,1,0:T(8,128)(2,1)} %bitcast.9, f32[2,512,1024]{2,1,0:T(8,128)} %bitcast.7, f32[2,1024,128]{2,1,0:T(8,128)} %prior.1), custom_call_target="tpu_custom_call" | custom-call | tf_op jit(solution)/shard_map/left_terms/pallas_call | solution.py:97
  4.6 14.8 %all_to_all.20.refs_0_ = f32[8,2,64,128]{3,2,1,0:T(8,128)S(1)} all-to-all(f32[8,2,64,128]{3,2,1,0:T(8,128)S(1)} %get-tuple-element.16), channel_id=1, replica_groups=mesh['zh'=4,'zl'=2,'y'=4,'x'=4,'core'=2] {'zl','y'}, dimensions={0} | all-to-all | bytes 1048576 | tf_op jit(solution)/shard_map/all_to_all | solution.py:369
  19.4 6.1 %collective-permute-start.2 = (f32[1,2,64,128]{3,2,1,0:T(8,128)S(1)}, f32[1,2,64,128]{3,2,1,0:T(8,128)S(1)}, u32[]{:S(2)}, u32[]{:S(2)}) collective-permute-start(f32[1,2,64,128]{3,2,1,0:T(8,128)S(1)} %share.2.refs_0_), channel_id=1, source_target_pairs={{0,128},{64,192},{128,0},{192,64},{1,129},{65,193},{129,1},{193,65... | collective-permute-start | bytes 196616 | tf_op jit(solution)/shard_map/ppermute | solution.py:377
  25.5 0.3 collective-permute-start.1
  25.8 0.9 collective-permute-start
  26.7 0.5 collective-permute-done.2.refs_3_
  27.2 4.0 %collective-permute-done.1.refs_2_ = f32[1,2,64,128]{3,2,1,0:T(8,128)S(1)} collective-permute-done((f32[1,2,64,128]{3,2,1,0:T(8,128)S(1)}, f32[1,2,64,128]{3,2,1,0:T(8,128)S(1)}, u32[]{:S(2)}, u32[]{:S(2)}) %collective-permute-start.1) | collective-permute-done | bytes 65568 | tf_op jit(solution)/shard_map/ppermute | solution.py:377
  31.3 0.0 collective-permute-done.refs_1_
  31.3 10.8 %all_to_all.21.left_mean = f32[8,2,64,128]{3,2,1,0:T(8,128)S(1)} all-to-all(f32[8,2,64,128]{3,2,1,0:T(8,128)S(1)} %share.3), channel_id=1, replica_groups=mesh['zh'=4,'zl'=2,'y'=4,'x'=4,'core'=2] {'zl','y'}, dimensions={0} | all-to-all | bytes 1048576 | tf_op jit(solution)/shard_map/all_to_all | solution.py:369
  42.1 0.9 right_terms.3
  43.0 4.5 %collective-permute-start.3 = (f32[1152,128]{1,0:T(8,128)S(1)}, f32[1152,128]{1,0:T(8,128)S(1)}, u32[]{:S(2)}, u32[]{:S(2)}) collective-permute-start(f32[1152,128]{1,0:T(8,128)S(1)} %get-tuple-element.18), channel_id=1, source_target_pairs={{0,1},{1,0},{2,3},{3,2},{4,5},{5,4},{6,7},{7,6},{8,9},{9,8},{10,11... | collective-permute-start | bytes 1769480 | tf_op jit(solution)/shard_map/ppermute | solution.py:373
  47.5 0.8 right_terms.2.right
  48.3 0.9 collective-permute-done.3.arrived
  49.2 0.1 parcels.1
  49.2 18.1 %all_to_all.22.parts = f32[32,48,128]{2,1,0:T(8,128)S(1)} all-to-all(f32[32,48,128]{2,1,0:T(8,128)S(1)} %parcels.1), channel_id=1, replica_groups=mesh['zh'=4,'zl'=2,'y'=4,'x'=4,'core'=2] {'x','zl','y'}, dimensions={0} | all-to-all | bytes 1572864 | tf_op jit(solution)/shard_map/all_to_all | solution.py:369
  67.4 4.0 %collective-permute-start.6 = (f32[32,128]{1,0:T(8,128)S(1)}, f32[32,128]{1,0:T(8,128)S(1)}, u32[]{:S(2)}, u32[]{:S(2)}) collective-permute-start(f32[32,128]{1,0:T(8,128)S(1)} %get-tuple-element.19.refs_0_), channel_id=1, source_target_pairs={{0,128},{64,192},{128,0},{192,64},{1,129},{65,193},{129,1},{193,65... | collective-permute-start | bytes 49160 | tf_op jit(solution)/shard_map/ppermute | solution.py:377
  71.4 1.5 %collective-permute-start.5 = (f32[32,128]{1,0:T(8,128)S(1)}, f32[32,128]{1,0:T(8,128)S(1)}, u32[]{:S(2)}, u32[]{:S(2)}) collective-permute-start(f32[32,128]{1,0:T(8,128)S(1)} %get-tuple-element.19.refs_0_), channel_id=1, source_target_pairs={{0,192},{64,128},{128,64},{192,0},{1,193},{65,129},{129,65},{193,1... | collective-permute-start | bytes 49160 | tf_op jit(solution)/shard_map/ppermute | solution.py:377
  72.9 0.2 collective-permute-start.4
  73.1 4.1 %inverse_factor.1.refs_4_.inverse = f32[128,128]{1,0:T(8,128)S(1)} custom-call(f32[128,128]{1,0:T(8,128)S(1)} %get-tuple-element.20.gram), custom_call_target="tpu_custom_call" | custom-call | flops 3000000000 | bytes 100000 | tf_op jit(solution)/shard_map/inverse_factor/pallas_call | solution.py:214
  77.2 0.0 collective-permute-done.6.refs_3_
  77.2 0.0 collective-permute-done.5.refs_2_
  77.2 0.0 collective-permute-done.4.refs_1_
  77.2 0.3 factor_rows.1
  77.5 13.5 %all_to_all.23 = f32[32,32,128]{2,1,0:T(8,128)S(1)} all-to-all(f32[32,32,128]{2,1,0:T(8,128)S(1)} %factor_rows.1), channel_id=1, replica_groups=mesh['zh'=4,'zl'=2,'y'=4,'x'=4,'core'=2] {'x','zl','y'}, dimensions={0} | all-to-all | bytes 1048576 | tf_op jit(solution)/shard_map/all_to_all | solution.py:369
  91.1 3.8 %collective-permute-start.7 = (f32[1152,128]{1,0:T(8,128)S(1)}, f32[1152,128]{1,0:T(8,128)S(1)}, u32[]{:S(2)}, u32[]{:S(2)}) collective-permute-start(f32[1152,128]{1,0:T(8,128)S(1)} %join.1.joined), channel_id=1, source_target_pairs={{0,1},{1,0},{2,3},{3,2},{4,5},{5,4},{6,7},{7,6},{8,9},{9,8},{10,11... | collective-permute-start | bytes 1769480 | tf_op jit(solution)/shard_map/ppermute | solution.py:373
  94.8 2.1 %finish.2 = (f32[2,512,1024]{2,1,0:T(8,128)}, f32[2,512,128]{2,1,0:T(8,128)}, f32[2,1024,128]{2,1,0:T(8,128)}) custom-call(s32[1]{0:T(128)} %bitcast.which, f32[2,512,1024]{2,1,0:T(8,128)S(1)} %get-tuple-element.15.merged, f32[8,2,64,128]{3,2,1,0:T(8,128)S(1)} %all_to_all.21.left_mean, f32[1152,128]{1,0:T(8,128)S(1)} %join.1.joined), custom_call_target="tpu_custom_call" | custom-call | flops 800000000 | bytes 6000000 | tf_op jit(solution)/shard_map/finish/pallas_call | solution.py:288
  96.9 0.0 collective-permute-done.7.joined
  96.9 2.1 %finish.3 = (f32[2,512,1024]{2,1,0:T(8,128)}, f32[2,512,128]{2,1,0:T(8,128)}, f32[2,1024,128]{2,1,0:T(8,128)}) custom-call(s32[1]{0:T(128)S(6)} %sub.3.other.which, f32[2,512,1024]{2,1,0:T(8,128)S(1)} %get-tuple-element.15.merged, f32[8,2,64,128]{3,2,1,0:T(8,128)S(1)} %all_to_all.21.left_mean, ...), custom_call_target="tpu_custom_call", output_to_operand_aliasing={{0}: (4, {}), {1}: (5, {}), {2}: (6, {})} | custom-call | flops 800000000 | bytes 6000000 | tf_op jit(solution)/shard_map/finish/pallas_call | solution.py:288
  (4 shorter events, 0.1 us)
Async XLA Ops:
  19.4 7.8 %collective-permute-start.2 = (f32[1,2,64,128]{3,2,1,0:T(8,128)S(1)}, f32[1,2,64,128]{3,2,1,0:T(8,128)S(1)}, u32[]{:S(2)}, u32[]{:S(2)}) collective-permute-start(f32[1,2,64,128]{3,2,1,0:T(8,128)S(1)} %share.2.refs_0_), channel_id=1, source_target_pairs={{0,128},{64,192},{128,0},{192,64},{1,129},{65,193},{129,1},{193,65... | collective-permute-start | bytes 196616 | tf_op jit(solution)/shard_map/ppermute | solution.py:377
  25.5 5.7 %collective-permute-start.1 = (f32[1,2,64,128]{3,2,1,0:T(8,128)S(1)}, f32[1,2,64,128]{3,2,1,0:T(8,128)S(1)}, u32[]{:S(2)}, u32[]{:S(2)}) collective-permute-start(f32[1,2,64,128]{3,2,1,0:T(8,128)S(1)} %share.2.refs_0_), channel_id=1, source_target_pairs={{0,192},{64,128},{128,64},{192,0},{1,193},{65,129},{129,65},{193,1... | collective-permute-start | bytes 196616 | tf_op jit(solution)/shard_map/ppermute | solution.py:377
  25.8 5.5 %collective-permute-start = (f32[1,2,64,128]{3,2,1,0:T(8,128)S(1)}, f32[1,2,64,128]{3,2,1,0:T(8,128)S(1)}, u32[]{:S(2)}, u32[]{:S(2)}) collective-permute-start(f32[1,2,64,128]{3,2,1,0:T(8,128)S(1)} %share.2.refs_0_), channel_id=1, source_target_pairs={{0,64},{64,0},{128,192},{192,128},{1,65},{65,1},{129,193},{193,129... | collective-permute-start | bytes 196616 | tf_op jit(solution)/shard_map/ppermute | solution.py:377
  43.0 6.1 %collective-permute-start.3 = (f32[1152,128]{1,0:T(8,128)S(1)}, f32[1152,128]{1,0:T(8,128)S(1)}, u32[]{:S(2)}, u32[]{:S(2)}) collective-permute-start(f32[1152,128]{1,0:T(8,128)S(1)} %get-tuple-element.18), channel_id=1, source_target_pairs={{0,1},{1,0},{2,3},{3,2},{4,5},{5,4},{6,7},{7,6},{8,9},{9,8},{10,11... | collective-permute-start | bytes 1769480 | tf_op jit(solution)/shard_map/ppermute | solution.py:373
  67.4 9.8 %collective-permute-start.6 = (f32[32,128]{1,0:T(8,128)S(1)}, f32[32,128]{1,0:T(8,128)S(1)}, u32[]{:S(2)}, u32[]{:S(2)}) collective-permute-start(f32[32,128]{1,0:T(8,128)S(1)} %get-tuple-element.19.refs_0_), channel_id=1, source_target_pairs={{0,128},{64,192},{128,0},{192,64},{1,129},{65,193},{129,1},{193,65... | collective-permute-start | bytes 49160 | tf_op jit(solution)/shard_map/ppermute | solution.py:377
  71.4 5.8 %collective-permute-start.5 = (f32[32,128]{1,0:T(8,128)S(1)}, f32[32,128]{1,0:T(8,128)S(1)}, u32[]{:S(2)}, u32[]{:S(2)}) collective-permute-start(f32[32,128]{1,0:T(8,128)S(1)} %get-tuple-element.19.refs_0_), channel_id=1, source_target_pairs={{0,192},{64,128},{128,64},{192,0},{1,193},{65,129},{129,65},{193,1... | collective-permute-start | bytes 49160 | tf_op jit(solution)/shard_map/ppermute | solution.py:377
  72.9 4.3 %collective-permute-start.4 = (f32[32,128]{1,0:T(8,128)S(1)}, f32[32,128]{1,0:T(8,128)S(1)}, u32[]{:S(2)}, u32[]{:S(2)}) collective-permute-start(f32[32,128]{1,0:T(8,128)S(1)} %get-tuple-element.19.refs_0_), channel_id=1, source_target_pairs={{0,64},{64,0},{128,192},{192,128},{1,65},{65,1},{129,193},{193,129... | collective-permute-start | bytes 49160 | tf_op jit(solution)/shard_map/ppermute | solution.py:377
  91.1 5.8 %collective-permute-start.7 = (f32[1152,128]{1,0:T(8,128)S(1)}, f32[1152,128]{1,0:T(8,128)S(1)}, u32[]{:S(2)}, u32[]{:S(2)}) collective-permute-start(f32[1152,128]{1,0:T(8,128)S(1)} %join.1.joined), channel_id=1, source_target_pairs={{0,1},{1,0},{2,3},{3,2},{4,5},{5,4},{6,7},{7,6},{8,9},{9,8},{10,11... | collective-permute-start | bytes 1769480 | tf_op jit(solution)/shard_map/ppermute | solution.py:373
